TPU v7x, 512 devices: a whole 4x8x8 slice. The times are simulated.
512 devices in a mesh: fsdp: 32 (over z, x), mp: 16 (over y, core).
Axes of the slice: x: 4, y: 8, z: 8, core: 2. Of those that a mesh axis runs over, the one named last changes fastest.
Arguments:
- tokens: bfloat16 [12288, 2048], P('fsdp', 'mp'), may hold values from -6 to 6
- cotangent: bfloat16 [12288, 2048], P('fsdp', 'mp'), may hold values from -6 to 6
- gate_weight: bfloat16 [2048, 6144], P('fsdp', 'mp'), may hold values from -0.125 to 0.125
- up_weight: bfloat16 [2048, 6144], P('fsdp', 'mp'), may hold values from -0.125 to 0.125
- down_weight: bfloat16 [2048, 6144], P('fsdp', 'mp'), may hold values from -0.125 to 0.125
Outputs:
- input_grad: bfloat16 [12288, 2048], P('fsdp', 'mp')
- grad_down: bfloat16 [2048, 6144], P('fsdp', 'mp')
All inputs are finite; a program needn't handle non-finite values.
Results may differ from a plain program's by a relative error of at most 0.022.
Values may be sent and summed in bfloat16 or wider, within the bound.
No kernel may reach another device: no remote copies, remote signals or barrier semaphores. Data moves between devices by JAX's collectives and lax.ppermute only.
A program may use at most 64 MiB of HBM per device.

v0:
```python
import math

import jax
import jax.numpy as jnp
from jax import lax
from jax.sharding import PartitionSpec as P

N_Z = 8
N_X = 4
N_Y = 8
N_CORE = 2
Z_GROUPS = [[z * N_X + x for z in range(N_Z)] for x in range(N_X)]
X_GROUPS = [[z * N_X + x for x in range(N_X)] for z in range(N_Z)]
Y_GROUPS = [[y * N_CORE + c for y in range(N_Y)] for c in range(N_CORE)]


def dot(left, right, dims):
    return lax.dot_general(left, right, (dims, ((), ())), preferred_element_type=jnp.float32)


def send_x(value, step):
    pairs = [
        (z * N_X + x, z * N_X + (x + step) % N_X) for z in range(N_Z) for x in range(N_X)
    ]
    return lax.ppermute(value, "fsdp", pairs)


def send_core(value):
    pairs = [(i, i ^ 1) for i in range(N_Y * N_CORE)]
    return lax.ppermute(value, "mp", pairs)


def gather_z(block):
    copies = jnp.broadcast_to(block[None], (N_Z,) + block.shape)
    return lax.all_to_all(copies, "fsdp", 0, 0, axis_index_groups=Z_GROUPS)


def add(left, right):
    return left.astype(jnp.float32) + right.astype(jnp.float32)


def put_x(blocks, me):
    n_z, rows, cols = blocks[0].shape
    full = jnp.zeros((n_z, N_X, rows, cols), blocks[0].dtype)
    for block, step in zip(blocks, (0, N_X - 1, 1, 2)):
        full = lax.dynamic_update_slice(full, block[:, None], (0, (me + step) % N_X, 0, 0))
    return full


def on_device(tokens, cotangent, gate_weight, up_weight, down_weight):
    n_fsdp = lax.axis_size("fsdp")
    rows, width = tokens.shape
    depth, cols = gate_weight.shape
    factor = 1.0 / math.sqrt(rows * n_fsdp)
    me_x = lax.axis_index("fsdp") % N_X
    core = lax.axis_index("mp") % N_CORE

    stacked = jnp.concatenate([tokens, cotangent])
    both = lax.all_gather(stacked, "mp", axis=1, tiled=True)
    token_rows, cotangent_rows = both[:rows], both[rows:]

    down_x = jnp.zeros((N_X, depth, cols), down_weight.dtype)
    down_x = lax.dynamic_update_slice(down_x, down_weight[None], (me_x, 0, 0))
    for step in (1, N_X - 1, 2):
        block = send_x(down_weight, step)
        down_x = lax.dynamic_update_slice(down_x, block[None], ((me_x - step) % N_X, 0, 0))

    gate_z = gather_z(gate_weight)
    gate_z, up_weight = lax.optimization_barrier((gate_z, up_weight))
    up_z = gather_z(up_weight)
    up_z, down_x = lax.optimization_barrier((up_z, down_x))
    down_full = gather_z(down_x).reshape(-1, cols)

    gate_left, gate_right = send_x(gate_z, 1), send_x(gate_z, -1)
    up_right, up_left = send_x(up_z, -1), send_x(up_z, 1)
    gate_far, up_far = send_x(gate_left, 1), send_x(up_right, -1)
    gate_full = put_x((gate_z, gate_left, gate_right, gate_far), me_x).reshape(-1, cols)
    up_full = put_x((up_z, up_left, up_right, up_far), me_x).reshape(-1, cols)

    gate_value = dot(token_rows, gate_full, ((1,), (0,)))
    up_value = dot(token_rows, up_full, ((1,), (0,)))
    sigmoid_gate = jax.nn.sigmoid(gate_value)
    hidden = (gate_value * sigmoid_gate * up_value).astype(jnp.bfloat16)

    down_partial = dot(cotangent_rows, hidden, ((0,), (0,))).astype(jnp.bfloat16)
    down_partial, cotangent_rows = lax.optimization_barrier((down_partial, cotangent_rows))
    hidden_grad = dot(cotangent_rows, down_full, ((1,), (0,)))
    gate_grad = (
        hidden_grad * up_value * sigmoid_gate * (1.0 + gate_value * (1.0 - sigmoid_gate))
    ).astype(jnp.bfloat16)
    up_grad = (hidden_grad * gate_value * sigmoid_gate).astype(jnp.bfloat16)

    def half_partial(which):
        pick = lambda full: lax.dynamic_index_in_dim(
            full.reshape(N_Y, N_CORE, width, cols), which, 1, keepdims=False
        ).reshape(N_Y * width, cols)
        value = dot(gate_grad, pick(gate_full), ((1,), (1,)))
        value = value + dot(up_grad, pick(up_full), ((1,), (1,)))
        return value.astype(jnp.bfloat16).reshape(rows, N_Y, width).transpose(1, 0, 2)

    from_core = send_core(half_partial(1 - core))
    pair_sum = add(half_partial(core), from_core).astype(jnp.bfloat16)
    summed = lax.all_to_all(pair_sum, "mp", 0, 0, axis_index_groups=Y_GROUPS)

    down_z = lax.psum_scatter(
        down_partial.reshape(N_Z, N_X, depth, cols).transpose(1, 0, 2, 3).reshape(-1, cols),
        "fsdp",
        scatter_dimension=0,
        axis_index_groups=X_GROUPS,
        tiled=True,
    ).reshape(N_Z, depth, cols)
    summed, down_z = lax.optimization_barrier((summed, down_z))
    input_grad = summed.astype(jnp.float32).sum(0).astype(jnp.bfloat16)
    down_z = lax.all_to_all(down_z, "fsdp", 0, 0, axis_index_groups=Z_GROUPS)
    grad_down = (down_z.astype(jnp.float32).sum(0) * factor).astype(jnp.bfloat16)
    return (input_grad, grad_down)


def solution(mesh):
    placed = P("fsdp", "mp")
    return jax.shard_map(
        on_device,
        mesh=mesh,
        in_specs=(placed,) * 5,
        out_specs=(placed, placed),
        check_vma=False,
    )
```

profile of v0, /device:TPU:6, one launch (start us, length us, event | category | flops | bytes accessed | tf_op | source)
XLA Modules:
  0.0 168.2 jit_solution(1719219536088278310)
XLA Ops:
  7.2 1.6 pad_maximum_fusion
  10.4 10.3 %all-to-all-start = ((bf16[8,64,384]{2,1,0:T(8,128)(2,1)}), bf16[8,64,384]{2,1,0:T(8,128)(2,1)S(1)}, u32[]{:S(2)}, u32[]{:S(2)}) async-start(bf16[8,64,384]{2,1,0:T(8,128)(2,1)} %broadcast_in_dim.57), calls=%async_computation | async-start | bytes 786432 | tf_op jit(solution)/shard_map/all_to_all | solution.py:35
  20.8 2.4 %collective-permute-start.3 = (bf16[64,384]{1,0:T(8,128)(2,1)S(1)}, bf16[64,384]{1,0:T(8,128)(2,1)S(1)}, u32[]{:S(2)}, u32[]{:S(2)}) collective-permute-start(bf16[64,384]{1,0:T(8,128)(2,1)S(1)} %copy-done.6), channel_id=1, source_target_pairs={{0,16},{16,32},{32,48},{48,0},{64,80},{80,96},{96,112},{112,64},{1... | collective-permute-start | bytes 147464 | tf_op jit(solution)/shard_map/ppermute | solution.py:25
  23.2 3.5 %collective-permute-start.4 = (bf16[64,384]{1,0:T(8,128)(2,1)S(1)}, bf16[64,384]{1,0:T(8,128)(2,1)S(1)}, u32[]{:S(2)}, u32[]{:S(2)}) collective-permute-start(bf16[64,384]{1,0:T(8,128)(2,1)S(1)} %copy-done.6), channel_id=1, source_target_pairs={{0,48},{16,0},{32,16},{48,32},{64,112},{80,64},{96,80},{112,96},{1... | collective-permute-start | bytes 147464 | tf_op jit(solution)/shard_map/ppermute | solution.py:25
  26.6 3.3 %collective-permute-start.5 = (bf16[64,384]{1,0:T(8,128)(2,1)S(1)}, bf16[64,384]{1,0:T(8,128)(2,1)S(1)}, u32[]{:S(2)}, u32[]{:S(2)}) collective-permute-start(bf16[64,384]{1,0:T(8,128)(2,1)S(1)} %copy-done.6), channel_id=1, source_target_pairs={{0,32},{16,48},{32,0},{48,16},{64,96},{80,112},{96,64},{112,80},{1... | collective-permute-start | bytes 147464 | tf_op jit(solution)/shard_map/ppermute | solution.py:25
  30.2 5.2 %all-to-all-done = bf16[8,64,384]{2,1,0:T(8,128)(2,1)S(1)} async-done(((bf16[8,64,384]{2,1,0:T(8,128)(2,1)}), bf16[8,64,384]{2,1,0:T(8,128)(2,1)S(1)}, u32[]{:S(2)}, u32[]{:S(2)}) %all-to-all-start) | async-done | bytes 393248 | tf_op jit(solution)/shard_map/all_to_all | solution.py:35
  36.2 3.5 %all-to-all-start.1 = ((bf16[8,64,384]{2,1,0:T(8,128)(2,1)}), bf16[8,64,384]{2,1,0:T(8,128)(2,1)S(1)}, u32[]{:S(2)}, u32[]{:S(2)}) async-start(bf16[8,64,384]{2,1,0:T(8,128)(2,1)} %broadcast_in_dim.62), calls=%async_computation.1 | async-start | bytes 786432 | tf_op jit(solution)/shard_map/all_to_all | solution.py:35
  39.7 2.5 %collective-permute-start = (bf16[8,64,384]{2,1,0:T(8,128)(2,1)S(1)}, bf16[8,64,384]{2,1,0:T(8,128)(2,1)}, u32[]{:S(2)}, u32[]{:S(2)}) collective-permute-start(bf16[8,64,384]{2,1,0:T(8,128)(2,1)S(1)} %all-to-all-done), channel_id=1, source_target_pairs={{0,16},{16,32},{32,48},{48,0},{64,80},{80,96},{96,112},{112,64},{1... | collective-permute-start | bytes 1179656 | tf_op jit(solution)/shard_map/ppermute | solution.py:25
  42.3 3.3 %collective-permute-start.1 = (bf16[8,64,384]{2,1,0:T(8,128)(2,1)S(1)}, bf16[8,64,384]{2,1,0:T(8,128)(2,1)S(1)}, u32[]{:S(2)}, u32[]{:S(2)}) collective-permute-start(bf16[8,64,384]{2,1,0:T(8,128)(2,1)S(1)} %all-to-all-done), channel_id=1, source_target_pairs={{0,48},{16,0},{32,16},{48,32},{64,112},{80,64},{96,80},{112,96},{1... | collective-permute-start | bytes 1179656 | tf_op jit(solution)/shard_map/ppermute | solution.py:25
  45.9 5.9 %collective-permute-done = bf16[8,64,384]{2,1,0:T(8,128)(2,1)} collective-permute-done((bf16[8,64,384]{2,1,0:T(8,128)(2,1)S(1)}, bf16[8,64,384]{2,1,0:T(8,128)(2,1)}, u32[]{:S(2)}, u32[]{:S(2)}) %collective-permute-start) | collective-permute-done | bytes 393248 | tf_op jit(solution)/shard_map/ppermute | solution.py:25
  51.8 3.6 %collective-permute-start.2 = (bf16[8,64,384]{2,1,0:T(8,128)(2,1)}, bf16[8,64,384]{2,1,0:T(8,128)(2,1)}, u32[]{:S(2)}, u32[]{:S(2)}) collective-permute-start(bf16[8,64,384]{2,1,0:T(8,128)(2,1)} %collective-permute-done), channel_id=1, source_target_pairs={{0,16},{16,32},{32,48},{48,0},{64,80},{80,96},{96,112},{112,64},{1... | collective-permute-start | bytes 1179656 | tf_op jit(solution)/shard_map/ppermute | solution.py:25
  56.9 6.8 %all-to-all-start.2 = ((bf16[8,4,64,384]{3,2,1,0:T(8,128)(2,1)}), bf16[8,4,64,384]{3,2,1,0:T(8,128)(2,1)}, u32[]{:S(2)}, u32[]{:S(2)}) async-start(bf16[8,4,64,384]{3,2,1,0:T(8,128)(2,1)} %broadcast_in_dim.72), calls=%async_computation.2 | async-start | bytes 3145728 | tf_op jit(solution)/shard_map/all_to_all | solution.py:35
  64.8 2.2 %collective-permute-start.6 = (bf16[8,64,384]{2,1,0:T(8,128)(2,1)S(1)}, bf16[8,64,384]{2,1,0:T(8,128)(2,1)S(1)}, u32[]{:S(2)}, u32[]{:S(2)}) collective-permute-start(bf16[8,64,384]{2,1,0:T(8,128)(2,1)S(1)} %all-to-all-done.1), channel_id=1, source_target_pairs={{0,16},{16,32},{32,48},{48,0},{64,80},{80,96},{96,112},{112,64},{1... | collective-permute-start | bytes 1179656 | tf_op jit(solution)/shard_map/ppermute | solution.py:25
  67.0 3.7 %collective-permute-start.7 = (bf16[8,64,384]{2,1,0:T(8,128)(2,1)S(1)}, bf16[8,64,384]{2,1,0:T(8,128)(2,1)S(1)}, u32[]{:S(2)}, u32[]{:S(2)}) collective-permute-start(bf16[8,64,384]{2,1,0:T(8,128)(2,1)S(1)} %all-to-all-done.1), channel_id=1, source_target_pairs={{0,48},{16,0},{32,16},{48,32},{64,112},{80,64},{96,80},{112,96},{1... | collective-permute-start | bytes 1179656 | tf_op jit(solution)/shard_map/ppermute | solution.py:25
  71.1 7.1 %collective-permute-done.7 = bf16[8,64,384]{2,1,0:T(8,128)(2,1)S(1)} collective-permute-done((bf16[8,64,384]{2,1,0:T(8,128)(2,1)S(1)}, bf16[8,64,384]{2,1,0:T(8,128)(2,1)S(1)}, u32[]{:S(2)}, u32[]{:S(2)}) %collective-permute-start.7) | collective-permute-done | bytes 393248 | tf_op jit(solution)/shard_map/ppermute | solution.py:25
  78.1 2.2 %collective-permute-start.8 = (bf16[8,64,384]{2,1,0:T(8,128)(2,1)S(1)}, bf16[8,64,384]{2,1,0:T(8,128)(2,1)S(1)}, u32[]{:S(2)}, u32[]{:S(2)}) collective-permute-start(bf16[8,64,384]{2,1,0:T(8,128)(2,1)S(1)} %collective-permute-done.7), channel_id=1, source_target_pairs={{0,48},{16,0},{32,16},{48,32},{64,112},{80,64},{96,80},{112,96},{1... | collective-permute-start | bytes 1179656 | tf_op jit(solution)/shard_map/ppermute | solution.py:25
  80.5 8.5 %collective-permute-done.8 = bf16[8,64,384]{2,1,0:T(8,128)(2,1)S(1)} collective-permute-done((bf16[8,64,384]{2,1,0:T(8,128)(2,1)S(1)}, bf16[8,64,384]{2,1,0:T(8,128)(2,1)S(1)}, u32[]{:S(2)}, u32[]{:S(2)}) %collective-permute-start.8) | collective-permute-done | bytes 393248 | tf_op jit(solution)/shard_map/ppermute | solution.py:25
  93.0 1.9 %copy-done.4 = bf16[768,2048]{1,0:T(8,128)(2,1)S(1)} copy-done((bf16[768,2048]{1,0:T(8,128)(2,1)S(1)}, bf16[768,2048]{1,0:T(8,128)(2,1)}, u32[]{:S(2)}) %copy-start.4) | copy-done | bytes 3145752
  99.4 1.8 %all-to-all-done.2 = bf16[8,4,64,384]{3,2,1,0:T(8,128)(2,1)} async-done(((bf16[8,4,64,384]{3,2,1,0:T(8,128)(2,1)}), bf16[8,4,64,384]{3,2,1,0:T(8,128)(2,1)}, u32[]{:S(2)}, u32[]{:S(2)}) %all-to-all-start.2) | async-done | bytes 1572896 | tf_op jit(solution)/shard_map/all_to_all | solution.py:35
  101.3 2.6 %multiply_convert_fusion = (bf16[384,384]{1,0:T(8,128)(2,1)S(1)}, bf16[384,384]{1,0:T(8,128)(2,1)S(1)}) fusion(f32[384,384]{1,0:T(8,128)S(1)} %copy-done.10, f32[384,384]{1,0:T(8,128)S(1)} %copy-done.8, bf16[384,2048]{1,0:T(8,128)(2,1)S(1)} %slice-done, bf16[2048,384]{1,0:T(8,128)(2,1)} %bitcast.20), kind=kOutput, calls=%fused_computation.14 | convolution fusion | flops 605896704 | bytes 4915200 | tf_op jit(solution)/shard_map/dot_general | solution.py:18
  105.8 2.1 %collective-permute-start.9 = (bf16[8,384,128]{2,1,0:T(8,128)(2,1)S(1)}, bf16[8,384,128]{2,1,0:T(8,128)(2,1)S(1)}, u32[]{:S(2)}, u32[]{:S(2)}) collective-permute-start(bf16[8,384,128]{2,1,0:T(8,128)(2,1)S(1)} %bitcast.94), channel_id=1, source_target_pairs={{0,1},{1,0},{2,3},{3,2},{4,5},{5,4},{6,7},{7,6},{8,9},{9,8},{10,11... | collective-permute-start | bytes 2359304 | tf_op jit(solution)/shard_map/ppermute | solution.py:30
  110.3 30.3 %all_to_all.25 = bf16[8,384,128]{2,1,0:T(8,128)(2,1)S(1)} all-to-all(bf16[8,384,128]{2,1,0:T(8,128)(2,1)S(1)} %fusion.1), channel_id=1, replica_groups={{0,2,4,6,8,10,12,14},{1,3,5,7,9,11,13,15},{16,18,20,22,24,26,28,30},{17..., dimensions={0} | all-to-all | bytes 1572864 | tf_op jit(solution)/shard_map/all_to_all | solution.py:103
  140.6 6.4 %all-to-all-start.4 = ((bf16[8,64,384]{2,1,0:T(8,128)(2,1)}), bf16[8,64,384]{2,1,0:T(8,128)(2,1)S(1)}, u32[]{:S(2)}, u32[]{:S(2)}) async-start(bf16[8,64,384]{2,1,0:T(8,128)(2,1)} %bitcast.95), calls=%async_computation.5 | async-start | bytes 786432 | tf_op jit(solution)/shard_map/all_to_all | solution.py:114
  147.8 12.9 %all-to-all-done.4 = bf16[8,64,384]{2,1,0:T(8,128)(2,1)S(1)} async-done(((bf16[8,64,384]{2,1,0:T(8,128)(2,1)}), bf16[8,64,384]{2,1,0:T(8,128)(2,1)S(1)}, u32[]{:S(2)}, u32[]{:S(2)}) %all-to-all-start.4) | async-done | bytes 393248 | tf_op jit(solution)/shard_map/all_to_all | solution.py:114
  (69 shorter events, 20.0 us)
Async XLA Ops:
  7.2 13.6 %copy-start.6 = (bf16[64,384]{1,0:T(8,128)(2,1)S(1)}, bf16[64,384]{1,0:T(8,128)(2,1)}, u32[]{:S(2)}) copy-start(bf16[64,384]{1,0:T(8,128)(2,1)} %param.9) | copy-start | bytes 147460
  7.2 28.3 %copy-start.5 = (bf16[64,384]{1,0:T(8,128)(2,1)S(1)}, bf16[64,384]{1,0:T(8,128)(2,1)}, u32[]{:S(2)}) copy-start(bf16[64,384]{1,0:T(8,128)(2,1)} %param.8) | copy-start | bytes 147460
  7.2 85.8 %all-gather.2.cloned.1.call-start = ((), (), s32[]{:S(2)}) async-start(), calls=%async_computation.6 | async-start | bytes 3342336 | tf_op jit(solution)/shard_map/all_gather | solution.py:59
  10.4 25.0 %all-to-all-start = ((bf16[8,64,384]{2,1,0:T(8,128)(2,1)}), bf16[8,64,384]{2,1,0:T(8,128)(2,1)S(1)}, u32[]{:S(2)}, u32[]{:S(2)}) async-start(bf16[8,64,384]{2,1,0:T(8,128)(2,1)} %broadcast_in_dim.57), calls=%async_computation | async-start | bytes 786432 | tf_op jit(solution)/shard_map/all_to_all | solution.py:35
  20.8 9.4 %collective-permute-start.3 = (bf16[64,384]{1,0:T(8,128)(2,1)S(1)}, bf16[64,384]{1,0:T(8,128)(2,1)S(1)}, u32[]{:S(2)}, u32[]{:S(2)}) collective-permute-start(bf16[64,384]{1,0:T(8,128)(2,1)S(1)} %copy-done.6), channel_id=1, source_target_pairs={{0,16},{16,32},{32,48},{48,0},{64,80},{80,96},{96,112},{112,64},{1... | collective-permute-start | bytes 147464 | tf_op jit(solution)/shard_map/ppermute | solution.py:25
  23.2 16.5 %collective-permute-start.4 = (bf16[64,384]{1,0:T(8,128)(2,1)S(1)}, bf16[64,384]{1,0:T(8,128)(2,1)S(1)}, u32[]{:S(2)}, u32[]{:S(2)}) collective-permute-start(bf16[64,384]{1,0:T(8,128)(2,1)S(1)} %copy-done.6), channel_id=1, source_target_pairs={{0,48},{16,0},{32,16},{48,32},{64,112},{80,64},{96,80},{112,96},{1... | collective-permute-start | bytes 147464 | tf_op jit(solution)/shard_map/ppermute | solution.py:25
  26.6 15.6 %collective-permute-start.5 = (bf16[64,384]{1,0:T(8,128)(2,1)S(1)}, bf16[64,384]{1,0:T(8,128)(2,1)S(1)}, u32[]{:S(2)}, u32[]{:S(2)}) collective-permute-start(bf16[64,384]{1,0:T(8,128)(2,1)S(1)} %copy-done.6), channel_id=1, source_target_pairs={{0,32},{16,48},{32,0},{48,16},{64,96},{80,112},{96,64},{112,80},{1... | collective-permute-start | bytes 147464 | tf_op jit(solution)/shard_map/ppermute | solution.py:25
  36.2 19.2 %all-to-all-start.1 = ((bf16[8,64,384]{2,1,0:T(8,128)(2,1)}), bf16[8,64,384]{2,1,0:T(8,128)(2,1)S(1)}, u32[]{:S(2)}, u32[]{:S(2)}) async-start(bf16[8,64,384]{2,1,0:T(8,128)(2,1)} %broadcast_in_dim.62), calls=%async_computation.1 | async-start | bytes 786432 | tf_op jit(solution)/shard_map/all_to_all | solution.py:35
  39.7 12.1 %collective-permute-start = (bf16[8,64,384]{2,1,0:T(8,128)(2,1)S(1)}, bf16[8,64,384]{2,1,0:T(8,128)(2,1)}, u32[]{:S(2)}, u32[]{:S(2)}) collective-permute-start(bf16[8,64,384]{2,1,0:T(8,128)(2,1)S(1)} %all-to-all-done), channel_id=1, source_target_pairs={{0,16},{16,32},{32,48},{48,0},{64,80},{80,96},{96,112},{112,64},{1... | collective-permute-start | bytes 1179656 | tf_op jit(solution)/shard_map/ppermute | solution.py:25
  42.3 28.4 %collective-permute-start.1 = (bf16[8,64,384]{2,1,0:T(8,128)(2,1)S(1)}, bf16[8,64,384]{2,1,0:T(8,128)(2,1)S(1)}, u32[]{:S(2)}, u32[]{:S(2)}) collective-permute-start(bf16[8,64,384]{2,1,0:T(8,128)(2,1)S(1)} %all-to-all-done), channel_id=1, source_target_pairs={{0,48},{16,0},{32,16},{48,32},{64,112},{80,64},{96,80},{112,96},{1... | collective-permute-start | bytes 1179656 | tf_op jit(solution)/shard_map/ppermute | solution.py:25
  51.8 28.7 %collective-permute-start.2 = (bf16[8,64,384]{2,1,0:T(8,128)(2,1)}, bf16[8,64,384]{2,1,0:T(8,128)(2,1)}, u32[]{:S(2)}, u32[]{:S(2)}) collective-permute-start(bf16[8,64,384]{2,1,0:T(8,128)(2,1)} %collective-permute-done), channel_id=1, source_target_pairs={{0,16},{16,32},{32,48},{48,0},{64,80},{80,96},{96,112},{112,64},{1... | collective-permute-start | bytes 1179656 | tf_op jit(solution)/shard_map/ppermute | solution.py:25
  56.9 44.4 %all-to-all-start.2 = ((bf16[8,4,64,384]{3,2,1,0:T(8,128)(2,1)}), bf16[8,4,64,384]{3,2,1,0:T(8,128)(2,1)}, u32[]{:S(2)}, u32[]{:S(2)}) async-start(bf16[8,4,64,384]{3,2,1,0:T(8,128)(2,1)} %broadcast_in_dim.72), calls=%async_computation.2 | async-start | bytes 3145728 | tf_op jit(solution)/shard_map/all_to_all | solution.py:35
  63.7 76.9 %reduce-scatter.2.cloned.1.call-start = ((), (), s32[]{:S(2)}) async-start(), calls=%async_computation.7 | async-start | bytes 1966080 | tf_op jit(solution)/shard_map/reduce_scatter | solution.py:105
  64.8 15.6 %collective-permute-start.6 = (bf16[8,64,384]{2,1,0:T(8,128)(2,1)S(1)}, bf16[8,64,384]{2,1,0:T(8,128)(2,1)S(1)}, u32[]{:S(2)}, u32[]{:S(2)}) collective-permute-start(bf16[8,64,384]{2,1,0:T(8,128)(2,1)S(1)} %all-to-all-done.1), channel_id=1, source_target_pairs={{0,16},{16,32},{32,48},{48,0},{64,80},{80,96},{96,112},{112,64},{1... | collective-permute-start | bytes 1179656 | tf_op jit(solution)/shard_map/ppermute | solution.py:25
  67.0 11.2 %collective-permute-start.7 = (bf16[8,64,384]{2,1,0:T(8,128)(2,1)S(1)}, bf16[8,64,384]{2,1,0:T(8,128)(2,1)S(1)}, u32[]{:S(2)}, u32[]{:S(2)}) collective-permute-start(bf16[8,64,384]{2,1,0:T(8,128)(2,1)S(1)} %all-to-all-done.1), channel_id=1, source_target_pairs={{0,48},{16,0},{32,16},{48,32},{64,112},{80,64},{96,80},{112,96},{1... | collective-permute-start | bytes 1179656 | tf_op jit(solution)/shard_map/ppermute | solution.py:25
  78.1 10.9 %collective-permute-start.8 = (bf16[8,64,384]{2,1,0:T(8,128)(2,1)S(1)}, bf16[8,64,384]{2,1,0:T(8,128)(2,1)S(1)}, u32[]{:S(2)}, u32[]{:S(2)}) collective-permute-start(bf16[8,64,384]{2,1,0:T(8,128)(2,1)S(1)} %collective-permute-done.7), channel_id=1, source_target_pairs={{0,48},{16,0},{32,16},{48,32},{64,112},{80,64},{96,80},{112,96},{1... | collective-permute-start | bytes 1179656 | tf_op jit(solution)/shard_map/ppermute | solution.py:25
  92.9 1.9 %copy-start.4 = (bf16[768,2048]{1,0:T(8,128)(2,1)S(1)}, bf16[768,2048]{1,0:T(8,128)(2,1)}, u32[]{:S(2)}) copy-start(bf16[768,2048]{1,0:T(8,128)(2,1)} %all-gather.2.cloned.1.call-done) | copy-start | bytes 9437188
  98.1 3.2 %copy-start.8 = (f32[384,384]{1,0:T(8,128)S(1)}, f32[384,384]{1,0:T(8,128)}, u32[]{:S(2)}) copy-start(f32[384,384]{1,0:T(8,128)} %copy-done.7) | copy-start | bytes 1769476
  98.1 3.2 %copy-start.10 = (f32[384,384]{1,0:T(8,128)S(1)}, f32[384,384]{1,0:T(8,128)}, u32[]{:S(2)}) copy-start(f32[384,384]{1,0:T(8,128)} %copy-done.9) | copy-start | bytes 1769476
  101.3 2.6 %copy-start.3 = (bf16[8,1,128,384]{3,2,1,0:T(8,128)(2,1)S(1)}, bf16[8,1,128,384]{3,2,1,0:T(8,128)(2,1)}, u32[]{:S(2)}) copy-start(bf16[8,1,128,384]{3,2,1,0:T(8,128)(2,1)} %get-tuple-element.20) | copy-start | bytes 2359300
  105.6 2.2 %copy-start.2 = (bf16[8,1,128,384]{3,2,1,0:T(8,128)(2,1)S(1)}, bf16[8,1,128,384]{3,2,1,0:T(8,128)(2,1)}, u32[]{:S(2)}) copy-start(bf16[8,1,128,384]{3,2,1,0:T(8,128)(2,1)} %get-tuple-element.21) | copy-start | bytes 2359300
  105.8 2.7 %copy-start = (bf16[8,1,128,384]{3,2,1,0:T(8,128)(2,1)S(1)}, bf16[8,1,128,384]{3,2,1,0:T(8,128)(2,1)}, u32[]{:S(2)}) copy-start(bf16[8,1,128,384]{3,2,1,0:T(8,128)(2,1)} %get-tuple-element.19) | copy-start | bytes 2359300
  105.8 4.3 %collective-permute-start.9 = (bf16[8,384,128]{2,1,0:T(8,128)(2,1)S(1)}, bf16[8,384,128]{2,1,0:T(8,128)(2,1)S(1)}, u32[]{:S(2)}, u32[]{:S(2)}) collective-permute-start(bf16[8,384,128]{2,1,0:T(8,128)(2,1)S(1)} %bitcast.94), channel_id=1, source_target_pairs={{0,1},{1,0},{2,3},{3,2},{4,5},{5,4},{6,7},{7,6},{8,9},{9,8},{10,11... | collective-permute-start | bytes 2359304 | tf_op jit(solution)/shard_map/ppermute | solution.py:30
  140.6 20.1 %all-to-all-start.4 = ((bf16[8,64,384]{2,1,0:T(8,128)(2,1)}), bf16[8,64,384]{2,1,0:T(8,128)(2,1)S(1)}, u32[]{:S(2)}, u32[]{:S(2)}) async-start(bf16[8,64,384]{2,1,0:T(8,128)(2,1)} %bitcast.95), calls=%async_computation.5 | async-start | bytes 786432 | tf_op jit(solution)/shard_map/all_to_all | solution.py:114
  (4 other events, 5.2 us)
Sparse Core Ops, SparseCore 0:
  10.1 52.2 all-gather.1
  99.6 30.9 reduce-scatter.1
where the time goes:
time: 169 us; the launch traced here: 168 us
  starting transfers between devices  55.8 us (33%)
  waiting for transfers between devices  42.4 us (25%)
  blocking collectives  30.3 us (18%)
  between operations  14.7 us (9%)
  local copies, waits for them, and re-layouts  13.6 us (8%)
  matrix products  8.15 us (5%)
  other arithmetic  3.21 us (2%)
    all_to_all x1, blocking collectives, on_device(): summed = lax.all_to_all(pair_sum, 'mp', 0, 0, axis_index_groups=Y_GROUPS)  30.3 us
    ppermute x9, starting transfers between devices, send_x(): return lax.ppermute(value, 'fsdp', pairs)  26.6 us
    ppermute x9, waiting for transfers between devices, send_x(): return lax.ppermute(value, 'fsdp', pairs)  21.5 us
    all_to_all x3, starting transfers between devices, gather_z(): return lax.all_to_all(copies, 'fsdp', 0, 0, axis_index_groups=Z_GROUPS)  20.6 us
    all_to_all x1, waiting for transfers between devices, on_device(): down_z = lax.all_to_all(down_z, 'fsdp', 0, 0, axis_index_groups=Z_GROUPS)  12.9 us
    dot_general x8, matrix products, dot(): lax.dot_general(left, right, (dims, ((), ())), preferred_element_type=jnp...  8.15 us
    all_to_all x3, waiting for transfers between devices, gather_z(): return lax.all_to_all(copies, 'fsdp', 0, 0, axis_index_groups=Z_GROUPS)  7.09 us
    all_to_all x1, starting transfers between devices, on_device(): down_z = lax.all_to_all(down_z, 'fsdp', 0, 0, axis_index_groups=Z_GROUPS)  6.44 us
  transfers between devices with their start and end apart: 16, of which 7 were waited for; matrix products, arithmetic and copies ran while one was open for 12% of the time, Pallas kernels for 0%

commit v1 on v0

--- a/solution.py
+++ b/solution.py
@@ -39,11 +39,9 @@
     return left.astype(jnp.float32) + right.astype(jnp.float32)
 
 
-def put_x(blocks, me):
-    n_z, rows, cols = blocks[0].shape
-    full = jnp.zeros((n_z, N_X, rows, cols), blocks[0].dtype)
+def put_x(full, blocks, me, row):
     for block, step in zip(blocks, (0, N_X - 1, 1, 2)):
-        full = lax.dynamic_update_slice(full, block[:, None], (0, (me + step) % N_X, 0, 0))
+        full = lax.dynamic_update_slice(full, block[:, None], (0, (me + step) % N_X, row, 0))
     return full
 
 
@@ -59,23 +57,34 @@
     both = lax.all_gather(stacked, "mp", axis=1, tiled=True)
     token_rows, cotangent_rows = both[:rows], both[rows:]
 
-    down_x = jnp.zeros((N_X, depth, cols), down_weight.dtype)
-    down_x = lax.dynamic_update_slice(down_x, down_weight[None], (me_x, 0, 0))
+    part = depth // 4
+    piece_a = jnp.concatenate([gate_weight, down_weight[:part]])
+    piece_b = jnp.concatenate([up_weight, down_weight[part : 2 * part]])
+    rest = down_weight[2 * part :]
+    rest_x = jnp.zeros((N_X,) + rest.shape, rest.dtype)
+    rest_x = lax.dynamic_update_slice(rest_x, rest[None], (me_x, 0, 0))
     for step in (1, N_X - 1, 2):
-        block = send_x(down_weight, step)
-        down_x = lax.dynamic_update_slice(down_x, block[None], ((me_x - step) % N_X, 0, 0))
+        block = send_x(rest, step)
+        rest_x = lax.dynamic_update_slice(rest_x, block[None], ((me_x - step) % N_X, 0, 0))
 
-    gate_z = gather_z(gate_weight)
-    gate_z, up_weight = lax.optimization_barrier((gate_z, up_weight))
-    up_z = gather_z(up_weight)
-    up_z, down_x = lax.optimization_barrier((up_z, down_x))
-    down_full = gather_z(down_x).reshape(-1, cols)
+    a_own = gather_z(piece_a)
+    a_own, piece_b = lax.optimization_barrier((a_own, piece_b))
+    b_own = gather_z(piece_b)
+    a_left, a_right = send_x(a_own, 1), send_x(a_own, -1)
+    a_left, b_own = lax.optimization_barrier((a_left, b_own))
+    b_right, b_left = send_x(b_own, -1), send_x(b_own, 1)
+    b_right, rest_x = lax.optimization_barrier((b_right, rest_x))
+    a_far, b_far = send_x(a_left, 1), send_x(b_right, -1)
+    rest_z = gather_z(rest_x)
 
-    gate_left, gate_right = send_x(gate_z, 1), send_x(gate_z, -1)
-    up_right, up_left = send_x(up_z, -1), send_x(up_z, 1)
-    gate_far, up_far = send_x(gate_left, 1), send_x(up_right, -1)
-    gate_full = put_x((gate_z, gate_left, gate_right, gate_far), me_x).reshape(-1, cols)
-    up_full = put_x((up_z, up_left, up_right, up_far), me_x).reshape(-1, cols)
+    a_blocks, b_blocks = (a_own, a_left, a_right, a_far), (b_own, b_left, b_right, b_far)
+    empty = jnp.zeros((N_Z, N_X, depth, cols), gate_weight.dtype)
+    gate_full = put_x(empty, [v[:, :depth] for v in a_blocks], me_x, 0).reshape(-1, cols)
+    up_full = put_x(empty, [v[:, :depth] for v in b_blocks], me_x, 0).reshape(-1, cols)
+    down_full = put_x(empty, [v[:, depth:] for v in a_blocks], me_x, 0)
+    down_full = put_x(down_full, [v[:, depth:] for v in b_blocks], me_x, part)
+    down_full = lax.dynamic_update_slice(down_full, rest_z, (0, 0, 2 * part, 0))
+    down_full = down_full.reshape(-1, cols)
 
     gate_value = dot(token_rows, gate_full, ((1,), (0,)))
     up_value = dot(token_rows, up_full, ((1,), (0,)))
@@ -103,16 +112,12 @@
     summed = lax.all_to_all(pair_sum, "mp", 0, 0, axis_index_groups=Y_GROUPS)
 
     down_z = lax.psum_scatter(
-        down_partial.reshape(N_Z, N_X, depth, cols).transpose(1, 0, 2, 3).reshape(-1, cols),
-        "fsdp",
-        scatter_dimension=0,
-        axis_index_groups=X_GROUPS,
-        tiled=True,
-    ).reshape(N_Z, depth, cols)
+        down_partial, "fsdp", scatter_dimension=0, axis_index_groups=Z_GROUPS, tiled=True
+    ).reshape(N_X, depth, cols)
     summed, down_z = lax.optimization_barrier((summed, down_z))
     input_grad = summed.astype(jnp.float32).sum(0).astype(jnp.bfloat16)
-    down_z = lax.all_to_all(down_z, "fsdp", 0, 0, axis_index_groups=Z_GROUPS)
-    grad_down = (down_z.astype(jnp.float32).sum(0) * factor).astype(jnp.bfloat16)
+    down_x = lax.all_to_all(down_z, "fsdp", 0, 0, axis_index_groups=X_GROUPS)
+    grad_down = (down_x.astype(jnp.float32).sum(0) * factor).astype(jnp.bfloat16)
     return (input_grad, grad_down)
 
 

time: 169 us -> 179 us (1.059); the launches traced: 168 us -> 176 us
  local copies, waits for them, and re-layouts: 13.6 us -> 34.5 us
  waiting for transfers between devices: 42.4 us -> 29.2 us
    dynamic_update_slice x11 -> x20, local copies, waits for them, and re-layouts: 2.63 us -> 22.5 us  [the longest x15 20.2 us: put_x(): lax.dynamic_update_slice(full, block[:, None], (0, (me + step) % N_X, row...]
    ppermute x9, waiting for transfers between devices: 21.5 us -> 7.75 us  [send_x(): return lax.ppermute(value, 'fsdp', pairs)]
    all_to_all x3, waiting for transfers between devices: 7.09 us -> 16.9 us  [gather_z(): return lax.all_to_all(copies, 'fsdp', 0, 0, axis_index_groups=Z_GROUPS)]
    all_to_all x1, waiting for transfers between devices: 12.9 us -> 3.5 us  [on_device(): down_x = lax.all_to_all(down_z, 'fsdp', 0, 0, axis_index_groups=X_GROUPS)]
    broadcast_in_dim x1 -> x4, local copies, waits for them, and re-layouts: 0.02 us -> 1.91 us  [the longest x3 1.9 us: on_device(): empty = jnp.zeros((N_Z, N_X, depth, cols), gate_weight.dtype)]
  transfers between devices with their start and end apart: 16 -> 16, of which waited for: 7 -> 7; matrix products, arithmetic and copies ran while one was open for 12% -> 21% of each run, Pallas kernels for 0% -> 0%
where the time goes in v1:
time: 179 us; the launch traced here: 176 us
  starting transfers between devices  54.1 us (30%)
  local copies, waits for them, and re-layouts  34.5 us (19%)
  blocking collectives  30.3 us (17%)
  waiting for transfers between devices  29.2 us (16%)
  between operations  14.6 us (8%)
  matrix products  9.49 us (5%)
  other arithmetic  4.06 us (2%)
    all_to_all x1, blocking collectives, on_device(): summed = lax.all_to_all(pair_sum, 'mp', 0, 0, axis_index_groups=Y_GROUPS)  30.3 us
    ppermute x9, starting transfers between devices, send_x(): return lax.ppermute(value, 'fsdp', pairs)  26.7 us
    dynamic_update_slice x15, local copies, waits for them, and re-layouts, put_x(): lax.dynamic_update_slice(full, block[:, None], (0, (me + step) % N_X, row...  20.2 us
    all_to_all x3, starting transfers between devices, gather_z(): return lax.all_to_all(copies, 'fsdp', 0, 0, axis_index_groups=Z_GROUPS)  19.1 us
    all_to_all x3, waiting for transfers between devices, gather_z(): return lax.all_to_all(copies, 'fsdp', 0, 0, axis_index_groups=Z_GROUPS)  16.9 us
    dot_general x8, matrix products, dot(): lax.dot_general(left, right, (dims, ((), ())), preferred_element_type=jnp...  9.49 us
    ppermute x9, waiting for transfers between devices, send_x(): return lax.ppermute(value, 'fsdp', pairs)  7.75 us
    all_to_all x1, starting transfers between devices, on_device(): down_x = lax.all_to_all(down_z, 'fsdp', 0, 0, axis_index_groups=X_GROUPS)  6.25 us
  transfers between devices with their start and end apart: 16, of which 7 were waited for; matrix products, arithmetic and copies ran while one was open for 21% of the time, Pallas kernels for 0%

profile of v1, /device:TPU:6, one launch (start us, length us, event | category | flops | bytes accessed | tf_op | source)
XLA Modules:
  0.0 176.3 jit_solution(18193266856302805723)
XLA Ops:
  11.2 10.3 %all-to-all-start = ((bf16[8,80,384]{2,1,0:T(8,128)(2,1)}), bf16[8,80,384]{2,1,0:T(8,128)(2,1)}, u32[]{:S(2)}, u32[]{:S(2)}) async-start(bf16[8,80,384]{2,1,0:T(8,128)(2,1)} %broadcast_in_dim.85), calls=%async_computation | async-start | bytes 983040 | tf_op jit(solution)/shard_map/all_to_all | solution.py:35
  21.6 2.4 %collective-permute-start.5 = (bf16[32,384]{1,0:T(8,128)(2,1)S(1)}, bf16[32,384]{1,0:T(8,128)(2,1)S(1)}, u32[]{:S(2)}, u32[]{:S(2)}) collective-permute-start(bf16[32,384]{1,0:T(8,128)(2,1)S(1)} %slice.73), channel_id=1, source_target_pairs={{0,16},{16,32},{32,48},{48,0},{64,80},{80,96},{96,112},{112,64},{1... | collective-permute-start | bytes 73736 | tf_op jit(solution)/shard_map/ppermute | solution.py:25
  24.0 3.5 %collective-permute-start.6 = (bf16[32,384]{1,0:T(8,128)(2,1)S(1)}, bf16[32,384]{1,0:T(8,128)(2,1)S(1)}, u32[]{:S(2)}, u32[]{:S(2)}) collective-permute-start(bf16[32,384]{1,0:T(8,128)(2,1)S(1)} %slice.73), channel_id=1, source_target_pairs={{0,48},{16,0},{32,16},{48,32},{64,112},{80,64},{96,80},{112,96},{1... | collective-permute-start | bytes 73736 | tf_op jit(solution)/shard_map/ppermute | solution.py:25
  27.4 3.3 %collective-permute-start.7 = (bf16[32,384]{1,0:T(8,128)(2,1)S(1)}, bf16[32,384]{1,0:T(8,128)(2,1)S(1)}, u32[]{:S(2)}, u32[]{:S(2)}) collective-permute-start(bf16[32,384]{1,0:T(8,128)(2,1)S(1)} %slice.73), channel_id=1, source_target_pairs={{0,32},{16,48},{32,0},{48,16},{64,96},{80,112},{96,64},{112,80},{1... | collective-permute-start | bytes 73736 | tf_op jit(solution)/shard_map/ppermute | solution.py:25
  31.0 7.4 %all-to-all-done = bf16[8,80,384]{2,1,0:T(8,128)(2,1)} async-done(((bf16[8,80,384]{2,1,0:T(8,128)(2,1)}), bf16[8,80,384]{2,1,0:T(8,128)(2,1)}, u32[]{:S(2)}, u32[]{:S(2)}) %all-to-all-start) | async-done | bytes 491552 | tf_op jit(solution)/shard_map/all_to_all | solution.py:35
  39.3 4.1 %all-to-all-start.1 = ((bf16[8,80,384]{2,1,0:T(8,128)(2,1)}), bf16[8,80,384]{2,1,0:T(8,128)(2,1)}, u32[]{:S(2)}, u32[]{:S(2)}) async-start(bf16[8,80,384]{2,1,0:T(8,128)(2,1)} %broadcast_in_dim.87), calls=%async_computation.1 | async-start | bytes 983040 | tf_op jit(solution)/shard_map/all_to_all | solution.py:35
  43.5 2.4 %collective-permute-start = (bf16[8,80,384]{2,1,0:T(8,128)(2,1)}, bf16[8,80,384]{2,1,0:T(8,128)(2,1)}, u32[]{:S(2)}, u32[]{:S(2)}) collective-permute-start(bf16[8,80,384]{2,1,0:T(8,128)(2,1)} %all-to-all-done), channel_id=1, source_target_pairs={{0,16},{16,32},{32,48},{48,0},{64,80},{80,96},{96,112},{112,64},{1... | collective-permute-start | bytes 1474568 | tf_op jit(solution)/shard_map/ppermute | solution.py:25
  45.9 3.5 %collective-permute-start.1 = (bf16[8,80,384]{2,1,0:T(8,128)(2,1)}, bf16[8,80,384]{2,1,0:T(8,128)(2,1)}, u32[]{:S(2)}, u32[]{:S(2)}) collective-permute-start(bf16[8,80,384]{2,1,0:T(8,128)(2,1)} %all-to-all-done), channel_id=1, source_target_pairs={{0,48},{16,0},{32,16},{48,32},{64,112},{80,64},{96,80},{112,96},{1... | collective-permute-start | bytes 1474568 | tf_op jit(solution)/shard_map/ppermute | solution.py:25
  53.7 5.1 %collective-permute-done = bf16[8,80,384]{2,1,0:T(8,128)(2,1)} collective-permute-done((bf16[8,80,384]{2,1,0:T(8,128)(2,1)}, bf16[8,80,384]{2,1,0:T(8,128)(2,1)}, u32[]{:S(2)}, u32[]{:S(2)}) %collective-permute-start) | collective-permute-done | bytes 491552 | tf_op jit(solution)/shard_map/ppermute | solution.py:25
  60.7 2.4 %collective-permute-start.3 = (bf16[8,80,384]{2,1,0:T(8,128)(2,1)}, bf16[8,80,384]{2,1,0:T(8,128)(2,1)}, u32[]{:S(2)}, u32[]{:S(2)}) collective-permute-start(bf16[8,80,384]{2,1,0:T(8,128)(2,1)} %all-to-all-done.1), channel_id=1, source_target_pairs={{0,16},{16,32},{32,48},{48,0},{64,80},{80,96},{96,112},{112,64},{1... | collective-permute-start | bytes 1474568 | tf_op jit(solution)/shard_map/ppermute | solution.py:25
  63.1 3.5 %collective-permute-start.4 = (bf16[8,80,384]{2,1,0:T(8,128)(2,1)}, bf16[8,80,384]{2,1,0:T(8,128)(2,1)}, u32[]{:S(2)}, u32[]{:S(2)}) collective-permute-start(bf16[8,80,384]{2,1,0:T(8,128)(2,1)} %all-to-all-done.1), channel_id=1, source_target_pairs={{0,48},{16,0},{32,16},{48,32},{64,112},{80,64},{96,80},{112,96},{1... | collective-permute-start | bytes 1474568 | tf_op jit(solution)/shard_map/ppermute | solution.py:25
  66.5 3.6 %collective-permute-start.2 = (bf16[8,80,384]{2,1,0:T(8,128)(2,1)}, bf16[8,80,384]{2,1,0:T(8,128)(2,1)}, u32[]{:S(2)}, u32[]{:S(2)}) collective-permute-start(bf16[8,80,384]{2,1,0:T(8,128)(2,1)} %collective-permute-done), channel_id=1, source_target_pairs={{0,16},{16,32},{32,48},{48,0},{64,80},{80,96},{96,112},{112,64},{1... | collective-permute-start | bytes 1474568 | tf_op jit(solution)/shard_map/ppermute | solution.py:25
  76.7 2.6 %collective-permute-done.4 = bf16[8,80,384]{2,1,0:T(8,128)(2,1)} collective-permute-done((bf16[8,80,384]{2,1,0:T(8,128)(2,1)}, bf16[8,80,384]{2,1,0:T(8,128)(2,1)}, u32[]{:S(2)}, u32[]{:S(2)}) %collective-permute-start.4) | collective-permute-done | bytes 491552 | tf_op jit(solution)/shard_map/ppermute | solution.py:25
  79.3 2.2 %collective-permute-start.8 = (bf16[8,80,384]{2,1,0:T(8,128)(2,1)}, bf16[8,80,384]{2,1,0:T(8,128)(2,1)}, u32[]{:S(2)}, u32[]{:S(2)}) collective-permute-start(bf16[8,80,384]{2,1,0:T(8,128)(2,1)} %collective-permute-done.4), channel_id=1, source_target_pairs={{0,48},{16,0},{32,16},{48,32},{64,112},{80,64},{96,80},{112,96},{1... | collective-permute-start | bytes 1474568 | tf_op jit(solution)/shard_map/ppermute | solution.py:25
  82.6 4.6 %all-to-all-start.2 = ((bf16[8,4,32,384]{3,2,1,0:T(8,128)(2,1)}), bf16[8,4,32,384]{3,2,1,0:T(8,128)(2,1)}, u32[]{:S(2)}, u32[]{:S(2)}) async-start(bf16[8,4,32,384]{3,2,1,0:T(8,128)(2,1)} %broadcast_in_dim.108), calls=%async_computation.2 | async-start | bytes 1572864 | tf_op jit(solution)/shard_map/all_to_all | solution.py:35
  101.3 7.6 %all-to-all-done.2 = bf16[8,4,32,384]{3,2,1,0:T(8,128)(2,1)} async-done(((bf16[8,4,32,384]{3,2,1,0:T(8,128)(2,1)}), bf16[8,4,32,384]{3,2,1,0:T(8,128)(2,1)}, u32[]{:S(2)}, u32[]{:S(2)}) %all-to-all-start.2) | async-done | bytes 786464 | tf_op jit(solution)/shard_map/all_to_all | solution.py:35
  109.0 2.2 %constant_dynamic-update-slice_fusion = bf16[8,4,64,384]{3,2,1,0:T(8,128)(2,1)} fusion(bf16[8,4,64,384]{3,2,1,0:T(8,128)(2,1)} %fusion.12, bf16[8,4,32,384]{3,2,1,0:T(8,128)(2,1)} %all-to-all-done.2), kind=kLoop, calls=%fused_computation.55 | loop fusion | bytes 1572864 | tf_op jit(solution)/shard_map/dynamic_update_slice | solution.py:86
  111.2 1.9 %copy-done.4 = bf16[768,2048]{1,0:T(8,128)(2,1)S(1)} copy-done((bf16[768,2048]{1,0:T(8,128)(2,1)S(1)}, bf16[768,2048]{1,0:T(8,128)(2,1)}, u32[]{:S(2)}) %copy-start.4) | copy-done | bytes 3145752
  115.1 2.4 %convolution_convert_fusion = bf16[2048,384]{1,0:T(8,128)(2,1)} fusion(f32[384,384]{1,0:T(8,128)S(1)} %fusion.2, f32[384,384]{1,0:T(8,128)S(1)} %fusion.4, bf16[768,2048]{1,0:T(8,128)(2,1)S(1)} %copy-done.4), kind=kOutput, calls=%fused_computation | convolution fusion | flops 605650944 | bytes 4325376 | tf_op jit(solution)/shard_map/dot_general | solution.py:18
  118.9 2.7 %multiply_convert_fusion = (bf16[384,384]{1,0:T(8,128)(2,1)S(1)}, bf16[384,384]{1,0:T(8,128)(2,1)S(1)}) fusion(f32[384,384]{1,0:T(8,128)S(1)} %fusion.4, f32[384,384]{1,0:T(8,128)} %copy-done.7, bf16[384,2048]{1,0:T(8,128)(2,1)S(1)} %slice-done, bf16[2048,384]{1,0:T(8,128)(2,1)} %bitcast.36), kind=kOutput, calls=%fused_computation.13 | convolution fusion | flops 605896704 | bytes 4915200 | tf_op jit(solution)/shard_map/dot_general | solution.py:18
  123.5 2.1 %collective-permute-start.9 = (bf16[8,384,128]{2,1,0:T(8,128)(2,1)S(1)}, bf16[8,384,128]{2,1,0:T(8,128)(2,1)S(1)}, u32[]{:S(2)}, u32[]{:S(2)}) collective-permute-start(bf16[8,384,128]{2,1,0:T(8,128)(2,1)S(1)} %bitcast.136), channel_id=1, source_target_pairs={{0,1},{1,0},{2,3},{3,2},{4,5},{5,4},{6,7},{7,6},{8,9},{9,8},{10,11... | collective-permute-start | bytes 2359304 | tf_op jit(solution)/shard_map/ppermute | solution.py:30
  128.0 30.3 %all_to_all.25 = bf16[8,384,128]{2,1,0:T(8,128)(2,1)S(1)} all-to-all(bf16[8,384,128]{2,1,0:T(8,128)(2,1)S(1)} %fusion.1), channel_id=1, replica_groups={{0,2,4,6,8,10,12,14},{1,3,5,7,9,11,13,15},{16,18,20,22,24,26,28,30},{17..., dimensions={0} | all-to-all | bytes 1572864 | tf_op jit(solution)/shard_map/all_to_all | solution.py:112
  158.3 6.3 %all-to-all-start.4 = ((bf16[4,64,384]{2,1,0:T(8,128)(2,1)}), bf16[4,64,384]{2,1,0:T(8,128)(2,1)S(1)}, u32[]{:S(2)}, u32[]{:S(2)}) async-start(bf16[4,64,384]{2,1,0:T(8,128)(2,1)} %bitcast.137), calls=%async_computation.5 | async-start | bytes 393216 | tf_op jit(solution)/shard_map/all_to_all | solution.py:119
  165.3 3.5 %all-to-all-done.4 = bf16[4,64,384]{2,1,0:T(8,128)(2,1)S(1)} async-done(((bf16[4,64,384]{2,1,0:T(8,128)(2,1)}), bf16[4,64,384]{2,1,0:T(8,128)(2,1)S(1)}, u32[]{:S(2)}, u32[]{:S(2)}) %all-to-all-start.4) | async-done | bytes 196640 | tf_op jit(solution)/shard_map/all_to_all | solution.py:119
  (76 shorter events, 41.9 us)
Async XLA Ops:
  7.2 14.4 %copy-start.5 = (bf16[64,384]{1,0:T(8,128)(2,1)S(1)}, bf16[64,384]{1,0:T(8,128)(2,1)}, u32[]{:S(2)}) copy-start(bf16[64,384]{1,0:T(8,128)(2,1)} %param.9) | copy-start | bytes 147460
  7.2 23.6 %copy-start.6 = (bf16[64,384]{1,0:T(8,128)(2,1)S(1)}, bf16[64,384]{1,0:T(8,128)(2,1)}, u32[]{:S(2)}) copy-start(bf16[64,384]{1,0:T(8,128)(2,1)} %param.8) | copy-start | bytes 147460
  7.2 104.0 %all-gather.2.cloned.1.call-start = ((), (), s32[]{:S(2)}) async-start(), calls=%async_computation.6 | async-start | bytes 3342336 | tf_op jit(solution)/shard_map/all_gather | solution.py:57
  11.2 27.2 %all-to-all-start = ((bf16[8,80,384]{2,1,0:T(8,128)(2,1)}), bf16[8,80,384]{2,1,0:T(8,128)(2,1)}, u32[]{:S(2)}, u32[]{:S(2)}) async-start(bf16[8,80,384]{2,1,0:T(8,128)(2,1)} %broadcast_in_dim.85), calls=%async_computation | async-start | bytes 983040 | tf_op jit(solution)/shard_map/all_to_all | solution.py:35
  21.6 9.4 %collective-permute-start.5 = (bf16[32,384]{1,0:T(8,128)(2,1)S(1)}, bf16[32,384]{1,0:T(8,128)(2,1)S(1)}, u32[]{:S(2)}, u32[]{:S(2)}) collective-permute-start(bf16[32,384]{1,0:T(8,128)(2,1)S(1)} %slice.73), channel_id=1, source_target_pairs={{0,16},{16,32},{32,48},{48,0},{64,80},{80,96},{96,112},{112,64},{1... | collective-permute-start | bytes 73736 | tf_op jit(solution)/shard_map/ppermute | solution.py:25
  24.0 19.5 %collective-permute-start.6 = (bf16[32,384]{1,0:T(8,128)(2,1)S(1)}, bf16[32,384]{1,0:T(8,128)(2,1)S(1)}, u32[]{:S(2)}, u32[]{:S(2)}) collective-permute-start(bf16[32,384]{1,0:T(8,128)(2,1)S(1)} %slice.73), channel_id=1, source_target_pairs={{0,48},{16,0},{32,16},{48,32},{64,112},{80,64},{96,80},{112,96},{1... | collective-permute-start | bytes 73736 | tf_op jit(solution)/shard_map/ppermute | solution.py:25
  27.4 18.4 %collective-permute-start.7 = (bf16[32,384]{1,0:T(8,128)(2,1)S(1)}, bf16[32,384]{1,0:T(8,128)(2,1)S(1)}, u32[]{:S(2)}, u32[]{:S(2)}) collective-permute-start(bf16[32,384]{1,0:T(8,128)(2,1)S(1)} %slice.73), channel_id=1, source_target_pairs={{0,32},{16,48},{32,0},{48,16},{64,96},{80,112},{96,64},{112,80},{1... | collective-permute-start | bytes 73736 | tf_op jit(solution)/shard_map/ppermute | solution.py:25
  39.3 21.4 %all-to-all-start.1 = ((bf16[8,80,384]{2,1,0:T(8,128)(2,1)}), bf16[8,80,384]{2,1,0:T(8,128)(2,1)}, u32[]{:S(2)}, u32[]{:S(2)}) async-start(bf16[8,80,384]{2,1,0:T(8,128)(2,1)} %broadcast_in_dim.87), calls=%async_computation.1 | async-start | bytes 983040 | tf_op jit(solution)/shard_map/all_to_all | solution.py:35
  43.5 15.3 %collective-permute-start = (bf16[8,80,384]{2,1,0:T(8,128)(2,1)}, bf16[8,80,384]{2,1,0:T(8,128)(2,1)}, u32[]{:S(2)}, u32[]{:S(2)}) collective-permute-start(bf16[8,80,384]{2,1,0:T(8,128)(2,1)} %all-to-all-done), channel_id=1, source_target_pairs={{0,16},{16,32},{32,48},{48,0},{64,80},{80,96},{96,112},{112,64},{1... | collective-permute-start | bytes 1474568 | tf_op jit(solution)/shard_map/ppermute | solution.py:25
  45.9 28.2 %collective-permute-start.1 = (bf16[8,80,384]{2,1,0:T(8,128)(2,1)}, bf16[8,80,384]{2,1,0:T(8,128)(2,1)}, u32[]{:S(2)}, u32[]{:S(2)}) collective-permute-start(bf16[8,80,384]{2,1,0:T(8,128)(2,1)} %all-to-all-done), channel_id=1, source_target_pairs={{0,48},{16,0},{32,16},{48,32},{64,112},{80,64},{96,80},{112,96},{1... | collective-permute-start | bytes 1474568 | tf_op jit(solution)/shard_map/ppermute | solution.py:25
  60.7 29.8 %collective-permute-start.3 = (bf16[8,80,384]{2,1,0:T(8,128)(2,1)}, bf16[8,80,384]{2,1,0:T(8,128)(2,1)}, u32[]{:S(2)}, u32[]{:S(2)}) collective-permute-start(bf16[8,80,384]{2,1,0:T(8,128)(2,1)} %all-to-all-done.1), channel_id=1, source_target_pairs={{0,16},{16,32},{32,48},{48,0},{64,80},{80,96},{96,112},{112,64},{1... | collective-permute-start | bytes 1474568 | tf_op jit(solution)/shard_map/ppermute | solution.py:25
  63.1 16.3 %collective-permute-start.4 = (bf16[8,80,384]{2,1,0:T(8,128)(2,1)}, bf16[8,80,384]{2,1,0:T(8,128)(2,1)}, u32[]{:S(2)}, u32[]{:S(2)}) collective-permute-start(bf16[8,80,384]{2,1,0:T(8,128)(2,1)} %all-to-all-done.1), channel_id=1, source_target_pairs={{0,48},{16,0},{32,16},{48,32},{64,112},{80,64},{96,80},{112,96},{1... | collective-permute-start | bytes 1474568 | tf_op jit(solution)/shard_map/ppermute | solution.py:25
  66.5 20.8 %collective-permute-start.2 = (bf16[8,80,384]{2,1,0:T(8,128)(2,1)}, bf16[8,80,384]{2,1,0:T(8,128)(2,1)}, u32[]{:S(2)}, u32[]{:S(2)}) collective-permute-start(bf16[8,80,384]{2,1,0:T(8,128)(2,1)} %collective-permute-done), channel_id=1, source_target_pairs={{0,16},{16,32},{32,48},{48,0},{64,80},{80,96},{96,112},{112,64},{1... | collective-permute-start | bytes 1474568 | tf_op jit(solution)/shard_map/ppermute | solution.py:25
  79.3 16.4 %collective-permute-start.8 = (bf16[8,80,384]{2,1,0:T(8,128)(2,1)}, bf16[8,80,384]{2,1,0:T(8,128)(2,1)}, u32[]{:S(2)}, u32[]{:S(2)}) collective-permute-start(bf16[8,80,384]{2,1,0:T(8,128)(2,1)} %collective-permute-done.4), channel_id=1, source_target_pairs={{0,48},{16,0},{32,16},{48,32},{64,112},{80,64},{96,80},{112,96},{1... | collective-permute-start | bytes 1474568 | tf_op jit(solution)/shard_map/ppermute | solution.py:25
  82.6 26.4 %all-to-all-start.2 = ((bf16[8,4,32,384]{3,2,1,0:T(8,128)(2,1)}), bf16[8,4,32,384]{3,2,1,0:T(8,128)(2,1)}, u32[]{:S(2)}, u32[]{:S(2)}) async-start(bf16[8,4,32,384]{3,2,1,0:T(8,128)(2,1)} %broadcast_in_dim.108), calls=%async_computation.2 | async-start | bytes 1572864 | tf_op jit(solution)/shard_map/all_to_all | solution.py:35
  87.2 71.1 %reduce-scatter.2.cloned.1.call-start = ((), (), s32[]{:S(2)}) async-start(), calls=%async_computation.7 | async-start | bytes 1769472 | tf_op jit(solution)/shard_map/reduce_scatter | solution.py:114
  111.2 1.9 %copy-start.4 = (bf16[768,2048]{1,0:T(8,128)(2,1)S(1)}, bf16[768,2048]{1,0:T(8,128)(2,1)}, u32[]{:S(2)}) copy-start(bf16[768,2048]{1,0:T(8,128)(2,1)} %all-gather.2.cloned.1.call-done) | copy-start | bytes 9437188
  117.5 1.4 slice-start
  118.9 2.7 %copy-start.3 = (bf16[8,1,128,384]{3,2,1,0:T(8,128)(2,1)S(1)}, bf16[8,1,128,384]{3,2,1,0:T(8,128)(2,1)}, u32[]{:S(2)}) copy-start(bf16[8,1,128,384]{3,2,1,0:T(8,128)(2,1)} %get-tuple-element.24) | copy-start | bytes 2359300
  121.6 1.1 copy-start.1
  123.4 2.2 %copy-start.2 = (bf16[8,1,128,384]{3,2,1,0:T(8,128)(2,1)S(1)}, bf16[8,1,128,384]{3,2,1,0:T(8,128)(2,1)}, u32[]{:S(2)}) copy-start(bf16[8,1,128,384]{3,2,1,0:T(8,128)(2,1)} %get-tuple-element.25) | copy-start | bytes 2359300
  123.5 2.7 %copy-start = (bf16[8,1,128,384]{3,2,1,0:T(8,128)(2,1)S(1)}, bf16[8,1,128,384]{3,2,1,0:T(8,128)(2,1)}, u32[]{:S(2)}) copy-start(bf16[8,1,128,384]{3,2,1,0:T(8,128)(2,1)} %get-tuple-element.23) | copy-start | bytes 2359300
  123.5 4.3 %collective-permute-start.9 = (bf16[8,384,128]{2,1,0:T(8,128)(2,1)S(1)}, bf16[8,384,128]{2,1,0:T(8,128)(2,1)S(1)}, u32[]{:S(2)}, u32[]{:S(2)}) collective-permute-start(bf16[8,384,128]{2,1,0:T(8,128)(2,1)S(1)} %bitcast.136), channel_id=1, source_target_pairs={{0,1},{1,0},{2,3},{3,2},{4,5},{5,4},{6,7},{7,6},{8,9},{9,8},{10,11... | collective-permute-start | bytes 2359304 | tf_op jit(solution)/shard_map/ppermute | solution.py:30
  158.3 10.5 %all-to-all-start.4 = ((bf16[4,64,384]{2,1,0:T(8,128)(2,1)}), bf16[4,64,384]{2,1,0:T(8,128)(2,1)S(1)}, u32[]{:S(2)}, u32[]{:S(2)}) async-start(bf16[4,64,384]{2,1,0:T(8,128)(2,1)} %bitcast.137), calls=%async_computation.5 | async-start | bytes 393216 | tf_op jit(solution)/shard_map/all_to_all | solution.py:119
  (1 other events, 1.0 us)
Sparse Core Ops, SparseCore 0:
  10.1 51.9 all-gather.1
  117.6 39.9 reduce-scatter.1

commit v2 on v0

--- a/solution.py
+++ b/solution.py
@@ -30,8 +30,11 @@
     return lax.ppermute(value, "mp", pairs)
 
 
-def gather_z(block):
-    copies = jnp.broadcast_to(block[None], (N_Z,) + block.shape)
+def copies_of(block):
+    return jnp.broadcast_to(block[None], (N_Z,) + block.shape)
+
+
+def gather_z(copies):
     return lax.all_to_all(copies, "fsdp", 0, 0, axis_index_groups=Z_GROUPS)
 
 
@@ -55,6 +58,8 @@
     me_x = lax.axis_index("fsdp") % N_X
     core = lax.axis_index("mp") % N_CORE
 
+    gate_copies = copies_of(gate_weight)
+    gate_copies, tokens, cotangent = lax.optimization_barrier((gate_copies, tokens, cotangent))
     stacked = jnp.concatenate([tokens, cotangent])
     both = lax.all_gather(stacked, "mp", axis=1, tiled=True)
     token_rows, cotangent_rows = both[:rows], both[rows:]
@@ -65,13 +70,13 @@
         block = send_x(down_weight, step)
         down_x = lax.dynamic_update_slice(down_x, block[None], ((me_x - step) % N_X, 0, 0))
 
-    gate_z = gather_z(gate_weight)
-    gate_z, up_weight = lax.optimization_barrier((gate_z, up_weight))
-    up_z = gather_z(up_weight)
-    up_z, down_x = lax.optimization_barrier((up_z, down_x))
-    down_full = gather_z(down_x).reshape(-1, cols)
+    gate_z = gather_z(gate_copies)
+    gate_left, gate_right = send_x(gate_z, 1), send_x(gate_z, -1)
+    gate_z, up_copies = lax.optimization_barrier((gate_z, copies_of(up_weight)))
+    up_z = gather_z(up_copies)
+    up_z, down_copies, gate_left = lax.optimization_barrier((up_z, copies_of(down_x), gate_left))
+    down_full = gather_z(down_copies).reshape(-1, cols)
 
-    gate_left, gate_right = send_x(gate_z, 1), send_x(gate_z, -1)
     up_right, up_left = send_x(up_z, -1), send_x(up_z, 1)
     gate_far, up_far = send_x(gate_left, 1), send_x(up_right, -1)
     gate_full = put_x((gate_z, gate_left, gate_right, gate_far), me_x).reshape(-1, cols)
@@ -103,16 +108,14 @@
     summed = lax.all_to_all(pair_sum, "mp", 0, 0, axis_index_groups=Y_GROUPS)
 
     down_z = lax.psum_scatter(
-        down_partial.reshape(N_Z, N_X, depth, cols).transpose(1, 0, 2, 3).reshape(-1, cols),
-        "fsdp",
-        scatter_dimension=0,
-        axis_index_groups=X_GROUPS,
-        tiled=True,
-    ).reshape(N_Z, depth, cols)
-    summed, down_z = lax.optimization_barrier((summed, down_z))
+        down_partial, "fsdp", scatter_dimension=0, axis_index_groups=Z_GROUPS, tiled=True
+    ).reshape(N_X, depth, cols)
+    down_sum = lax.dynamic_index_in_dim(down_z, me_x, 0, False).astype(jnp.float32)
+    for step in (1, N_X - 1, 2):
+        block = lax.dynamic_index_in_dim(down_z, (me_x + step) % N_X, 0, False)
+        down_sum = down_sum + send_x(block, step).astype(jnp.float32)
+    grad_down = (down_sum * factor).astype(jnp.bfloat16)
     input_grad = summed.astype(jnp.float32).sum(0).astype(jnp.bfloat16)
-    down_z = lax.all_to_all(down_z, "fsdp", 0, 0, axis_index_groups=Z_GROUPS)
-    grad_down = (down_z.astype(jnp.float32).sum(0) * factor).astype(jnp.bfloat16)
     return (input_grad, grad_down)
 
 

time: 169 us -> 167 us (0.988)
  blocking collectives: 30.3 us -> 0 us
  waiting for transfers between devices: 42.4 us -> 52.5 us
  starting transfers between devices: 55.8 us -> 65.1 us
  local copies, waits for them, and re-layouts: 13.6 us -> 17.9 us
    all_to_all x1 -> x0, blocking collectives: 30.3 us -> none  [on_device(): summed = lax.all_to_all(pair_sum, 'mp', 0, 0, axis_index_groups=Y_GROUPS)]
    reduce_scatter x1, waiting for transfers between devices: 0.01 us -> 16.3 us  [on_device(): lax.psum_scatter(down_partial, 'fsdp', scatter_dimension=0, axis_index_gr...]
    all_to_all x1, waiting for transfers between devices: 12.9 us -> 0.01 us  [on_device(): summed = lax.all_to_all(pair_sum, 'mp', 0, 0, axis_index_groups=Y_GROUPS)]
    all_to_all x3, waiting for transfers between devices: 7.09 us -> 18.9 us  [gather_z(): return lax.all_to_all(copies, 'fsdp', 0, 0, axis_index_groups=Z_GROUPS)]
    ppermute x9 -> x12, starting transfers between devices: 26.6 us -> 35.6 us  [send_x(): return lax.ppermute(value, 'fsdp', pairs)]
    ppermute x9 -> x12, waiting for transfers between devices: 21.5 us -> 16.3 us  [send_x(): return lax.ppermute(value, 'fsdp', pairs)]
    dynamic_update_slice x7, local copies, waits for them, and re-layouts: 2.56 us -> 6.54 us  [put_x(): lax.dynamic_update_slice(full, block[:, None], (0, (me + step) % N_X, 0, 0))]
  transfers between devices with their start and end apart: 16 -> 19, of which waited for: 7 -> 8; matrix products, arithmetic and copies ran while one was open for 12% -> 15% of each run, Pallas kernels for 0% -> 0%
where the time goes in v2:
time: 167 us; the launch traced here: 165 us
  starting transfers between devices  65.1 us (39%)
  waiting for transfers between devices  52.5 us (31%)
  local copies, waits for them, and re-layouts  17.9 us (11%)
  between operations  14.7 us (9%)
  matrix products  9.63 us (6%)
  other arithmetic  4.89 us (3%)
    ppermute x12, starting transfers between devices, send_x(): return lax.ppermute(value, 'fsdp', pairs)  35.6 us
    all_to_all x3, starting transfers between devices, gather_z(): return lax.all_to_all(copies, 'fsdp', 0, 0, axis_index_groups=Z_GROUPS)  20.4 us
    all_to_all x3, waiting for transfers between devices, gather_z(): return lax.all_to_all(copies, 'fsdp', 0, 0, axis_index_groups=Z_GROUPS)  18.9 us
    ppermute x12, waiting for transfers between devices, send_x(): return lax.ppermute(value, 'fsdp', pairs)  16.3 us
    reduce_scatter x1, waiting for transfers between devices, on_device(): lax.psum_scatter(down_partial, 'fsdp', scatter_dimension=0, axis_index_gr...  16.3 us
    dot_general x8, matrix products, dot(): lax.dot_general(left, right, (dims, ((), ())), preferred_element_type=jnp...  9.63 us
    all_to_all x1, starting transfers between devices, on_device(): summed = lax.all_to_all(pair_sum, 'mp', 0, 0, axis_index_groups=Y_GROUPS)  7.01 us
    dynamic_update_slice x7, local copies, waits for them, and re-layouts, put_x(): lax.dynamic_update_slice(full, block[:, None], (0, (me + step) % N_X, 0, 0))  6.54 us
  transfers between devices with their start and end apart: 19, of which 8 were waited for; matrix products, arithmetic and copies ran while one was open for 15% of the time, Pallas kernels for 0%

profile of v2, /device:TPU:6, one launch (start us, length us, event | category | flops | bytes accessed | tf_op | source)
XLA Modules:
  0.0 164.7 jit_solution(8470638114198884967)
XLA Ops:
  10.5 10.3 %all-to-all-start = ((bf16[8,64,384]{2,1,0:T(8,128)(2,1)}), bf16[8,64,384]{2,1,0:T(8,128)(2,1)S(1)}, u32[]{:S(2)}, u32[]{:S(2)}) async-start(bf16[8,64,384]{2,1,0:T(8,128)(2,1)} %broadcast_in_dim.57), calls=%async_computation | async-start | bytes 786432 | tf_op jit(solution)/shard_map/all_to_all | solution.py:38
  20.8 2.4 %collective-permute-start = (bf16[64,384]{1,0:T(8,128)(2,1)S(1)}, bf16[64,384]{1,0:T(8,128)(2,1)S(1)}, u32[]{:S(2)}, u32[]{:S(2)}) collective-permute-start(bf16[64,384]{1,0:T(8,128)(2,1)S(1)} %copy-done.6), channel_id=1, source_target_pairs={{0,16},{16,32},{32,48},{48,0},{64,80},{80,96},{96,112},{112,64},{1... | collective-permute-start | bytes 147464 | tf_op jit(solution)/shard_map/ppermute | solution.py:25
  23.2 3.5 %collective-permute-start.1 = (bf16[64,384]{1,0:T(8,128)(2,1)S(1)}, bf16[64,384]{1,0:T(8,128)(2,1)S(1)}, u32[]{:S(2)}, u32[]{:S(2)}) collective-permute-start(bf16[64,384]{1,0:T(8,128)(2,1)S(1)} %copy-done.6), channel_id=1, source_target_pairs={{0,48},{16,0},{32,16},{48,32},{64,112},{80,64},{96,80},{112,96},{1... | collective-permute-start | bytes 147464 | tf_op jit(solution)/shard_map/ppermute | solution.py:25
  26.7 3.3 %collective-permute-start.2 = (bf16[64,384]{1,0:T(8,128)(2,1)S(1)}, bf16[64,384]{1,0:T(8,128)(2,1)S(1)}, u32[]{:S(2)}, u32[]{:S(2)}) collective-permute-start(bf16[64,384]{1,0:T(8,128)(2,1)S(1)} %copy-done.6), channel_id=1, source_target_pairs={{0,32},{16,48},{32,0},{48,16},{64,96},{80,112},{96,64},{112,80},{1... | collective-permute-start | bytes 147464 | tf_op jit(solution)/shard_map/ppermute | solution.py:25
  30.2 5.2 %all-to-all-done = bf16[8,64,384]{2,1,0:T(8,128)(2,1)S(1)} async-done(((bf16[8,64,384]{2,1,0:T(8,128)(2,1)}), bf16[8,64,384]{2,1,0:T(8,128)(2,1)S(1)}, u32[]{:S(2)}, u32[]{:S(2)}) %all-to-all-start) | async-done | bytes 393248 | tf_op jit(solution)/shard_map/all_to_all | solution.py:38
  36.3 4.1 %all-to-all-start.1 = ((bf16[8,64,384]{2,1,0:T(8,128)(2,1)}), bf16[8,64,384]{2,1,0:T(8,128)(2,1)}, u32[]{:S(2)}, u32[]{:S(2)}) async-start(bf16[8,64,384]{2,1,0:T(8,128)(2,1)} %broadcast_in_dim.58), calls=%async_computation.1 | async-start | bytes 786432 | tf_op jit(solution)/shard_map/all_to_all | solution.py:38
  40.4 2.4 %collective-permute-start.3 = (bf16[8,64,384]{2,1,0:T(8,128)(2,1)S(1)}, bf16[8,64,384]{2,1,0:T(8,128)(2,1)}, u32[]{:S(2)}, u32[]{:S(2)}) collective-permute-start(bf16[8,64,384]{2,1,0:T(8,128)(2,1)S(1)} %all-to-all-done), channel_id=1, source_target_pairs={{0,16},{16,32},{32,48},{48,0},{64,80},{80,96},{96,112},{112,64},{1... | collective-permute-start | bytes 1179656 | tf_op jit(solution)/shard_map/ppermute | solution.py:25
  42.9 3.4 %collective-permute-start.4 = (bf16[8,64,384]{2,1,0:T(8,128)(2,1)S(1)}, bf16[8,64,384]{2,1,0:T(8,128)(2,1)}, u32[]{:S(2)}, u32[]{:S(2)}) collective-permute-start(bf16[8,64,384]{2,1,0:T(8,128)(2,1)S(1)} %all-to-all-done), channel_id=1, source_target_pairs={{0,48},{16,0},{32,16},{48,32},{64,112},{80,64},{96,80},{112,96},{1... | collective-permute-start | bytes 1179656 | tf_op jit(solution)/shard_map/ppermute | solution.py:25
  46.6 5.9 %collective-permute-done.3 = bf16[8,64,384]{2,1,0:T(8,128)(2,1)} collective-permute-done((bf16[8,64,384]{2,1,0:T(8,128)(2,1)S(1)}, bf16[8,64,384]{2,1,0:T(8,128)(2,1)}, u32[]{:S(2)}, u32[]{:S(2)}) %collective-permute-start.3) | collective-permute-done | bytes 393248 | tf_op jit(solution)/shard_map/ppermute | solution.py:25
  52.5 2.1 %all-to-all-done.1 = bf16[8,64,384]{2,1,0:T(8,128)(2,1)} async-done(((bf16[8,64,384]{2,1,0:T(8,128)(2,1)}), bf16[8,64,384]{2,1,0:T(8,128)(2,1)}, u32[]{:S(2)}, u32[]{:S(2)}) %all-to-all-start.1) | async-done | bytes 393248 | tf_op jit(solution)/shard_map/all_to_all | solution.py:38
  56.0 2.4 %collective-permute-start.6 = (bf16[8,64,384]{2,1,0:T(8,128)(2,1)}, bf16[8,64,384]{2,1,0:T(8,128)(2,1)}, u32[]{:S(2)}, u32[]{:S(2)}) collective-permute-start(bf16[8,64,384]{2,1,0:T(8,128)(2,1)} %all-to-all-done.1), channel_id=1, source_target_pairs={{0,16},{16,32},{32,48},{48,0},{64,80},{80,96},{96,112},{112,64},{1... | collective-permute-start | bytes 1179656 | tf_op jit(solution)/shard_map/ppermute | solution.py:25
  58.4 3.4 %collective-permute-start.7 = (bf16[8,64,384]{2,1,0:T(8,128)(2,1)}, bf16[8,64,384]{2,1,0:T(8,128)(2,1)}, u32[]{:S(2)}, u32[]{:S(2)}) collective-permute-start(bf16[8,64,384]{2,1,0:T(8,128)(2,1)} %all-to-all-done.1), channel_id=1, source_target_pairs={{0,48},{16,0},{32,16},{48,32},{64,112},{80,64},{96,80},{112,96},{1... | collective-permute-start | bytes 1179656 | tf_op jit(solution)/shard_map/ppermute | solution.py:25
  61.8 3.6 %collective-permute-start.5 = (bf16[8,64,384]{2,1,0:T(8,128)(2,1)}, bf16[8,64,384]{2,1,0:T(8,128)(2,1)}, u32[]{:S(2)}, u32[]{:S(2)}) collective-permute-start(bf16[8,64,384]{2,1,0:T(8,128)(2,1)} %collective-permute-done.3), channel_id=1, source_target_pairs={{0,16},{16,32},{32,48},{48,0},{64,80},{80,96},{96,112},{112,64},{1... | collective-permute-start | bytes 1179656 | tf_op jit(solution)/shard_map/ppermute | solution.py:25
  65.5 6.0 %all-to-all-start.2 = ((bf16[8,4,64,384]{3,2,1,0:T(8,128)(2,1)}), bf16[8,4,64,384]{3,2,1,0:T(8,128)(2,1)}, u32[]{:S(2)}, u32[]{:S(2)}) async-start(bf16[8,4,64,384]{3,2,1,0:T(8,128)(2,1)} %broadcast_in_dim.65), calls=%async_computation.2 | async-start | bytes 3145728 | tf_op jit(solution)/shard_map/all_to_all | solution.py:38
  79.0 7.0 %collective-permute-done.8 = bf16[8,64,384]{2,1,0:T(8,128)(2,1)S(1)} collective-permute-done((bf16[8,64,384]{2,1,0:T(8,128)(2,1)}, bf16[8,64,384]{2,1,0:T(8,128)(2,1)S(1)}, u32[]{:S(2)}, u32[]{:S(2)}) %collective-permute-start.8) | collective-permute-done | bytes 393248 | tf_op jit(solution)/shard_map/ppermute | solution.py:25
  94.7 2.4 %convolution_convert_fusion = bf16[2048,384]{1,0:T(8,128)(2,1)} fusion(f32[384,384]{1,0:T(8,128)S(1)} %fusion.2, f32[384,384]{1,0:T(8,128)S(1)} %fusion.4, bf16[768,2048]{1,0:T(8,128)(2,1)S(1)} %copy-done.4), kind=kOutput, calls=%fused_computation | convolution fusion | flops 605650944 | bytes 4325376 | tf_op jit(solution)/shard_map/dot_general | solution.py:18
  97.1 11.6 %all-to-all-done.2 = bf16[8,4,64,384]{3,2,1,0:T(8,128)(2,1)} async-done(((bf16[8,4,64,384]{3,2,1,0:T(8,128)(2,1)}), bf16[8,4,64,384]{3,2,1,0:T(8,128)(2,1)}, u32[]{:S(2)}, u32[]{:S(2)}) %all-to-all-start.2) | async-done | bytes 1572896 | tf_op jit(solution)/shard_map/all_to_all | solution.py:38
  108.7 2.9 %multiply_convert_fusion = (bf16[384,384]{1,0:T(8,128)(2,1)S(1)}, bf16[384,384]{1,0:T(8,128)(2,1)S(1)}) fusion(f32[384,384]{1,0:T(8,128)} %copy-done.8, f32[384,384]{1,0:T(8,128)} %copy-done.7, bf16[384,2048]{1,0:T(8,128)(2,1)S(1)} %slice-done, bf16[2048,384]{1,0:T(8,128)(2,1)} %bitcast.20), kind=kOutput, calls=%fused_computation.13 | convolution fusion | flops 605896704 | bytes 4915200 | tf_op jit(solution)/shard_map/dot_general | solution.py:18
  118.9 7.0 %all-to-all-start.3 = ((bf16[8,384,128]{2,1,0:T(8,128)(2,1)}), bf16[8,384,128]{2,1,0:T(8,128)(2,1)S(1)}, u32[]{:S(2)}, u32[]{:S(2)}) async-start(bf16[8,384,128]{2,1,0:T(8,128)(2,1)} %fusion.1), calls=%async_computation.3 | async-start | bytes 1572864 | tf_op jit(solution)/shard_map/all_to_all | solution.py:108
  126.0 16.3 %reduce-scatter.2.cloned.1.call-done = bf16[256,384]{1,0:T(8,128)(2,1)} async-done(((bf16[2048,384]{1,0:T(8,128)(2,1)}), bf16[256,384]{1,0:T(8,128)(2,1)}) %reduce-scatter.2.cloned.1.call-update) | async-done | bytes 196624 | tf_op jit(solution)/shard_map/reduce_scatter | solution.py:110
  143.1 2.5 %collective-permute-start.10 = (bf16[64,384]{1,0:T(8,128)(2,1)S(1)}, bf16[64,384]{1,0:T(8,128)(2,1)S(1)}, u32[]{:S(2)}, u32[]{:S(2)}) collective-permute-start(bf16[64,384]{1,0:T(8,128)(2,1)S(1)} %get-tuple-element.28), channel_id=1, source_target_pairs={{0,16},{16,32},{32,48},{48,0},{64,80},{80,96},{96,112},{112,64},{1... | collective-permute-start | bytes 147464 | tf_op jit(solution)/shard_map/ppermute | solution.py:25
  145.5 3.4 %collective-permute-start.11 = (bf16[64,384]{1,0:T(8,128)(2,1)S(1)}, bf16[64,384]{1,0:T(8,128)(2,1)S(1)}, u32[]{:S(2)}, u32[]{:S(2)}) collective-permute-start(bf16[64,384]{1,0:T(8,128)(2,1)S(1)} %get-tuple-element.30), channel_id=1, source_target_pairs={{0,48},{16,0},{32,16},{48,32},{64,112},{80,64},{96,80},{112,96},{1... | collective-permute-start | bytes 147464 | tf_op jit(solution)/shard_map/ppermute | solution.py:25
  148.9 3.3 %collective-permute-start.12 = (bf16[64,384]{1,0:T(8,128)(2,1)S(1)}, bf16[64,384]{1,0:T(8,128)(2,1)S(1)}, u32[]{:S(2)}, u32[]{:S(2)}) collective-permute-start(bf16[64,384]{1,0:T(8,128)(2,1)S(1)} %get-tuple-element.29), channel_id=1, source_target_pairs={{0,32},{16,48},{32,0},{48,16},{64,96},{80,112},{96,64},{112,80},{1... | collective-permute-start | bytes 147464 | tf_op jit(solution)/shard_map/ppermute | solution.py:25
  153.0 3.4 %collective-permute-done.12 = bf16[64,384]{1,0:T(8,128)(2,1)S(1)} collective-permute-done((bf16[64,384]{1,0:T(8,128)(2,1)S(1)}, bf16[64,384]{1,0:T(8,128)(2,1)S(1)}, u32[]{:S(2)}, u32[]{:S(2)}) %collective-permute-start.12) | collective-permute-done | bytes 49184 | tf_op jit(solution)/shard_map/ppermute | solution.py:25
  (69 shorter events, 32.3 us)
Async XLA Ops:
  7.2 13.6 %copy-start.6 = (bf16[64,384]{1,0:T(8,128)(2,1)S(1)}, bf16[64,384]{1,0:T(8,128)(2,1)}, u32[]{:S(2)}) copy-start(bf16[64,384]{1,0:T(8,128)(2,1)} %param.9) | copy-start | bytes 147460
  7.2 28.3 %copy-start.5 = (bf16[64,384]{1,0:T(8,128)(2,1)S(1)}, bf16[64,384]{1,0:T(8,128)(2,1)}, u32[]{:S(2)}) copy-start(bf16[64,384]{1,0:T(8,128)(2,1)} %param.8) | copy-start | bytes 147460
  7.2 82.8 %all-gather.2.cloned.1.call-start = ((), (), s32[]{:S(2)}) async-start(), calls=%async_computation.5 | async-start | bytes 3342336 | tf_op jit(solution)/shard_map/all_gather | solution.py:64
  10.5 25.0 %all-to-all-start = ((bf16[8,64,384]{2,1,0:T(8,128)(2,1)}), bf16[8,64,384]{2,1,0:T(8,128)(2,1)S(1)}, u32[]{:S(2)}, u32[]{:S(2)}) async-start(bf16[8,64,384]{2,1,0:T(8,128)(2,1)} %broadcast_in_dim.57), calls=%async_computation | async-start | bytes 786432 | tf_op jit(solution)/shard_map/all_to_all | solution.py:38
  20.8 9.4 %collective-permute-start = (bf16[64,384]{1,0:T(8,128)(2,1)S(1)}, bf16[64,384]{1,0:T(8,128)(2,1)S(1)}, u32[]{:S(2)}, u32[]{:S(2)}) collective-permute-start(bf16[64,384]{1,0:T(8,128)(2,1)S(1)} %copy-done.6), channel_id=1, source_target_pairs={{0,16},{16,32},{32,48},{48,0},{64,80},{80,96},{96,112},{112,64},{1... | collective-permute-start | bytes 147464 | tf_op jit(solution)/shard_map/ppermute | solution.py:25
  23.2 17.2 %collective-permute-start.1 = (bf16[64,384]{1,0:T(8,128)(2,1)S(1)}, bf16[64,384]{1,0:T(8,128)(2,1)S(1)}, u32[]{:S(2)}, u32[]{:S(2)}) collective-permute-start(bf16[64,384]{1,0:T(8,128)(2,1)S(1)} %copy-done.6), channel_id=1, source_target_pairs={{0,48},{16,0},{32,16},{48,32},{64,112},{80,64},{96,80},{112,96},{1... | collective-permute-start | bytes 147464 | tf_op jit(solution)/shard_map/ppermute | solution.py:25
  26.7 16.2 %collective-permute-start.2 = (bf16[64,384]{1,0:T(8,128)(2,1)S(1)}, bf16[64,384]{1,0:T(8,128)(2,1)S(1)}, u32[]{:S(2)}, u32[]{:S(2)}) collective-permute-start(bf16[64,384]{1,0:T(8,128)(2,1)S(1)} %copy-done.6), channel_id=1, source_target_pairs={{0,32},{16,48},{32,0},{48,16},{64,96},{80,112},{96,64},{112,80},{1... | collective-permute-start | bytes 147464 | tf_op jit(solution)/shard_map/ppermute | solution.py:25
  36.3 18.3 %all-to-all-start.1 = ((bf16[8,64,384]{2,1,0:T(8,128)(2,1)}), bf16[8,64,384]{2,1,0:T(8,128)(2,1)}, u32[]{:S(2)}, u32[]{:S(2)}) async-start(bf16[8,64,384]{2,1,0:T(8,128)(2,1)} %broadcast_in_dim.58), calls=%async_computation.1 | async-start | bytes 786432 | tf_op jit(solution)/shard_map/all_to_all | solution.py:38
  40.4 12.1 %collective-permute-start.3 = (bf16[8,64,384]{2,1,0:T(8,128)(2,1)S(1)}, bf16[8,64,384]{2,1,0:T(8,128)(2,1)}, u32[]{:S(2)}, u32[]{:S(2)}) collective-permute-start(bf16[8,64,384]{2,1,0:T(8,128)(2,1)S(1)} %all-to-all-done), channel_id=1, source_target_pairs={{0,16},{16,32},{32,48},{48,0},{64,80},{80,96},{96,112},{112,64},{1... | collective-permute-start | bytes 1179656 | tf_op jit(solution)/shard_map/ppermute | solution.py:25
  42.9 31.0 %collective-permute-start.4 = (bf16[8,64,384]{2,1,0:T(8,128)(2,1)S(1)}, bf16[8,64,384]{2,1,0:T(8,128)(2,1)}, u32[]{:S(2)}, u32[]{:S(2)}) collective-permute-start(bf16[8,64,384]{2,1,0:T(8,128)(2,1)S(1)} %all-to-all-done), channel_id=1, source_target_pairs={{0,48},{16,0},{32,16},{48,32},{64,112},{80,64},{96,80},{112,96},{1... | collective-permute-start | bytes 1179656 | tf_op jit(solution)/shard_map/ppermute | solution.py:25
  56.0 20.9 %collective-permute-start.6 = (bf16[8,64,384]{2,1,0:T(8,128)(2,1)}, bf16[8,64,384]{2,1,0:T(8,128)(2,1)}, u32[]{:S(2)}, u32[]{:S(2)}) collective-permute-start(bf16[8,64,384]{2,1,0:T(8,128)(2,1)} %all-to-all-done.1), channel_id=1, source_target_pairs={{0,16},{16,32},{32,48},{48,0},{64,80},{80,96},{96,112},{112,64},{1... | collective-permute-start | bytes 1179656 | tf_op jit(solution)/shard_map/ppermute | solution.py:25
  58.4 16.5 %collective-permute-start.7 = (bf16[8,64,384]{2,1,0:T(8,128)(2,1)}, bf16[8,64,384]{2,1,0:T(8,128)(2,1)}, u32[]{:S(2)}, u32[]{:S(2)}) collective-permute-start(bf16[8,64,384]{2,1,0:T(8,128)(2,1)} %all-to-all-done.1), channel_id=1, source_target_pairs={{0,48},{16,0},{32,16},{48,32},{64,112},{80,64},{96,80},{112,96},{1... | collective-permute-start | bytes 1179656 | tf_op jit(solution)/shard_map/ppermute | solution.py:25
  61.8 17.2 %collective-permute-start.5 = (bf16[8,64,384]{2,1,0:T(8,128)(2,1)}, bf16[8,64,384]{2,1,0:T(8,128)(2,1)}, u32[]{:S(2)}, u32[]{:S(2)}) collective-permute-start(bf16[8,64,384]{2,1,0:T(8,128)(2,1)} %collective-permute-done.3), channel_id=1, source_target_pairs={{0,16},{16,32},{32,48},{48,0},{64,80},{80,96},{96,112},{112,64},{1... | collective-permute-start | bytes 1179656 | tf_op jit(solution)/shard_map/ppermute | solution.py:25
  65.5 43.2 %all-to-all-start.2 = ((bf16[8,4,64,384]{3,2,1,0:T(8,128)(2,1)}), bf16[8,4,64,384]{3,2,1,0:T(8,128)(2,1)}, u32[]{:S(2)}, u32[]{:S(2)}) async-start(bf16[8,4,64,384]{3,2,1,0:T(8,128)(2,1)} %broadcast_in_dim.65), calls=%async_computation.2 | async-start | bytes 3145728 | tf_op jit(solution)/shard_map/all_to_all | solution.py:38
  71.4 70.8 %reduce-scatter.2.cloned.1.call-start = ((), (), s32[]{:S(2)}) async-start(), calls=%async_computation.6 | async-start | bytes 1769472 | tf_op jit(solution)/shard_map/reduce_scatter | solution.py:110
  74.9 11.1 %collective-permute-start.8 = (bf16[8,64,384]{2,1,0:T(8,128)(2,1)}, bf16[8,64,384]{2,1,0:T(8,128)(2,1)S(1)}, u32[]{:S(2)}, u32[]{:S(2)}) collective-permute-start(bf16[8,64,384]{2,1,0:T(8,128)(2,1)} %collective-permute-done.7), channel_id=1, source_target_pairs={{0,48},{16,0},{32,16},{48,32},{64,112},{80,64},{96,80},{112,96},{1... | collective-permute-start | bytes 1179656 | tf_op jit(solution)/shard_map/ppermute | solution.py:25
  97.0 11.7 %slice-start = ((bf16[768,2048]{1,0:T(8,128)(2,1)}), bf16[384,2048]{1,0:T(8,128)(2,1)S(1)}, s32[]{:S(2)}) async-start(bf16[768,2048]{1,0:T(8,128)(2,1)} %all-gather.2.cloned.1.call-done), calls=%async_computation.7 | async-start | bytes 3145728 | tf_op jit(solution)/shard_map/slice | solution.py:65
  108.7 2.9 %copy-start.3 = (bf16[8,1,128,384]{3,2,1,0:T(8,128)(2,1)S(1)}, bf16[8,1,128,384]{3,2,1,0:T(8,128)(2,1)}, u32[]{:S(2)}) copy-start(bf16[8,1,128,384]{3,2,1,0:T(8,128)(2,1)} %get-tuple-element.24) | copy-start | bytes 2359300
  113.6 2.7 %copy-start = (bf16[8,1,128,384]{3,2,1,0:T(8,128)(2,1)S(1)}, bf16[8,1,128,384]{3,2,1,0:T(8,128)(2,1)}, u32[]{:S(2)}) copy-start(bf16[8,1,128,384]{3,2,1,0:T(8,128)(2,1)} %get-tuple-element.23) | copy-start | bytes 2359300
  113.6 4.3 %collective-permute-start.9 = (bf16[8,384,128]{2,1,0:T(8,128)(2,1)S(1)}, bf16[8,384,128]{2,1,0:T(8,128)(2,1)S(1)}, u32[]{:S(2)}, u32[]{:S(2)}) collective-permute-start(bf16[8,384,128]{2,1,0:T(8,128)(2,1)S(1)} %bitcast.97), channel_id=1, source_target_pairs={{0,1},{1,0},{2,3},{3,2},{4,5},{5,4},{6,7},{7,6},{8,9},{9,8},{10,11... | collective-permute-start | bytes 2359304 | tf_op jit(solution)/shard_map/ppermute | solution.py:30
  118.9 33.3 %all-to-all-start.3 = ((bf16[8,384,128]{2,1,0:T(8,128)(2,1)}), bf16[8,384,128]{2,1,0:T(8,128)(2,1)S(1)}, u32[]{:S(2)}, u32[]{:S(2)}) async-start(bf16[8,384,128]{2,1,0:T(8,128)(2,1)} %fusion.1), calls=%async_computation.3 | async-start | bytes 1572864 | tf_op jit(solution)/shard_map/all_to_all | solution.py:108
  143.1 10.0 %collective-permute-start.10 = (bf16[64,384]{1,0:T(8,128)(2,1)S(1)}, bf16[64,384]{1,0:T(8,128)(2,1)S(1)}, u32[]{:S(2)}, u32[]{:S(2)}) collective-permute-start(bf16[64,384]{1,0:T(8,128)(2,1)S(1)} %get-tuple-element.28), channel_id=1, source_target_pairs={{0,16},{16,32},{32,48},{48,0},{64,80},{80,96},{96,112},{112,64},{1... | collective-permute-start | bytes 147464 | tf_op jit(solution)/shard_map/ppermute | solution.py:25
  145.5 7.5 %collective-permute-start.11 = (bf16[64,384]{1,0:T(8,128)(2,1)S(1)}, bf16[64,384]{1,0:T(8,128)(2,1)S(1)}, u32[]{:S(2)}, u32[]{:S(2)}) collective-permute-start(bf16[64,384]{1,0:T(8,128)(2,1)S(1)} %get-tuple-element.30), channel_id=1, source_target_pairs={{0,48},{16,0},{32,16},{48,32},{64,112},{80,64},{96,80},{112,96},{1... | collective-permute-start | bytes 147464 | tf_op jit(solution)/shard_map/ppermute | solution.py:25
  148.9 7.5 %collective-permute-start.12 = (bf16[64,384]{1,0:T(8,128)(2,1)S(1)}, bf16[64,384]{1,0:T(8,128)(2,1)S(1)}, u32[]{:S(2)}, u32[]{:S(2)}) collective-permute-start(bf16[64,384]{1,0:T(8,128)(2,1)S(1)} %get-tuple-element.29), channel_id=1, source_target_pairs={{0,32},{16,48},{32,0},{48,16},{64,96},{80,112},{96,64},{112,80},{1... | collective-permute-start | bytes 147464 | tf_op jit(solution)/shard_map/ppermute | solution.py:25
  (5 other events, 7.1 us)
Sparse Core Ops, SparseCore 0:
  10.6 52.2 all-gather.1
  97.2 44.9 reduce-scatter.1

commit v3 on v2

v3 whole, which is shorter than its diff:
```python
import math

import jax
import jax.numpy as jnp
from jax import lax
from jax.experimental import pallas as pl
from jax.experimental.pallas import tpu as pltpu
from jax.sharding import PartitionSpec as P

N_Z = 8
N_X = 4
N_Y = 8
N_CORE = 2
Z_GROUPS = [[z * N_X + x for z in range(N_Z)] for x in range(N_X)]
X_GROUPS = [[z * N_X + x for x in range(N_X)] for z in range(N_Z)]
Y_GROUPS = [[y * N_CORE + c for y in range(N_Y)] for c in range(N_CORE)]


def dot(left, right, dims):
    return lax.dot_general(left, right, (dims, ((), ())), preferred_element_type=jnp.float32)


def copy_blocks(blocks, full, sems, me_x):
    depth = blocks[0].shape[1]
    copies = []
    for i, step in enumerate((0, N_X - 1, 1, 2)):
        x = lax.rem(me_x + step, N_X)
        row = pl.multiple_of(lax.rem(x, 2) * depth, depth)
        target = full.at[:, lax.div(x, 2), pl.ds(row, depth), :]
        copies.append(pltpu.make_async_copy(blocks[i], target, sems.at[i]))
    for copy in copies:
        copy.start()
    return copies


def forward_kernel(
    place, rows_ref, g0, g1, g2, g3, u0, u1, u2, u3, gate_out, up_out, partial_out,
    tok, cot, gate_full, up_full, row_sems, gate_sems, up_sems,
):
    me_x = place[0]
    count = tok.shape[0]
    tok_copy = pltpu.make_async_copy(rows_ref.at[pl.ds(0, count)], tok, row_sems.at[0])
    cot_copy = pltpu.make_async_copy(rows_ref.at[pl.ds(count, count)], cot, row_sems.at[1])
    tok_copy.start()
    gate_copies = copy_blocks((g0, g1, g2, g3), gate_full, gate_sems, me_x)
    up_copies = copy_blocks((u0, u1, u2, u3), up_full, up_sems, me_x)
    cot_copy.start()
    n_feat, cols = partial_out.shape
    tok_copy.wait()
    for copy in gate_copies:
        copy.wait()
    gate_value = jnp.dot(
        tok[...], gate_full[...].reshape(n_feat, cols), preferred_element_type=jnp.float32
    )
    gate_out[...] = gate_value
    for copy in up_copies:
        copy.wait()
    up_value = jnp.dot(
        tok[...], up_full[...].reshape(n_feat, cols), preferred_element_type=jnp.float32
    )
    up_out[...] = up_value
    hidden = (gate_value * jax.nn.sigmoid(gate_value) * up_value).astype(jnp.bfloat16)
    cot_copy.wait()
    partial_out[...] = dot(cot[...], hidden, ((0,), (0,))).astype(jnp.bfloat16)


def backward_kernel(
    place, rows_ref, down_ref, g0, g1, g2, g3, u0, u1, u2, u3, gate_in, up_in, other_out, mine_out,
    cot, down_full, gate_full, up_full, row_sem, down_sem, gate_sems, up_sems,
):
    me_x, core = place[0], place[1]
    count = cot.shape[0]
    n_z, _, wide, cols = gate_full.shape
    cot_copy = pltpu.make_async_copy(rows_ref.at[pl.ds(count, count)], cot, row_sem.at[0])
    down_copy = pltpu.make_async_copy(down_ref, down_full, down_sem.at[0])
    cot_copy.start()
    down_copy.start()
    gate_copies = copy_blocks((g0, g1, g2, g3), gate_full, gate_sems, me_x)
    up_copies = copy_blocks((u0, u1, u2, u3), up_full, up_sems, me_x)
    gate_value, up_value = gate_in[...], up_in[...]
    sigmoid_gate = jax.nn.sigmoid(gate_value)
    cot_copy.wait()
    down_copy.wait()
    hidden_grad = jnp.dot(
        cot[...], down_full[...].reshape(-1, cols), preferred_element_type=jnp.float32
    )
    gate_grad = (
        hidden_grad * up_value * sigmoid_gate * (1.0 + gate_value * (1.0 - sigmoid_gate))
    ).astype(jnp.bfloat16)
    up_grad = (hidden_grad * gate_value * sigmoid_gate).astype(jnp.bfloat16)
    grads = jnp.concatenate([gate_grad, up_grad], axis=1)
    for copy in gate_copies + up_copies:
        copy.wait()
    for out, which in ((other_out, 1 - core), (mine_out, core)):
        for y in range(0, n_z, 2):
            pair = [
                jnp.concatenate([gate_full[y + i, which], up_full[y + i, which]], axis=1)
                for i in range(2)
            ]
            value = dot(grads, jnp.concatenate(pair), ((1,), (1,))).astype(jnp.bfloat16)
            out[y] = value[:, :wide]
            out[y + 1] = value[:, wide:]


def call_kernel(kernel, n_smem_any, operands, out_shapes, scratch, flops):
    in_specs = [pl.BlockSpec(memory_space=pltpu.SMEM)]
    in_specs += [pl.BlockSpec(memory_space=pl.ANY)] * n_smem_any
    in_specs += [pl.BlockSpec(memory_space=pltpu.VMEM)] * (len(operands) - 1 - n_smem_any)
    return pl.pallas_call(
        kernel,
        out_shape=out_shapes,
        in_specs=in_specs,
        out_specs=[pl.BlockSpec(memory_space=pltpu.VMEM)] * len(out_shapes),
        scratch_shapes=scratch,
        compiler_params=pltpu.CompilerParams(vmem_limit_bytes=28 * 1024 * 1024),
        cost_estimate=pl.CostEstimate(flops=flops, bytes_accessed=10_000_000, transcendentals=0),
    )(*operands)


def send_x(value, step):
    pairs = [
        (z * N_X + x, z * N_X + (x + step) % N_X) for z in range(N_Z) for x in range(N_X)
    ]
    return lax.ppermute(value, "fsdp", pairs)


def send_core(value):
    pairs = [(i, i ^ 1) for i in range(N_Y * N_CORE)]
    return lax.ppermute(value, "mp", pairs)


def copies_of(block):
    return jnp.broadcast_to(block[None], (N_Z,) + block.shape)


def gather_z(copies):
    return lax.all_to_all(copies, "fsdp", 0, 0, axis_index_groups=Z_GROUPS)


def add(left, right):
    return left.astype(jnp.float32) + right.astype(jnp.float32)


def on_device(tokens, cotangent, gate_weight, up_weight, down_weight):
    n_fsdp = lax.axis_size("fsdp")
    rows, width = tokens.shape
    depth, cols = gate_weight.shape
    n_feat = depth * n_fsdp
    factor = 1.0 / math.sqrt(rows * n_fsdp)
    me_x = lax.axis_index("fsdp") % N_X
    core = lax.axis_index("mp") % N_CORE

    gate_copies = copies_of(gate_weight)
    gate_copies, tokens, cotangent = lax.optimization_barrier((gate_copies, tokens, cotangent))
    stacked = jnp.concatenate([tokens, cotangent])
    both = lax.all_gather(stacked, "mp", axis=1, tiled=True)

    down_x = jnp.zeros((N_X, depth, cols), down_weight.dtype)
    down_x = lax.dynamic_update_slice(down_x, down_weight[None], (me_x, 0, 0))
    for step in (1, N_X - 1, 2):
        block = send_x(down_weight, step)
        down_x = lax.dynamic_update_slice(down_x, block[None], ((me_x - step) % N_X, 0, 0))

    gate_z = gather_z(gate_copies)
    gate_left, gate_right = send_x(gate_z, 1), send_x(gate_z, -1)
    gate_z, up_copies = lax.optimization_barrier((gate_z, copies_of(up_weight)))
    up_z = gather_z(up_copies)
    up_z, down_copies = lax.optimization_barrier((up_z, copies_of(down_x)))
    down_full = gather_z(down_copies).reshape(N_Z, N_CORE, 2 * depth, cols)

    up_z, gate_left, gate_right = lax.optimization_barrier((up_z, gate_left, gate_right))
    up_right, up_left = send_x(up_z, -1), send_x(up_z, 1)
    gate_far, up_far = send_x(gate_left, 1), send_x(up_right, -1)
    blocks = (gate_z, gate_left, gate_right, gate_far, up_z, up_left, up_right, up_far)

    place = jnp.stack([me_x, core]).astype(jnp.int32)
    value = jax.ShapeDtypeStruct((rows, cols), jnp.float32)
    full = pltpu.VMEM((N_Z, N_CORE, 2 * depth, cols), jnp.bfloat16)
    row_block = pltpu.VMEM((rows, n_feat), jnp.bfloat16)
    sems = pltpu.SemaphoreType.DMA
    gate_value, up_value, down_partial = call_kernel(
        forward_kernel,
        9,
        (place, both) + blocks,
        (value, value, jax.ShapeDtypeStruct((n_feat, cols), jnp.bfloat16)),
        [row_block, row_block, full, full, sems((2,)), sems((N_X,)), sems((N_X,))],
        6 * rows * n_feat * cols,
    )
    half = jax.ShapeDtypeStruct((N_Y, rows, width), jnp.bfloat16)
    other, mine = call_kernel(
        backward_kernel,
        10,
        (place, both, down_full) + blocks + (gate_value, up_value),
        (half, half),
        [row_block, full, full, full, sems((1,)), sems((1,)), sems((N_X,)), sems((N_X,))],
        6 * rows * n_feat * cols,
    )
    pair_sum = add(mine, send_core(other)).astype(jnp.bfloat16)
    summed = lax.all_to_all(pair_sum, "mp", 0, 0, axis_index_groups=Y_GROUPS)

    down_z = lax.psum_scatter(
        down_partial, "fsdp", scatter_dimension=0, axis_index_groups=Z_GROUPS, tiled=True
    ).reshape(N_X, depth, cols)
    down_sum = lax.dynamic_index_in_dim(down_z, me_x, 0, False).astype(jnp.float32)
    for step in (1, N_X - 1, 2):
        block = lax.dynamic_index_in_dim(down_z, (me_x + step) % N_X, 0, False)
        down_sum = down_sum + send_x(block, step).astype(jnp.float32)
    grad_down = (down_sum * factor).astype(jnp.bfloat16)
    input_grad = summed.astype(jnp.float32).sum(0).astype(jnp.bfloat16)
    return (input_grad, grad_down)


def solution(mesh):
    placed = P("fsdp", "mp")
    return jax.shard_map(
        on_device,
        mesh=mesh,
        in_specs=(placed,) * 5,
        out_specs=(placed, placed),
        check_vma=False,
    )
```

time: 167 us -> 177 us (1.060)
  waiting for transfers between devices: 52.5 us -> 63.5 us
  matrix products: 9.63 us -> 0 us
  Pallas kernels: 0 us -> 8.75 us
  local copies, waits for them, and re-layouts: 17.9 us -> 20.7 us
  starting transfers between devices: 65.1 us -> 62.4 us
    unnamed x18 -> x34, local copies, waits for them, and re-layouts: 3.3 us -> 16 us
    dot_general x8 -> x0, matrix products: 9.63 us -> none  [dot(): lax.dot_general(left, right, (dims, ((), ())), preferred_element_type=jnp...]
    pallas_call x0 -> x2, Pallas kernels: none -> 8.75 us  [call_kernel(): pl.pallas_call(kernel, out_shape=out_shapes, in_specs=in_specs, out_specs...]
    dynamic_update_slice x7 -> x0, local copies, waits for them, and re-layouts: 6.54 us -> none  [put_x(): lax.dynamic_update_slice(full, block[:, None], (0, (me + step) % N_X, 0, 0))]
    reduce_scatter x1, waiting for transfers between devices: 16.3 us -> 22.8 us  [on_device(): lax.psum_scatter(down_partial, 'fsdp', scatter_dimension=0, axis_index_gr...]
    all_to_all x3, starting transfers between devices: 20.4 us -> 17.4 us  [gather_z(): return lax.all_to_all(copies, 'fsdp', 0, 0, axis_index_groups=Z_GROUPS)]
    ppermute x12, waiting for transfers between devices: 16.3 us -> 19 us  [send_x(): return lax.ppermute(value, 'fsdp', pairs)]
    dynamic_slice x2 -> x0, local copies, waits for them, and re-layouts: 2.74 us -> none  [half_partial(): lax.dynamic_index_in_dim(full.reshape(N_Y, N_CORE, width, cols), which, 1...]
  transfers between devices with their start and end apart: 19 -> 19, of which waited for: 8 -> 10; matrix products, arithmetic and copies ran while one was open for 15% -> 3% of each run, Pallas kernels for 0% -> 5%
where the time goes in v3:
time: 177 us; the launch traced here: 175 us
  waiting for transfers between devices  63.5 us (36%)
  starting transfers between devices  62.4 us (35%)
  local copies, waits for them, and re-layouts  20.7 us (12%)
  between operations  14.4 us (8%)
  Pallas kernels  8.75 us (5%)
  other arithmetic  4.99 us (3%)
    ppermute x12, starting transfers between devices, send_x(): return lax.ppermute(value, 'fsdp', pairs)  36 us
    reduce_scatter x1, waiting for transfers between devices, on_device(): lax.psum_scatter(down_partial, 'fsdp', scatter_dimension=0, axis_index_gr...  22.8 us
    all_to_all x3, waiting for transfers between devices, gather_z(): return lax.all_to_all(copies, 'fsdp', 0, 0, axis_index_groups=Z_GROUPS)  19.4 us
    ppermute x12, waiting for transfers between devices, send_x(): return lax.ppermute(value, 'fsdp', pairs)  19 us
    all_to_all x3, starting transfers between devices, gather_z(): return lax.all_to_all(copies, 'fsdp', 0, 0, axis_index_groups=Z_GROUPS)  17.4 us
    unnamed x34, local copies, waits for them, and re-layouts  16 us
    pallas_call x2, Pallas kernels, call_kernel(): pl.pallas_call(kernel, out_shape=out_shapes, in_specs=in_specs, out_specs...  8.75 us
    all_to_all x1, starting transfers between devices, on_device(): summed = lax.all_to_all(pair_sum, 'mp', 0, 0, axis_index_groups=Y_GROUPS)  7.02 us
  transfers between devices with their start and end apart: 19, of which 10 were waited for; matrix products, arithmetic and copies ran while one was open for 3% of the time, Pallas kernels for 5%

profile of v3, /device:TPU:6, one launch (start us, length us, event | category | flops | bytes accessed | tf_op | source)
XLA Modules:
  0.0 174.8 jit_solution(7506183901118615594)
XLA Ops:
  10.5 10.3 %all-to-all-start = ((bf16[8,64,384]{2,1,0:T(8,128)(2,1)}), bf16[8,64,384]{2,1,0:T(8,128)(2,1)S(1)}, u32[]{:S(2)}, u32[]{:S(2)}) async-start(bf16[8,64,384]{2,1,0:T(8,128)(2,1)} %broadcast_in_dim.16), calls=%async_computation | async-start | bytes 786432 | tf_op jit(solution)/shard_map/all_to_all | solution.py:137
  20.8 2.4 %collective-permute-start = (bf16[64,384]{1,0:T(8,128)(2,1)S(1)}, bf16[64,384]{1,0:T(8,128)(2,1)S(1)}, u32[]{:S(2)}, u32[]{:S(2)}) collective-permute-start(bf16[64,384]{1,0:T(8,128)(2,1)S(1)} %copy-done.16), channel_id=1, source_target_pairs={{0,16},{16,32},{32,48},{48,0},{64,80},{80,96},{96,112},{112,64},{1... | collective-permute-start | bytes 147464 | tf_op jit(solution)/shard_map/ppermute | solution.py:124
  23.2 3.5 %collective-permute-start.1 = (bf16[64,384]{1,0:T(8,128)(2,1)S(1)}, bf16[64,384]{1,0:T(8,128)(2,1)S(1)}, u32[]{:S(2)}, u32[]{:S(2)}) collective-permute-start(bf16[64,384]{1,0:T(8,128)(2,1)S(1)} %copy-done.16), channel_id=1, source_target_pairs={{0,48},{16,0},{32,16},{48,32},{64,112},{80,64},{96,80},{112,96},{1... | collective-permute-start | bytes 147464 | tf_op jit(solution)/shard_map/ppermute | solution.py:124
  26.6 3.3 %collective-permute-start.2 = (bf16[64,384]{1,0:T(8,128)(2,1)S(1)}, bf16[64,384]{1,0:T(8,128)(2,1)S(1)}, u32[]{:S(2)}, u32[]{:S(2)}) collective-permute-start(bf16[64,384]{1,0:T(8,128)(2,1)S(1)} %copy-done.16), channel_id=1, source_target_pairs={{0,32},{16,48},{32,0},{48,16},{64,96},{80,112},{96,64},{112,80},{1... | collective-permute-start | bytes 147464 | tf_op jit(solution)/shard_map/ppermute | solution.py:124
  30.0 5.5 %all-to-all-done.g0 = bf16[8,64,384]{2,1,0:T(8,128)(2,1)S(1)} async-done(((bf16[8,64,384]{2,1,0:T(8,128)(2,1)}), bf16[8,64,384]{2,1,0:T(8,128)(2,1)S(1)}, u32[]{:S(2)}, u32[]{:S(2)}) %all-to-all-start) | async-done | bytes 393248 | tf_op jit(solution)/shard_map/all_to_all | solution.py:137
  36.3 3.5 %all-to-all-start.1 = ((bf16[8,64,384]{2,1,0:T(8,128)(2,1)}), bf16[8,64,384]{2,1,0:T(8,128)(2,1)S(1)}, u32[]{:S(2)}, u32[]{:S(2)}) async-start(bf16[8,64,384]{2,1,0:T(8,128)(2,1)} %broadcast_in_dim.34), calls=%async_computation.1 | async-start | bytes 786432 | tf_op jit(solution)/shard_map/all_to_all | solution.py:137
  39.9 13.9 %all-to-all-done.1.u0 = bf16[8,64,384]{2,1,0:T(8,128)(2,1)S(1)} async-done(((bf16[8,64,384]{2,1,0:T(8,128)(2,1)}), bf16[8,64,384]{2,1,0:T(8,128)(2,1)S(1)}, u32[]{:S(2)}, u32[]{:S(2)}) %all-to-all-start.1) | async-done | bytes 393248 | tf_op jit(solution)/shard_map/all_to_all | solution.py:137
  55.3 3.6 %all-to-all-start.2 = ((bf16[8,4,64,384]{3,2,1,0:T(8,128)(2,1)}), bf16[8,4,64,384]{3,2,1,0:T(8,128)(2,1)S(1)}, u32[]{:S(2)}, u32[]{:S(2)}) async-start(bf16[8,4,64,384]{3,2,1,0:T(8,128)(2,1)} %broadcast_in_dim.40), calls=%async_computation.2 | async-start | bytes 3145728 | tf_op jit(solution)/shard_map/all_to_all | solution.py:137
  59.0 2.4 %collective-permute-start.3 = (bf16[8,64,384]{2,1,0:T(8,128)(2,1)S(1)}, bf16[8,64,384]{2,1,0:T(8,128)(2,1)S(1)}, u32[]{:S(2)}, u32[]{:S(2)}) collective-permute-start(bf16[8,64,384]{2,1,0:T(8,128)(2,1)S(1)} %all-to-all-done.g0), channel_id=1, source_target_pairs={{0,16},{16,32},{32,48},{48,0},{64,80},{80,96},{96,112},{112,64},{1... | collective-permute-start | bytes 1179656 | tf_op jit(solution)/shard_map/ppermute | solution.py:124
  61.4 3.4 %collective-permute-start.4 = (bf16[8,64,384]{2,1,0:T(8,128)(2,1)S(1)}, bf16[8,64,384]{2,1,0:T(8,128)(2,1)S(1)}, u32[]{:S(2)}, u32[]{:S(2)}) collective-permute-start(bf16[8,64,384]{2,1,0:T(8,128)(2,1)S(1)} %all-to-all-done.g0), channel_id=1, source_target_pairs={{0,48},{16,0},{32,16},{48,32},{64,112},{80,64},{96,80},{112,96},{1... | collective-permute-start | bytes 1179656 | tf_op jit(solution)/shard_map/ppermute | solution.py:124
  64.8 4.7 %collective-permute-done.3.g1 = bf16[8,64,384]{2,1,0:T(8,128)(2,1)S(1)} collective-permute-done((bf16[8,64,384]{2,1,0:T(8,128)(2,1)S(1)}, bf16[8,64,384]{2,1,0:T(8,128)(2,1)S(1)}, u32[]{:S(2)}, u32[]{:S(2)}) %collective-permute-start.3) | collective-permute-done | bytes 393248 | tf_op jit(solution)/shard_map/ppermute | solution.py:124
  69.5 3.4 %collective-permute-done.4.g2 = bf16[8,64,384]{2,1,0:T(8,128)(2,1)S(1)} collective-permute-done((bf16[8,64,384]{2,1,0:T(8,128)(2,1)S(1)}, bf16[8,64,384]{2,1,0:T(8,128)(2,1)S(1)}, u32[]{:S(2)}, u32[]{:S(2)}) %collective-permute-start.4) | collective-permute-done | bytes 393248 | tf_op jit(solution)/shard_map/ppermute | solution.py:124
  75.8 4.9 %collective-permute-start.6 = (bf16[8,64,384]{2,1,0:T(8,128)(2,1)S(1)}, bf16[8,64,384]{2,1,0:T(8,128)(2,1)S(1)}, u32[]{:S(2)}, u32[]{:S(2)}) collective-permute-start(bf16[8,64,384]{2,1,0:T(8,128)(2,1)S(1)} %all-to-all-done.1.u0), channel_id=1, source_target_pairs={{0,16},{16,32},{32,48},{48,0},{64,80},{80,96},{96,112},{112,64},{1... | collective-permute-start | bytes 1179656 | tf_op jit(solution)/shard_map/ppermute | solution.py:124
  84.5 2.8 %collective-permute-start.8 = (bf16[8,64,384]{2,1,0:T(8,128)(2,1)S(1)}, bf16[8,64,384]{2,1,0:T(8,128)(2,1)}, u32[]{:S(2)}, u32[]{:S(2)}) collective-permute-start(bf16[8,64,384]{2,1,0:T(8,128)(2,1)S(1)} %collective-permute-done.7.u2), channel_id=1, source_target_pairs={{0,48},{16,0},{32,16},{48,32},{64,112},{80,64},{96,80},{112,96},{1... | collective-permute-start | bytes 1179656 | tf_op jit(solution)/shard_map/ppermute | solution.py:124
  88.3 5.7 %collective-permute-done.5.g3 = bf16[8,64,384]{2,1,0:T(8,128)(2,1)} collective-permute-done((bf16[8,64,384]{2,1,0:T(8,128)(2,1)S(1)}, bf16[8,64,384]{2,1,0:T(8,128)(2,1)}, u32[]{:S(2)}, u32[]{:S(2)}) %collective-permute-start.5) | collective-permute-done | bytes 393248 | tf_op jit(solution)/shard_map/ppermute | solution.py:124
  101.4 5.0 %shard_map.68 = (f32[384,384]{1,0:T(8,128)S(1)}, f32[384,384]{1,0:T(8,128)S(1)}, bf16[2048,384]{1,0:T(8,128)(2,1)S(1)}) custom-call(s32[2]{0:T(128)S(1)} %pad_add_fusion.place, bf16[768,2048]{1,0:T(8,128)(2,1)S(1)} %copy-done, bf16[8,64,384]{2,1,0:T(8,128)(2,1)S(1)} %all-to-all-done.g0, bf16[8,64,384]{2,1,0:T(8,128)(2,1)S(1)} %copy-done.4, ...), custom_call_target="tpu_custom_call" | custom-call | flops 1811939328 | bytes 10000000 | tf_op jit(solution)/shard_map/pallas_call | solution.py:109
  113.5 3.7 %shard_map.69 = (bf16[8,384,128]{2,1,0:T(8,128)(2,1)S(1)}, bf16[8,384,128]{2,1,0:T(8,128)(2,1)S(1)}) custom-call(s32[2]{0:T(128)S(1)} %pad_add_fusion.place, bf16[768,2048]{1,0:T(8,128)(2,1)S(1)} %copy-done.1, bf16[8,2,128,384]{3,2,1,0:T(8,128)(2,1)S(1)} %bitcast.21, bf16[8,64,384]{2,1,0:T(8,128)(2,1)S(1)} %all-to-all-done.g0, ...), custom_call_target="tpu_custom_call" | custom-call | flops 1811939328 | bytes 10000000 | tf_op jit(solution)/shard_map/pallas_call | solution.py:109
  119.1 2.3 %collective-permute-done.9 = bf16[8,384,128]{2,1,0:T(8,128)(2,1)S(1)} collective-permute-done((bf16[8,384,128]{2,1,0:T(8,128)(2,1)S(1)}, bf16[8,384,128]{2,1,0:T(8,128)(2,1)S(1)}, u32[]{:S(2)}, u32[]{:S(2)}) %collective-permute-start.9) | collective-permute-done | bytes 786464 | tf_op jit(solution)/shard_map/ppermute | solution.py:129
  122.5 7.0 %all-to-all-start.3 = ((bf16[8,384,128]{2,1,0:T(8,128)(2,1)}), bf16[8,384,128]{2,1,0:T(8,128)(2,1)S(1)}, u32[]{:S(2)}, u32[]{:S(2)}) async-start(bf16[8,384,128]{2,1,0:T(8,128)(2,1)} %add_convert_fusion), calls=%async_computation.3 | async-start | bytes 1572864 | tf_op jit(solution)/shard_map/all_to_all | solution.py:199
  129.5 22.8 %reduce-scatter.2.cloned.1.call-done = bf16[256,384]{1,0:T(8,128)(2,1)} async-done(((bf16[2048,384]{1,0:T(8,128)(2,1)}), bf16[256,384]{1,0:T(8,128)(2,1)}) %reduce-scatter.2.cloned.1.call-update) | async-done | bytes 196624 | tf_op jit(solution)/shard_map/reduce_scatter | solution.py:201
  153.2 2.4 %collective-permute-start.10 = (bf16[64,384]{1,0:T(8,128)(2,1)S(1)}, bf16[64,384]{1,0:T(8,128)(2,1)S(1)}, u32[]{:S(2)}, u32[]{:S(2)}) collective-permute-start(bf16[64,384]{1,0:T(8,128)(2,1)S(1)} %get-tuple-element.32), channel_id=1, source_target_pairs={{0,16},{16,32},{32,48},{48,0},{64,80},{80,96},{96,112},{112,64},{1... | collective-permute-start | bytes 147464 | tf_op jit(solution)/shard_map/ppermute | solution.py:124
  155.6 3.4 %collective-permute-start.11 = (bf16[64,384]{1,0:T(8,128)(2,1)S(1)}, bf16[64,384]{1,0:T(8,128)(2,1)S(1)}, u32[]{:S(2)}, u32[]{:S(2)}) collective-permute-start(bf16[64,384]{1,0:T(8,128)(2,1)S(1)} %get-tuple-element.34), channel_id=1, source_target_pairs={{0,48},{16,0},{32,16},{48,32},{64,112},{80,64},{96,80},{112,96},{1... | collective-permute-start | bytes 147464 | tf_op jit(solution)/shard_map/ppermute | solution.py:124
  159.0 3.4 %collective-permute-start.12 = (bf16[64,384]{1,0:T(8,128)(2,1)S(1)}, bf16[64,384]{1,0:T(8,128)(2,1)S(1)}, u32[]{:S(2)}, u32[]{:S(2)}) collective-permute-start(bf16[64,384]{1,0:T(8,128)(2,1)S(1)} %get-tuple-element.33), channel_id=1, source_target_pairs={{0,32},{16,48},{32,0},{48,16},{64,96},{80,112},{96,64},{112,80},{1... | collective-permute-start | bytes 147464 | tf_op jit(solution)/shard_map/ppermute | solution.py:124
  163.2 3.3 %collective-permute-done.12 = bf16[64,384]{1,0:T(8,128)(2,1)S(1)} collective-permute-done((bf16[64,384]{1,0:T(8,128)(2,1)S(1)}, bf16[64,384]{1,0:T(8,128)(2,1)S(1)}, u32[]{:S(2)}, u32[]{:S(2)}) %collective-permute-start.12) | collective-permute-done | bytes 49184 | tf_op jit(solution)/shard_map/ppermute | solution.py:124
  (66 shorter events, 33.8 us)
Async XLA Ops:
  7.2 13.6 %copy-start.16 = (bf16[64,384]{1,0:T(8,128)(2,1)S(1)}, bf16[64,384]{1,0:T(8,128)(2,1)}, u32[]{:S(2)}) copy-start(bf16[64,384]{1,0:T(8,128)(2,1)} %param.9) | copy-start | bytes 147460
  7.2 28.3 %copy-start.15 = (bf16[64,384]{1,0:T(8,128)(2,1)S(1)}, bf16[64,384]{1,0:T(8,128)(2,1)}, u32[]{:S(2)}) copy-start(bf16[64,384]{1,0:T(8,128)(2,1)} %param.8) | copy-start | bytes 147460
  7.2 88.3 %all-gather.2.cloned.1.call-start = ((), (), s32[]{:S(2)}) async-start(), calls=%async_computation.5 | async-start | bytes 3342336 | tf_op jit(solution)/shard_map/all_gather | solution.py:156
  10.5 25.0 %all-to-all-start = ((bf16[8,64,384]{2,1,0:T(8,128)(2,1)}), bf16[8,64,384]{2,1,0:T(8,128)(2,1)S(1)}, u32[]{:S(2)}, u32[]{:S(2)}) async-start(bf16[8,64,384]{2,1,0:T(8,128)(2,1)} %broadcast_in_dim.16), calls=%async_computation | async-start | bytes 786432 | tf_op jit(solution)/shard_map/all_to_all | solution.py:137
  20.8 19.1 %collective-permute-start = (bf16[64,384]{1,0:T(8,128)(2,1)S(1)}, bf16[64,384]{1,0:T(8,128)(2,1)S(1)}, u32[]{:S(2)}, u32[]{:S(2)}) collective-permute-start(bf16[64,384]{1,0:T(8,128)(2,1)S(1)} %copy-done.16), channel_id=1, source_target_pairs={{0,16},{16,32},{32,48},{48,0},{64,80},{80,96},{96,112},{112,64},{1... | collective-permute-start | bytes 147464 | tf_op jit(solution)/shard_map/ppermute | solution.py:124
  23.2 16.7 %collective-permute-start.1 = (bf16[64,384]{1,0:T(8,128)(2,1)S(1)}, bf16[64,384]{1,0:T(8,128)(2,1)S(1)}, u32[]{:S(2)}, u32[]{:S(2)}) collective-permute-start(bf16[64,384]{1,0:T(8,128)(2,1)S(1)} %copy-done.16), channel_id=1, source_target_pairs={{0,48},{16,0},{32,16},{48,32},{64,112},{80,64},{96,80},{112,96},{1... | collective-permute-start | bytes 147464 | tf_op jit(solution)/shard_map/ppermute | solution.py:124
  26.6 13.3 %collective-permute-start.2 = (bf16[64,384]{1,0:T(8,128)(2,1)S(1)}, bf16[64,384]{1,0:T(8,128)(2,1)S(1)}, u32[]{:S(2)}, u32[]{:S(2)}) collective-permute-start(bf16[64,384]{1,0:T(8,128)(2,1)S(1)} %copy-done.16), channel_id=1, source_target_pairs={{0,32},{16,48},{32,0},{48,16},{64,96},{80,112},{96,64},{112,80},{1... | collective-permute-start | bytes 147464 | tf_op jit(solution)/shard_map/ppermute | solution.py:124
  36.3 17.6 %all-to-all-start.1 = ((bf16[8,64,384]{2,1,0:T(8,128)(2,1)}), bf16[8,64,384]{2,1,0:T(8,128)(2,1)S(1)}, u32[]{:S(2)}, u32[]{:S(2)}) async-start(bf16[8,64,384]{2,1,0:T(8,128)(2,1)} %broadcast_in_dim.34), calls=%async_computation.1 | async-start | bytes 786432 | tf_op jit(solution)/shard_map/all_to_all | solution.py:137
  55.3 52.3 %all-to-all-start.2 = ((bf16[8,4,64,384]{3,2,1,0:T(8,128)(2,1)}), bf16[8,4,64,384]{3,2,1,0:T(8,128)(2,1)S(1)}, u32[]{:S(2)}, u32[]{:S(2)}) async-start(bf16[8,4,64,384]{3,2,1,0:T(8,128)(2,1)} %broadcast_in_dim.40), calls=%async_computation.2 | async-start | bytes 3145728 | tf_op jit(solution)/shard_map/all_to_all | solution.py:137
  58.9 93.4 %reduce-scatter.2.cloned.1.call-start = ((), (), s32[]{:S(2)}) async-start(), calls=%async_computation.6 | async-start | bytes 1769472 | tf_op jit(solution)/shard_map/reduce_scatter | solution.py:201
  59.0 10.6 %collective-permute-start.3 = (bf16[8,64,384]{2,1,0:T(8,128)(2,1)S(1)}, bf16[8,64,384]{2,1,0:T(8,128)(2,1)S(1)}, u32[]{:S(2)}, u32[]{:S(2)}) collective-permute-start(bf16[8,64,384]{2,1,0:T(8,128)(2,1)S(1)} %all-to-all-done.g0), channel_id=1, source_target_pairs={{0,16},{16,32},{32,48},{48,0},{64,80},{80,96},{96,112},{112,64},{1... | collective-permute-start | bytes 1179656 | tf_op jit(solution)/shard_map/ppermute | solution.py:124
  61.4 11.6 %collective-permute-start.4 = (bf16[8,64,384]{2,1,0:T(8,128)(2,1)S(1)}, bf16[8,64,384]{2,1,0:T(8,128)(2,1)S(1)}, u32[]{:S(2)}, u32[]{:S(2)}) collective-permute-start(bf16[8,64,384]{2,1,0:T(8,128)(2,1)S(1)} %all-to-all-done.g0), channel_id=1, source_target_pairs={{0,48},{16,0},{32,16},{48,32},{64,112},{80,64},{96,80},{112,96},{1... | collective-permute-start | bytes 1179656 | tf_op jit(solution)/shard_map/ppermute | solution.py:124
  73.7 10.9 %collective-permute-start.7 = (bf16[8,64,384]{2,1,0:T(8,128)(2,1)S(1)}, bf16[8,64,384]{2,1,0:T(8,128)(2,1)S(1)}, u32[]{:S(2)}, u32[]{:S(2)}) collective-permute-start(bf16[8,64,384]{2,1,0:T(8,128)(2,1)S(1)} %all-to-all-done.1.u0), channel_id=1, source_target_pairs={{0,48},{16,0},{32,16},{48,32},{64,112},{80,64},{96,80},{112,96},{1... | collective-permute-start | bytes 1179656 | tf_op jit(solution)/shard_map/ppermute | solution.py:124
  75.8 18.1 %collective-permute-start.6 = (bf16[8,64,384]{2,1,0:T(8,128)(2,1)S(1)}, bf16[8,64,384]{2,1,0:T(8,128)(2,1)S(1)}, u32[]{:S(2)}, u32[]{:S(2)}) collective-permute-start(bf16[8,64,384]{2,1,0:T(8,128)(2,1)S(1)} %all-to-all-done.1.u0), channel_id=1, source_target_pairs={{0,16},{16,32},{32,48},{48,0},{64,80},{80,96},{96,112},{112,64},{1... | collective-permute-start | bytes 1179656 | tf_op jit(solution)/shard_map/ppermute | solution.py:124
  80.7 13.2 %collective-permute-start.5 = (bf16[8,64,384]{2,1,0:T(8,128)(2,1)S(1)}, bf16[8,64,384]{2,1,0:T(8,128)(2,1)}, u32[]{:S(2)}, u32[]{:S(2)}) collective-permute-start(bf16[8,64,384]{2,1,0:T(8,128)(2,1)S(1)} %collective-permute-done.3.g1), channel_id=1, source_target_pairs={{0,16},{16,32},{32,48},{48,0},{64,80},{80,96},{96,112},{112,64},{1... | collective-permute-start | bytes 1179656 | tf_op jit(solution)/shard_map/ppermute | solution.py:124
  84.5 11.0 %collective-permute-start.8 = (bf16[8,64,384]{2,1,0:T(8,128)(2,1)S(1)}, bf16[8,64,384]{2,1,0:T(8,128)(2,1)}, u32[]{:S(2)}, u32[]{:S(2)}) collective-permute-start(bf16[8,64,384]{2,1,0:T(8,128)(2,1)S(1)} %collective-permute-done.7.u2), channel_id=1, source_target_pairs={{0,48},{16,0},{32,16},{48,32},{64,112},{80,64},{96,80},{112,96},{1... | collective-permute-start | bytes 1179656 | tf_op jit(solution)/shard_map/ppermute | solution.py:124
  95.5 1.9 %copy-start = (bf16[768,2048]{1,0:T(8,128)(2,1)S(1)}, bf16[768,2048]{1,0:T(8,128)(2,1)}, u32[]{:S(2)}) copy-start(bf16[768,2048]{1,0:T(8,128)(2,1)} %all-gather.2.cloned.1.call-done.rows_ref) | copy-start | bytes 9437188
  106.4 1.1 copy-start.2
  107.6 1.9 %copy-start.1 = (bf16[768,2048]{1,0:T(8,128)(2,1)S(1)}, bf16[768,2048]{1,0:T(8,128)(2,1)}, u32[]{:S(2)}) copy-start(bf16[768,2048]{1,0:T(8,128)(2,1)} %all-gather.2.cloned.1.call-done.rows_ref) | copy-start | bytes 9437188
  117.2 4.2 %collective-permute-start.9 = (bf16[8,384,128]{2,1,0:T(8,128)(2,1)S(1)}, bf16[8,384,128]{2,1,0:T(8,128)(2,1)S(1)}, u32[]{:S(2)}, u32[]{:S(2)}) collective-permute-start(bf16[8,384,128]{2,1,0:T(8,128)(2,1)S(1)} %get-tuple-element.30), channel_id=1, source_target_pairs={{0,1},{1,0},{2,3},{3,2},{4,5},{5,4},{6,7},{7,6},{8,9},{9,8},{10,11... | collective-permute-start | bytes 2359304 | tf_op jit(solution)/shard_map/ppermute | solution.py:129
  122.5 39.9 %all-to-all-start.3 = ((bf16[8,384,128]{2,1,0:T(8,128)(2,1)}), bf16[8,384,128]{2,1,0:T(8,128)(2,1)S(1)}, u32[]{:S(2)}, u32[]{:S(2)}) async-start(bf16[8,384,128]{2,1,0:T(8,128)(2,1)} %add_convert_fusion), calls=%async_computation.3 | async-start | bytes 1572864 | tf_op jit(solution)/shard_map/all_to_all | solution.py:199
  153.2 10.0 %collective-permute-start.10 = (bf16[64,384]{1,0:T(8,128)(2,1)S(1)}, bf16[64,384]{1,0:T(8,128)(2,1)S(1)}, u32[]{:S(2)}, u32[]{:S(2)}) collective-permute-start(bf16[64,384]{1,0:T(8,128)(2,1)S(1)} %get-tuple-element.32), channel_id=1, source_target_pairs={{0,16},{16,32},{32,48},{48,0},{64,80},{80,96},{96,112},{112,64},{1... | collective-permute-start | bytes 147464 | tf_op jit(solution)/shard_map/ppermute | solution.py:124
  155.6 7.6 %collective-permute-start.11 = (bf16[64,384]{1,0:T(8,128)(2,1)S(1)}, bf16[64,384]{1,0:T(8,128)(2,1)S(1)}, u32[]{:S(2)}, u32[]{:S(2)}) collective-permute-start(bf16[64,384]{1,0:T(8,128)(2,1)S(1)} %get-tuple-element.34), channel_id=1, source_target_pairs={{0,48},{16,0},{32,16},{48,32},{64,112},{80,64},{96,80},{112,96},{1... | collective-permute-start | bytes 147464 | tf_op jit(solution)/shard_map/ppermute | solution.py:124
  159.0 7.5 %collective-permute-start.12 = (bf16[64,384]{1,0:T(8,128)(2,1)S(1)}, bf16[64,384]{1,0:T(8,128)(2,1)S(1)}, u32[]{:S(2)}, u32[]{:S(2)}) collective-permute-start(bf16[64,384]{1,0:T(8,128)(2,1)S(1)} %get-tuple-element.33), channel_id=1, source_target_pairs={{0,32},{16,48},{32,0},{48,16},{64,96},{80,112},{96,64},{112,80},{1... | collective-permute-start | bytes 147464 | tf_op jit(solution)/shard_map/ppermute | solution.py:124
  (12 other events, 11.1 us)
Sparse Core Ops, SparseCore 0:
  10.6 52.2 all-gather.1
  107.7 44.5 reduce-scatter.1

commit v4 on v3

--- a/solution.py
+++ b/solution.py
@@ -112,7 +112,7 @@
         in_specs=in_specs,
         out_specs=[pl.BlockSpec(memory_space=pltpu.VMEM)] * len(out_shapes),
         scratch_shapes=scratch,
-        compiler_params=pltpu.CompilerParams(vmem_limit_bytes=28 * 1024 * 1024),
+        compiler_params=pltpu.CompilerParams(vmem_limit_bytes=60 * 1024 * 1024),
         cost_estimate=pl.CostEstimate(flops=flops, bytes_accessed=10_000_000, transcendentals=0),
     )(*operands)
 
@@ -165,10 +165,9 @@
     gate_left, gate_right = send_x(gate_z, 1), send_x(gate_z, -1)
     gate_z, up_copies = lax.optimization_barrier((gate_z, copies_of(up_weight)))
     up_z = gather_z(up_copies)
-    up_z, down_copies = lax.optimization_barrier((up_z, copies_of(down_x)))
+    up_z, down_copies, gate_left = lax.optimization_barrier((up_z, copies_of(down_x), gate_left))
     down_full = gather_z(down_copies).reshape(N_Z, N_CORE, 2 * depth, cols)
 
-    up_z, gate_left, gate_right = lax.optimization_barrier((up_z, gate_left, gate_right))
     up_right, up_left = send_x(up_z, -1), send_x(up_z, 1)
     gate_far, up_far = send_x(gate_left, 1), send_x(up_right, -1)
     blocks = (gate_z, gate_left, gate_right, gate_far, up_z, up_left, up_right, up_far)

time: 177 us -> 166 us (0.938)
  local copies, waits for them, and re-layouts: 20.7 us -> 6.05 us
  Pallas kernels: 8.75 us -> 14.3 us
  waiting for transfers between devices: 63.5 us -> 59.3 us
    unnamed x34 -> x16, local copies, waits for them, and re-layouts: 16 us -> 1.23 us
    all_to_all x3, waiting for transfers between devices: 19.4 us -> 9.01 us  [gather_z(): return lax.all_to_all(copies, 'fsdp', 0, 0, axis_index_groups=Z_GROUPS)]
    ppermute x12, waiting for transfers between devices: 19 us -> 26 us  [send_x(): return lax.ppermute(value, 'fsdp', pairs)]
    pallas_call x2, Pallas kernels: 8.75 us -> 14.3 us  [call_kernel(): pl.pallas_call(kernel, out_shape=out_shapes, in_specs=in_specs, out_specs...]
  transfers between devices with their start and end apart: 19 -> 19, of which waited for: 10 -> 11; matrix products, arithmetic and copies ran while one was open for 3% -> 4% of each run, Pallas kernels for 5% -> 9%
where the time goes in v4:
time: 166 us; the launch traced here: 164 us
  starting transfers between devices  63.3 us (38%)
  waiting for transfers between devices  59.3 us (36%)
  between operations  14.4 us (9%)
  Pallas kernels  14.3 us (9%)
  other arithmetic  6.67 us (4%)
  local copies, waits for them, and re-layouts  6.05 us (4%)
    ppermute x12, starting transfers between devices, send_x(): return lax.ppermute(value, 'fsdp', pairs)  35.6 us
    ppermute x12, waiting for transfers between devices, send_x(): return lax.ppermute(value, 'fsdp', pairs)  26 us
    reduce_scatter x1, waiting for transfers between devices, on_device(): lax.psum_scatter(down_partial, 'fsdp', scatter_dimension=0, axis_index_gr...  21.8 us
    all_to_all x3, starting transfers between devices, gather_z(): return lax.all_to_all(copies, 'fsdp', 0, 0, axis_index_groups=Z_GROUPS)  18.6 us
    pallas_call x2, Pallas kernels, call_kernel(): pl.pallas_call(kernel, out_shape=out_shapes, in_specs=in_specs, out_specs...  14.3 us
    all_to_all x3, waiting for transfers between devices, gather_z(): return lax.all_to_all(copies, 'fsdp', 0, 0, axis_index_groups=Z_GROUPS)  9.01 us
    all_to_all x1, starting transfers between devices, on_device(): summed = lax.all_to_all(pair_sum, 'mp', 0, 0, axis_index_groups=Y_GROUPS)  7.12 us
    broadcast_in_dim x4, local copies, waits for them, and re-layouts, copies_of(): return jnp.broadcast_to(block[None], (N_Z,) + block.shape)  3.88 us
  transfers between devices with their start and end apart: 19, of which 11 were waited for; matrix products, arithmetic and copies ran while one was open for 4% of the time, Pallas kernels for 9%

profile of v4, /device:TPU:6, one launch (start us, length us, event | category | flops | bytes accessed | tf_op | source)
XLA Modules:
  0.0 164.1 jit_solution(1189218531666329233)
XLA Ops:
  10.5 10.3 %all-to-all-start = ((bf16[8,64,384]{2,1,0:T(8,128)(2,1)}), bf16[8,64,384]{2,1,0:T(8,128)(2,1)S(1)}, u32[]{:S(2)}, u32[]{:S(2)}) async-start(bf16[8,64,384]{2,1,0:T(8,128)(2,1)} %broadcast_in_dim.16), calls=%async_computation | async-start | bytes 786432 | tf_op jit(solution)/shard_map/all_to_all | solution.py:137
  20.8 2.4 %collective-permute-start = (bf16[64,384]{1,0:T(8,128)(2,1)S(1)}, bf16[64,384]{1,0:T(8,128)(2,1)S(1)}, u32[]{:S(2)}, u32[]{:S(2)}) collective-permute-start(bf16[64,384]{1,0:T(8,128)(2,1)S(1)} %copy-done.7), channel_id=1, source_target_pairs={{0,16},{16,32},{32,48},{48,0},{64,80},{80,96},{96,112},{112,64},{1... | collective-permute-start | bytes 147464 | tf_op jit(solution)/shard_map/ppermute | solution.py:124
  23.2 3.5 %collective-permute-start.1 = (bf16[64,384]{1,0:T(8,128)(2,1)S(1)}, bf16[64,384]{1,0:T(8,128)(2,1)S(1)}, u32[]{:S(2)}, u32[]{:S(2)}) collective-permute-start(bf16[64,384]{1,0:T(8,128)(2,1)S(1)} %copy-done.7), channel_id=1, source_target_pairs={{0,48},{16,0},{32,16},{48,32},{64,112},{80,64},{96,80},{112,96},{1... | collective-permute-start | bytes 147464 | tf_op jit(solution)/shard_map/ppermute | solution.py:124
  26.6 3.3 %collective-permute-start.2 = (bf16[64,384]{1,0:T(8,128)(2,1)S(1)}, bf16[64,384]{1,0:T(8,128)(2,1)S(1)}, u32[]{:S(2)}, u32[]{:S(2)}) collective-permute-start(bf16[64,384]{1,0:T(8,128)(2,1)S(1)} %copy-done.7), channel_id=1, source_target_pairs={{0,32},{16,48},{32,0},{48,16},{64,96},{80,112},{96,64},{112,80},{1... | collective-permute-start | bytes 147464 | tf_op jit(solution)/shard_map/ppermute | solution.py:124
  30.0 5.5 %all-to-all-done.g0 = bf16[8,64,384]{2,1,0:T(8,128)(2,1)S(1)} async-done(((bf16[8,64,384]{2,1,0:T(8,128)(2,1)}), bf16[8,64,384]{2,1,0:T(8,128)(2,1)S(1)}, u32[]{:S(2)}, u32[]{:S(2)}) %all-to-all-start) | async-done | bytes 393248 | tf_op jit(solution)/shard_map/all_to_all | solution.py:137
  36.3 3.5 %all-to-all-start.1 = ((bf16[8,64,384]{2,1,0:T(8,128)(2,1)}), bf16[8,64,384]{2,1,0:T(8,128)(2,1)S(1)}, u32[]{:S(2)}, u32[]{:S(2)}) async-start(bf16[8,64,384]{2,1,0:T(8,128)(2,1)} %broadcast_in_dim.34), calls=%async_computation.1 | async-start | bytes 786432 | tf_op jit(solution)/shard_map/all_to_all | solution.py:137
  39.9 2.4 %collective-permute-start.3 = (bf16[8,64,384]{2,1,0:T(8,128)(2,1)S(1)}, bf16[8,64,384]{2,1,0:T(8,128)(2,1)S(1)}, u32[]{:S(2)}, u32[]{:S(2)}) collective-permute-start(bf16[8,64,384]{2,1,0:T(8,128)(2,1)S(1)} %all-to-all-done.g0), channel_id=1, source_target_pairs={{0,16},{16,32},{32,48},{48,0},{64,80},{80,96},{96,112},{112,64},{1... | collective-permute-start | bytes 1179656 | tf_op jit(solution)/shard_map/ppermute | solution.py:124
  42.4 9.5 %collective-permute-done.3.g1 = bf16[8,64,384]{2,1,0:T(8,128)(2,1)S(1)} collective-permute-done((bf16[8,64,384]{2,1,0:T(8,128)(2,1)S(1)}, bf16[8,64,384]{2,1,0:T(8,128)(2,1)S(1)}, u32[]{:S(2)}, u32[]{:S(2)}) %collective-permute-start.3) | collective-permute-done | bytes 393248 | tf_op jit(solution)/shard_map/ppermute | solution.py:124
  55.3 4.9 %all-to-all-start.2 = ((bf16[8,4,64,384]{3,2,1,0:T(8,128)(2,1)}), bf16[8,4,64,384]{3,2,1,0:T(8,128)(2,1)S(1)}, u32[]{:S(2)}, u32[]{:S(2)}) async-start(bf16[8,4,64,384]{3,2,1,0:T(8,128)(2,1)} %broadcast_in_dim.40), calls=%async_computation.2 | async-start | bytes 3145728 | tf_op jit(solution)/shard_map/all_to_all | solution.py:137
  60.2 2.7 %collective-permute-start.7 = (bf16[8,64,384]{2,1,0:T(8,128)(2,1)S(1)}, bf16[8,64,384]{2,1,0:T(8,128)(2,1)S(1)}, u32[]{:S(2)}, u32[]{:S(2)}) collective-permute-start(bf16[8,64,384]{2,1,0:T(8,128)(2,1)S(1)} %all-to-all-done.1.u0), channel_id=1, source_target_pairs={{0,48},{16,0},{32,16},{48,32},{64,112},{80,64},{96,80},{112,96},{1... | collective-permute-start | bytes 1179656 | tf_op jit(solution)/shard_map/ppermute | solution.py:124
  63.0 2.4 %collective-permute-start.4 = (bf16[8,64,384]{2,1,0:T(8,128)(2,1)S(1)}, bf16[8,64,384]{2,1,0:T(8,128)(2,1)S(1)}, u32[]{:S(2)}, u32[]{:S(2)}) collective-permute-start(bf16[8,64,384]{2,1,0:T(8,128)(2,1)S(1)} %all-to-all-done.g0), channel_id=1, source_target_pairs={{0,48},{16,0},{32,16},{48,32},{64,112},{80,64},{96,80},{112,96},{1... | collective-permute-start | bytes 1179656 | tf_op jit(solution)/shard_map/ppermute | solution.py:124
  65.5 4.6 %collective-permute-start.6 = (bf16[8,64,384]{2,1,0:T(8,128)(2,1)S(1)}, bf16[8,64,384]{2,1,0:T(8,128)(2,1)}, u32[]{:S(2)}, u32[]{:S(2)}) collective-permute-start(bf16[8,64,384]{2,1,0:T(8,128)(2,1)S(1)} %all-to-all-done.1.u0), channel_id=1, source_target_pairs={{0,16},{16,32},{32,48},{48,0},{64,80},{80,96},{96,112},{112,64},{1... | collective-permute-start | bytes 1179656 | tf_op jit(solution)/shard_map/ppermute | solution.py:124
  70.1 3.1 %collective-permute-start.5 = (bf16[8,64,384]{2,1,0:T(8,128)(2,1)S(1)}, bf16[8,64,384]{2,1,0:T(8,128)(2,1)}, u32[]{:S(2)}, u32[]{:S(2)}) collective-permute-start(bf16[8,64,384]{2,1,0:T(8,128)(2,1)S(1)} %collective-permute-done.3.g1), channel_id=1, source_target_pairs={{0,16},{16,32},{32,48},{48,0},{64,80},{80,96},{96,112},{112,64},{1... | collective-permute-start | bytes 1179656 | tf_op jit(solution)/shard_map/ppermute | solution.py:124
  77.9 5.9 %collective-permute-done.4.g2 = bf16[8,64,384]{2,1,0:T(8,128)(2,1)S(1)} collective-permute-done((bf16[8,64,384]{2,1,0:T(8,128)(2,1)S(1)}, bf16[8,64,384]{2,1,0:T(8,128)(2,1)S(1)}, u32[]{:S(2)}, u32[]{:S(2)}) %collective-permute-start.4) | collective-permute-done | bytes 393248 | tf_op jit(solution)/shard_map/ppermute | solution.py:124
  84.1 4.9 %collective-permute-done.8.u3 = bf16[8,64,384]{2,1,0:T(8,128)(2,1)} collective-permute-done((bf16[8,64,384]{2,1,0:T(8,128)(2,1)S(1)}, bf16[8,64,384]{2,1,0:T(8,128)(2,1)}, u32[]{:S(2)}, u32[]{:S(2)}) %collective-permute-start.8) | collective-permute-done | bytes 393248 | tf_op jit(solution)/shard_map/ppermute | solution.py:124
  88.9 7.7 %shard_map.68 = (f32[384,384]{1,0:T(8,128)}, f32[384,384]{1,0:T(8,128)}, bf16[2048,384]{1,0:T(8,128)(2,1)}) custom-call(s32[2]{0:T(128)} %pad_add_fusion.place, bf16[768,2048]{1,0:T(8,128)(2,1)} %all-gather.2.cloned.1.call-done.rows_ref, bf16[8,64,384]{2,1,0:T(8,128)(2,1)} %copy-done.1, bf16[8,64,384]{2,1,0:T(8,128)(2,1)} %copy-done.3, ...), custom_call_target="tpu_custom_call" | custom-call | flops 1811939328 | bytes 10000000 | tf_op jit(solution)/shard_map/pallas_call | solution.py:109
  99.4 6.6 %shard_map.69 = (bf16[8,384,128]{2,1,0:T(8,128)(2,1)}, bf16[8,384,128]{2,1,0:T(8,128)(2,1)}) custom-call(s32[2]{0:T(128)} %pad_add_fusion.place, bf16[768,2048]{1,0:T(8,128)(2,1)} %all-gather.2.cloned.1.call-done.rows_ref, bf16[8,2,128,384]{3,2,1,0:T(8,128)(2,1)} %bitcast.21, bf16[8,64,384]{2,1,0:T(8,128)(2,1)} %copy-done.1, bf16[8,64,384]{2,1,0:T(8,128)(2,1)} %copy-done.3, ...), custom_call_target="tpu_custom_call" | custom-call | flops 1811939328 | bytes 10000000 | tf_op jit(solution)/shard_map/pallas_call | solution.py:109
  108.0 2.5 %collective-permute-done.9 = bf16[8,384,128]{2,1,0:T(8,128)(2,1)S(1)} collective-permute-done((bf16[8,384,128]{2,1,0:T(8,128)(2,1)}, bf16[8,384,128]{2,1,0:T(8,128)(2,1)S(1)}, u32[]{:S(2)}, u32[]{:S(2)}) %collective-permute-start.9) | collective-permute-done | bytes 786464 | tf_op jit(solution)/shard_map/ppermute | solution.py:129
  112.7 7.1 %all-to-all-start.3 = ((bf16[8,384,128]{2,1,0:T(8,128)(2,1)}), bf16[8,384,128]{2,1,0:T(8,128)(2,1)S(1)}, u32[]{:S(2)}, u32[]{:S(2)}) async-start(bf16[8,384,128]{2,1,0:T(8,128)(2,1)} %add_convert_fusion), calls=%async_computation.3 | async-start | bytes 1572864 | tf_op jit(solution)/shard_map/all_to_all | solution.py:198
  119.8 21.8 %reduce-scatter.2.cloned.1.call-done = bf16[256,384]{1,0:T(8,128)(2,1)} async-done(((bf16[2048,384]{1,0:T(8,128)(2,1)}), bf16[256,384]{1,0:T(8,128)(2,1)}) %reduce-scatter.2.cloned.1.call-update) | async-done | bytes 196624 | tf_op jit(solution)/shard_map/reduce_scatter | solution.py:200
  142.4 2.5 %collective-permute-start.10 = (bf16[64,384]{1,0:T(8,128)(2,1)S(1)}, bf16[64,384]{1,0:T(8,128)(2,1)S(1)}, u32[]{:S(2)}, u32[]{:S(2)}) collective-permute-start(bf16[64,384]{1,0:T(8,128)(2,1)S(1)} %get-tuple-element.28), channel_id=1, source_target_pairs={{0,16},{16,32},{32,48},{48,0},{64,80},{80,96},{96,112},{112,64},{1... | collective-permute-start | bytes 147464 | tf_op jit(solution)/shard_map/ppermute | solution.py:124
  144.9 3.4 %collective-permute-start.11 = (bf16[64,384]{1,0:T(8,128)(2,1)S(1)}, bf16[64,384]{1,0:T(8,128)(2,1)S(1)}, u32[]{:S(2)}, u32[]{:S(2)}) collective-permute-start(bf16[64,384]{1,0:T(8,128)(2,1)S(1)} %get-tuple-element.30), channel_id=1, source_target_pairs={{0,48},{16,0},{32,16},{48,32},{64,112},{80,64},{96,80},{112,96},{1... | collective-permute-start | bytes 147464 | tf_op jit(solution)/shard_map/ppermute | solution.py:124
  148.3 3.4 %collective-permute-start.12 = (bf16[64,384]{1,0:T(8,128)(2,1)S(1)}, bf16[64,384]{1,0:T(8,128)(2,1)S(1)}, u32[]{:S(2)}, u32[]{:S(2)}) collective-permute-start(bf16[64,384]{1,0:T(8,128)(2,1)S(1)} %get-tuple-element.29), channel_id=1, source_target_pairs={{0,32},{16,48},{32,0},{48,16},{64,96},{80,112},{96,64},{112,80},{1... | collective-permute-start | bytes 147464 | tf_op jit(solution)/shard_map/ppermute | solution.py:124
  152.4 3.3 %collective-permute-done.12 = bf16[64,384]{1,0:T(8,128)(2,1)S(1)} collective-permute-done((bf16[64,384]{1,0:T(8,128)(2,1)S(1)}, bf16[64,384]{1,0:T(8,128)(2,1)S(1)}, u32[]{:S(2)}, u32[]{:S(2)}) %collective-permute-start.12) | collective-permute-done | bytes 49184 | tf_op jit(solution)/shard_map/ppermute | solution.py:124
  (48 shorter events, 22.6 us)
Async XLA Ops:
  7.2 13.6 %copy-start.7 = (bf16[64,384]{1,0:T(8,128)(2,1)S(1)}, bf16[64,384]{1,0:T(8,128)(2,1)}, u32[]{:S(2)}) copy-start(bf16[64,384]{1,0:T(8,128)(2,1)} %param.9) | copy-start | bytes 147460
  7.2 28.3 %copy-start.6 = (bf16[64,384]{1,0:T(8,128)(2,1)S(1)}, bf16[64,384]{1,0:T(8,128)(2,1)}, u32[]{:S(2)}) copy-start(bf16[64,384]{1,0:T(8,128)(2,1)} %param.8) | copy-start | bytes 147460
  7.2 81.7 %all-gather.2.cloned.1.call-start = ((), (), s32[]{:S(2)}) async-start(), calls=%async_computation.5 | async-start | bytes 3342336 | tf_op jit(solution)/shard_map/all_gather | solution.py:156
  10.5 25.0 %all-to-all-start = ((bf16[8,64,384]{2,1,0:T(8,128)(2,1)}), bf16[8,64,384]{2,1,0:T(8,128)(2,1)S(1)}, u32[]{:S(2)}, u32[]{:S(2)}) async-start(bf16[8,64,384]{2,1,0:T(8,128)(2,1)} %broadcast_in_dim.16), calls=%async_computation | async-start | bytes 786432 | tf_op jit(solution)/shard_map/all_to_all | solution.py:137
  20.8 19.1 %collective-permute-start = (bf16[64,384]{1,0:T(8,128)(2,1)S(1)}, bf16[64,384]{1,0:T(8,128)(2,1)S(1)}, u32[]{:S(2)}, u32[]{:S(2)}) collective-permute-start(bf16[64,384]{1,0:T(8,128)(2,1)S(1)} %copy-done.7), channel_id=1, source_target_pairs={{0,16},{16,32},{32,48},{48,0},{64,80},{80,96},{96,112},{112,64},{1... | collective-permute-start | bytes 147464 | tf_op jit(solution)/shard_map/ppermute | solution.py:124
  23.2 19.2 %collective-permute-start.1 = (bf16[64,384]{1,0:T(8,128)(2,1)S(1)}, bf16[64,384]{1,0:T(8,128)(2,1)S(1)}, u32[]{:S(2)}, u32[]{:S(2)}) collective-permute-start(bf16[64,384]{1,0:T(8,128)(2,1)S(1)} %copy-done.7), channel_id=1, source_target_pairs={{0,48},{16,0},{32,16},{48,32},{64,112},{80,64},{96,80},{112,96},{1... | collective-permute-start | bytes 147464 | tf_op jit(solution)/shard_map/ppermute | solution.py:124
  26.6 15.7 %collective-permute-start.2 = (bf16[64,384]{1,0:T(8,128)(2,1)S(1)}, bf16[64,384]{1,0:T(8,128)(2,1)S(1)}, u32[]{:S(2)}, u32[]{:S(2)}) collective-permute-start(bf16[64,384]{1,0:T(8,128)(2,1)S(1)} %copy-done.7), channel_id=1, source_target_pairs={{0,32},{16,48},{32,0},{48,16},{64,96},{80,112},{96,64},{112,80},{1... | collective-permute-start | bytes 147464 | tf_op jit(solution)/shard_map/ppermute | solution.py:124
  35.5 27.5 %copy-start.1 = (bf16[8,64,384]{2,1,0:T(8,128)(2,1)}, bf16[8,64,384]{2,1,0:T(8,128)(2,1)S(1)}, u32[]{:S(2)}) copy-start(bf16[8,64,384]{2,1,0:T(8,128)(2,1)S(1)} %all-to-all-done.g0) | copy-start | bytes 1179652
  36.3 17.6 %all-to-all-start.1 = ((bf16[8,64,384]{2,1,0:T(8,128)(2,1)}), bf16[8,64,384]{2,1,0:T(8,128)(2,1)S(1)}, u32[]{:S(2)}, u32[]{:S(2)}) async-start(bf16[8,64,384]{2,1,0:T(8,128)(2,1)} %broadcast_in_dim.34), calls=%async_computation.1 | async-start | bytes 786432 | tf_op jit(solution)/shard_map/all_to_all | solution.py:137
  39.9 12.0 %collective-permute-start.3 = (bf16[8,64,384]{2,1,0:T(8,128)(2,1)S(1)}, bf16[8,64,384]{2,1,0:T(8,128)(2,1)S(1)}, u32[]{:S(2)}, u32[]{:S(2)}) collective-permute-start(bf16[8,64,384]{2,1,0:T(8,128)(2,1)S(1)} %all-to-all-done.g0), channel_id=1, source_target_pairs={{0,16},{16,32},{32,48},{48,0},{64,80},{80,96},{96,112},{112,64},{1... | collective-permute-start | bytes 1179656 | tf_op jit(solution)/shard_map/ppermute | solution.py:124
  51.9 18.2 %copy-start.3 = (bf16[8,64,384]{2,1,0:T(8,128)(2,1)}, bf16[8,64,384]{2,1,0:T(8,128)(2,1)S(1)}, u32[]{:S(2)}) copy-start(bf16[8,64,384]{2,1,0:T(8,128)(2,1)S(1)} %collective-permute-done.3.g1) | copy-start | bytes 1179652
  55.3 42.9 %all-to-all-start.2 = ((bf16[8,4,64,384]{3,2,1,0:T(8,128)(2,1)}), bf16[8,4,64,384]{3,2,1,0:T(8,128)(2,1)S(1)}, u32[]{:S(2)}, u32[]{:S(2)}) async-start(bf16[8,4,64,384]{3,2,1,0:T(8,128)(2,1)} %broadcast_in_dim.40), calls=%async_computation.2 | async-start | bytes 3145728 | tf_op jit(solution)/shard_map/all_to_all | solution.py:137
  60.2 81.4 %reduce-scatter.2.cloned.1.call-start = ((), (), s32[]{:S(2)}) async-start(), calls=%async_computation.6 | async-start | bytes 1769472 | tf_op jit(solution)/shard_map/reduce_scatter | solution.py:200
  60.2 15.2 %collective-permute-start.7 = (bf16[8,64,384]{2,1,0:T(8,128)(2,1)S(1)}, bf16[8,64,384]{2,1,0:T(8,128)(2,1)S(1)}, u32[]{:S(2)}, u32[]{:S(2)}) collective-permute-start(bf16[8,64,384]{2,1,0:T(8,128)(2,1)S(1)} %all-to-all-done.1.u0), channel_id=1, source_target_pairs={{0,48},{16,0},{32,16},{48,32},{64,112},{80,64},{96,80},{112,96},{1... | collective-permute-start | bytes 1179656 | tf_op jit(solution)/shard_map/ppermute | solution.py:124
  63.0 20.8 %collective-permute-start.4 = (bf16[8,64,384]{2,1,0:T(8,128)(2,1)S(1)}, bf16[8,64,384]{2,1,0:T(8,128)(2,1)S(1)}, u32[]{:S(2)}, u32[]{:S(2)}) collective-permute-start(bf16[8,64,384]{2,1,0:T(8,128)(2,1)S(1)} %all-to-all-done.g0), channel_id=1, source_target_pairs={{0,48},{16,0},{32,16},{48,32},{64,112},{80,64},{96,80},{112,96},{1... | collective-permute-start | bytes 1179656 | tf_op jit(solution)/shard_map/ppermute | solution.py:124
  65.5 18.6 %collective-permute-start.6 = (bf16[8,64,384]{2,1,0:T(8,128)(2,1)S(1)}, bf16[8,64,384]{2,1,0:T(8,128)(2,1)}, u32[]{:S(2)}, u32[]{:S(2)}) collective-permute-start(bf16[8,64,384]{2,1,0:T(8,128)(2,1)S(1)} %all-to-all-done.1.u0), channel_id=1, source_target_pairs={{0,16},{16,32},{32,48},{48,0},{64,80},{80,96},{96,112},{112,64},{1... | collective-permute-start | bytes 1179656 | tf_op jit(solution)/shard_map/ppermute | solution.py:124
  70.1 14.0 %collective-permute-start.5 = (bf16[8,64,384]{2,1,0:T(8,128)(2,1)S(1)}, bf16[8,64,384]{2,1,0:T(8,128)(2,1)}, u32[]{:S(2)}, u32[]{:S(2)}) collective-permute-start(bf16[8,64,384]{2,1,0:T(8,128)(2,1)S(1)} %collective-permute-done.3.g1), channel_id=1, source_target_pairs={{0,16},{16,32},{32,48},{48,0},{64,80},{80,96},{96,112},{112,64},{1... | collective-permute-start | bytes 1179656 | tf_op jit(solution)/shard_map/ppermute | solution.py:124
  75.4 13.5 %copy-start.4 = (bf16[8,64,384]{2,1,0:T(8,128)(2,1)}, bf16[8,64,384]{2,1,0:T(8,128)(2,1)S(1)}, u32[]{:S(2)}) copy-start(bf16[8,64,384]{2,1,0:T(8,128)(2,1)S(1)} %collective-permute-done.7.u2) | copy-start | bytes 1179652
  75.4 13.5 %collective-permute-start.8 = (bf16[8,64,384]{2,1,0:T(8,128)(2,1)S(1)}, bf16[8,64,384]{2,1,0:T(8,128)(2,1)}, u32[]{:S(2)}, u32[]{:S(2)}) collective-permute-start(bf16[8,64,384]{2,1,0:T(8,128)(2,1)S(1)} %collective-permute-done.7.u2), channel_id=1, source_target_pairs={{0,48},{16,0},{32,16},{48,32},{64,112},{80,64},{96,80},{112,96},{1... | collective-permute-start | bytes 1179656 | tf_op jit(solution)/shard_map/ppermute | solution.py:124
  106.0 4.4 %collective-permute-start.9 = (bf16[8,384,128]{2,1,0:T(8,128)(2,1)}, bf16[8,384,128]{2,1,0:T(8,128)(2,1)S(1)}, u32[]{:S(2)}, u32[]{:S(2)}) collective-permute-start(bf16[8,384,128]{2,1,0:T(8,128)(2,1)} %get-tuple-element.26), channel_id=1, source_target_pairs={{0,1},{1,0},{2,3},{3,2},{4,5},{5,4},{6,7},{7,6},{8,9},{9,8},{10,11... | collective-permute-start | bytes 2359304 | tf_op jit(solution)/shard_map/ppermute | solution.py:129
  112.7 39.0 %all-to-all-start.3 = ((bf16[8,384,128]{2,1,0:T(8,128)(2,1)}), bf16[8,384,128]{2,1,0:T(8,128)(2,1)S(1)}, u32[]{:S(2)}, u32[]{:S(2)}) async-start(bf16[8,384,128]{2,1,0:T(8,128)(2,1)} %add_convert_fusion), calls=%async_computation.3 | async-start | bytes 1572864 | tf_op jit(solution)/shard_map/all_to_all | solution.py:198
  142.4 10.0 %collective-permute-start.10 = (bf16[64,384]{1,0:T(8,128)(2,1)S(1)}, bf16[64,384]{1,0:T(8,128)(2,1)S(1)}, u32[]{:S(2)}, u32[]{:S(2)}) collective-permute-start(bf16[64,384]{1,0:T(8,128)(2,1)S(1)} %get-tuple-element.28), channel_id=1, source_target_pairs={{0,16},{16,32},{32,48},{48,0},{64,80},{80,96},{96,112},{112,64},{1... | collective-permute-start | bytes 147464 | tf_op jit(solution)/shard_map/ppermute | solution.py:124
  144.9 7.5 %collective-permute-start.11 = (bf16[64,384]{1,0:T(8,128)(2,1)S(1)}, bf16[64,384]{1,0:T(8,128)(2,1)S(1)}, u32[]{:S(2)}, u32[]{:S(2)}) collective-permute-start(bf16[64,384]{1,0:T(8,128)(2,1)S(1)} %get-tuple-element.30), channel_id=1, source_target_pairs={{0,48},{16,0},{32,16},{48,32},{64,112},{80,64},{96,80},{112,96},{1... | collective-permute-start | bytes 147464 | tf_op jit(solution)/shard_map/ppermute | solution.py:124
  148.3 7.5 %collective-permute-start.12 = (bf16[64,384]{1,0:T(8,128)(2,1)S(1)}, bf16[64,384]{1,0:T(8,128)(2,1)S(1)}, u32[]{:S(2)}, u32[]{:S(2)}) collective-permute-start(bf16[64,384]{1,0:T(8,128)(2,1)S(1)} %get-tuple-element.29), channel_id=1, source_target_pairs={{0,32},{16,48},{32,0},{48,16},{64,96},{80,112},{96,64},{112,80},{1... | collective-permute-start | bytes 147464 | tf_op jit(solution)/shard_map/ppermute | solution.py:124
  (3 other events, 17.9 us)
Sparse Core Ops, SparseCore 0:
  10.6 52.2 all-gather.1
  96.8 44.7 reduce-scatter.1

commit v5 on v4

--- a/solution.py
+++ b/solution.py
@@ -33,33 +33,39 @@
     return copies
 
 
+def gate_kernel(place, rows_ref, g0, g1, g2, g3, gate_out, tok, gate_full, row_sem, gate_sems):
+    count, n_feat = tok.shape
+    tok_copy = pltpu.make_async_copy(rows_ref.at[pl.ds(0, count)], tok, row_sem.at[0])
+    tok_copy.start()
+    gate_copies = copy_blocks((g0, g1, g2, g3), gate_full, gate_sems, place[0])
+    tok_copy.wait()
+    for copy in gate_copies:
+        copy.wait()
+    gate_out[...] = jnp.dot(
+        tok[...], gate_full[...].reshape(n_feat, -1), preferred_element_type=jnp.float32
+    )
+
+
 def forward_kernel(
-    place, rows_ref, g0, g1, g2, g3, u0, u1, u2, u3, gate_out, up_out, partial_out,
-    tok, cot, gate_full, up_full, row_sems, gate_sems, up_sems,
+    place, rows_ref, u0, u1, u2, u3, gate_in, up_out, partial_out,
+    tok, cot, up_full, row_sems, up_sems,
 ):
-    me_x = place[0]
-    count = tok.shape[0]
+    count, n_feat = tok.shape
     tok_copy = pltpu.make_async_copy(rows_ref.at[pl.ds(0, count)], tok, row_sems.at[0])
     cot_copy = pltpu.make_async_copy(rows_ref.at[pl.ds(count, count)], cot, row_sems.at[1])
     tok_copy.start()
-    gate_copies = copy_blocks((g0, g1, g2, g3), gate_full, gate_sems, me_x)
-    up_copies = copy_blocks((u0, u1, u2, u3), up_full, up_sems, me_x)
+    up_copies = copy_blocks((u0, u1, u2, u3), up_full, up_sems, place[0])
     cot_copy.start()
-    n_feat, cols = partial_out.shape
+    gate_value = gate_in[...]
+    silu = gate_value * jax.nn.sigmoid(gate_value)
     tok_copy.wait()
-    for copy in gate_copies:
-        copy.wait()
-    gate_value = jnp.dot(
-        tok[...], gate_full[...].reshape(n_feat, cols), preferred_element_type=jnp.float32
-    )
-    gate_out[...] = gate_value
     for copy in up_copies:
         copy.wait()
     up_value = jnp.dot(
-        tok[...], up_full[...].reshape(n_feat, cols), preferred_element_type=jnp.float32
+        tok[...], up_full[...].reshape(n_feat, -1), preferred_element_type=jnp.float32
     )
     up_out[...] = up_value
-    hidden = (gate_value * jax.nn.sigmoid(gate_value) * up_value).astype(jnp.bfloat16)
+    hidden = (silu * up_value).astype(jnp.bfloat16)
     cot_copy.wait()
     partial_out[...] = dot(cot[...], hidden, ((0,), (0,))).astype(jnp.bfloat16)
 
@@ -124,6 +130,11 @@
     return lax.ppermute(value, "fsdp", pairs)
 
 
+def swap_x(value, flip):
+    pairs = [(z * N_X + x, z * N_X + (x ^ flip)) for z in range(N_Z) for x in range(N_X)]
+    return lax.ppermute(value, "fsdp", pairs)
+
+
 def send_core(value):
     pairs = [(i, i ^ 1) for i in range(N_Y * N_CORE)]
     return lax.ppermute(value, "mp", pairs)
@@ -165,7 +176,9 @@
     gate_left, gate_right = send_x(gate_z, 1), send_x(gate_z, -1)
     gate_z, up_copies = lax.optimization_barrier((gate_z, copies_of(up_weight)))
     up_z = gather_z(up_copies)
-    up_z, down_copies, gate_left = lax.optimization_barrier((up_z, copies_of(down_x), gate_left))
+    up_z, down_copies, gate_left, gate_right = lax.optimization_barrier(
+        (up_z, copies_of(down_x), gate_left, gate_right)
+    )
     down_full = gather_z(down_copies).reshape(N_Z, N_CORE, 2 * depth, cols)
 
     up_right, up_left = send_x(up_z, -1), send_x(up_z, 1)
@@ -177,13 +190,21 @@
     full = pltpu.VMEM((N_Z, N_CORE, 2 * depth, cols), jnp.bfloat16)
     row_block = pltpu.VMEM((rows, n_feat), jnp.bfloat16)
     sems = pltpu.SemaphoreType.DMA
-    gate_value, up_value, down_partial = call_kernel(
+    (gate_value,) = call_kernel(
+        gate_kernel,
+        5,
+        (place, both) + blocks[:4],
+        (value,),
+        [row_block, full, sems((1,)), sems((N_X,))],
+        2 * rows * n_feat * cols,
+    )
+    up_value, down_partial = call_kernel(
         forward_kernel,
-        9,
-        (place, both) + blocks,
-        (value, value, jax.ShapeDtypeStruct((n_feat, cols), jnp.bfloat16)),
-        [row_block, row_block, full, full, sems((2,)), sems((N_X,)), sems((N_X,))],
-        6 * rows * n_feat * cols,
+        5,
+        (place, both) + blocks[4:] + (gate_value,),
+        (value, jax.ShapeDtypeStruct((n_feat, cols), jnp.bfloat16)),
+        [row_block, row_block, full, sems((2,)), sems((N_X,))],
+        4 * rows * n_feat * cols,
     )
     half = jax.ShapeDtypeStruct((N_Y, rows, width), jnp.bfloat16)
     other, mine = call_kernel(
@@ -200,10 +221,10 @@
     down_z = lax.psum_scatter(
         down_partial, "fsdp", scatter_dimension=0, axis_index_groups=Z_GROUPS, tiled=True
     ).reshape(N_X, depth, cols)
-    down_sum = lax.dynamic_index_in_dim(down_z, me_x, 0, False).astype(jnp.float32)
-    for step in (1, N_X - 1, 2):
-        block = lax.dynamic_index_in_dim(down_z, (me_x + step) % N_X, 0, False)
-        down_sum = down_sum + send_x(block, step).astype(jnp.float32)
+    block = lambda flip: lax.dynamic_index_in_dim(down_z, me_x ^ flip, 0, False)
+    received = swap_x(jnp.stack([block(1), block(2)]), 1)
+    passed = swap_x(add(block(3), received[1]).astype(jnp.bfloat16), 3)
+    down_sum = add(block(0), received[0]) + passed.astype(jnp.float32)
     grad_down = (down_sum * factor).astype(jnp.bfloat16)
     input_grad = summed.astype(jnp.float32).sum(0).astype(jnp.bfloat16)
     return (input_grad, grad_down)

time: 166 us -> 164 us (0.988)
  waiting for transfers between devices: 59.3 us -> 55.4 us
  Pallas kernels: 14.3 us -> 17.7 us
  starting transfers between devices: 63.3 us -> 60.9 us
    ppermute x12 -> x9, waiting for transfers between devices: 26 us -> 15.3 us  [send_x(): return lax.ppermute(value, 'fsdp', pairs)]
    ppermute x12 -> x9, starting transfers between devices: 35.6 us -> 25.9 us  [send_x(): return lax.ppermute(value, 'fsdp', pairs)]
    ppermute x0 -> x2, waiting for transfers between devices: none -> 7.55 us  [swap_x(): return lax.ppermute(value, 'fsdp', pairs)]
    reduce_scatter x1, waiting for transfers between devices: 21.8 us -> 16.1 us  [on_device(): lax.psum_scatter(down_partial, 'fsdp', scatter_dimension=0, axis_index_gr...]
    ppermute x0 -> x2, starting transfers between devices: none -> 5.36 us  [swap_x(): return lax.ppermute(value, 'fsdp', pairs)]
    all_to_all x3, waiting for transfers between devices: 9.01 us -> 14 us  [gather_z(): return lax.all_to_all(copies, 'fsdp', 0, 0, axis_index_groups=Z_GROUPS)]
    pallas_call x2 -> x3, Pallas kernels: 14.3 us -> 17.7 us  [call_kernel(): pl.pallas_call(kernel, out_shape=out_shapes, in_specs=in_specs, out_specs...]
    all_to_all x3, starting transfers between devices: 18.6 us -> 20.6 us  [gather_z(): return lax.all_to_all(copies, 'fsdp', 0, 0, axis_index_groups=Z_GROUPS)]
  transfers between devices with their start and end apart: 19 -> 18, of which waited for: 11 -> 11; matrix products, arithmetic and copies ran while one was open for 4% -> 5% of each run, Pallas kernels for 9% -> 11%
where the time goes in v5:
time: 164 us; the launch traced here: 163 us
  starting transfers between devices  60.9 us (37%)
  waiting for transfers between devices  55.4 us (34%)
  Pallas kernels  17.7 us (11%)
  between operations  14.4 us (9%)
  other arithmetic  7.5 us (5%)
  local copies, waits for them, and re-layouts  6.84 us (4%)
    ppermute x9, starting transfers between devices, send_x(): return lax.ppermute(value, 'fsdp', pairs)  25.9 us
    all_to_all x3, starting transfers between devices, gather_z(): return lax.all_to_all(copies, 'fsdp', 0, 0, axis_index_groups=Z_GROUPS)  20.6 us
    pallas_call x3, Pallas kernels, call_kernel(): pl.pallas_call(kernel, out_shape=out_shapes, in_specs=in_specs, out_specs...  17.7 us
    reduce_scatter x1, waiting for transfers between devices, on_device(): lax.psum_scatter(down_partial, 'fsdp', scatter_dimension=0, axis_index_gr...  16.1 us
    ppermute x9, waiting for transfers between devices, send_x(): return lax.ppermute(value, 'fsdp', pairs)  15.3 us
    all_to_all x3, waiting for transfers between devices, gather_z(): return lax.all_to_all(copies, 'fsdp', 0, 0, axis_index_groups=Z_GROUPS)  14 us
    ppermute x2, waiting for transfers between devices, swap_x(): return lax.ppermute(value, 'fsdp', pairs)  7.55 us
    all_to_all x1, starting transfers between devices, on_device(): summed = lax.all_to_all(pair_sum, 'mp', 0, 0, axis_index_groups=Y_GROUPS)  7.05 us
  transfers between devices with their start and end apart: 18, of which 11 were waited for; matrix products, arithmetic and copies ran while one was open for 5% of the time, Pallas kernels for 11%

profile of v5, /device:TPU:6, one launch (start us, length us, event | category | flops | bytes accessed | tf_op | source)
XLA Modules:
  0.0 162.7 jit_solution(9090135113937010407)
XLA Ops:
  10.5 10.3 %all-to-all-start = ((bf16[8,64,384]{2,1,0:T(8,128)(2,1)}), bf16[8,64,384]{2,1,0:T(8,128)(2,1)S(1)}, u32[]{:S(2)}, u32[]{:S(2)}) async-start(bf16[8,64,384]{2,1,0:T(8,128)(2,1)} %broadcast_in_dim.16), calls=%async_computation | async-start | bytes 786432 | tf_op jit(solution)/shard_map/all_to_all | solution.py:148
  23.2 3.5 %collective-permute-start.1 = (bf16[64,384]{1,0:T(8,128)(2,1)S(1)}, bf16[64,384]{1,0:T(8,128)(2,1)S(1)}, u32[]{:S(2)}, u32[]{:S(2)}) collective-permute-start(bf16[64,384]{1,0:T(8,128)(2,1)S(1)} %copy-done.9), channel_id=1, source_target_pairs={{0,48},{16,0},{32,16},{48,32},{64,112},{80,64},{96,80},{112,96},{1... | collective-permute-start | bytes 147464 | tf_op jit(solution)/shard_map/ppermute | solution.py:130
  26.7 3.3 %collective-permute-start.2 = (bf16[64,384]{1,0:T(8,128)(2,1)S(1)}, bf16[64,384]{1,0:T(8,128)(2,1)S(1)}, u32[]{:S(2)}, u32[]{:S(2)}) collective-permute-start(bf16[64,384]{1,0:T(8,128)(2,1)S(1)} %copy-done.9), channel_id=1, source_target_pairs={{0,32},{16,48},{32,0},{48,16},{64,96},{80,112},{96,64},{112,80},{1... | collective-permute-start | bytes 147464 | tf_op jit(solution)/shard_map/ppermute | solution.py:130
  30.0 5.5 %all-to-all-done.g0 = bf16[8,64,384]{2,1,0:T(8,128)(2,1)S(1)} async-done(((bf16[8,64,384]{2,1,0:T(8,128)(2,1)}), bf16[8,64,384]{2,1,0:T(8,128)(2,1)S(1)}, u32[]{:S(2)}, u32[]{:S(2)}) %all-to-all-start) | async-done | bytes 393248 | tf_op jit(solution)/shard_map/all_to_all | solution.py:148
  36.3 3.5 %all-to-all-start.1 = ((bf16[8,64,384]{2,1,0:T(8,128)(2,1)}), bf16[8,64,384]{2,1,0:T(8,128)(2,1)S(1)}, u32[]{:S(2)}, u32[]{:S(2)}) async-start(bf16[8,64,384]{2,1,0:T(8,128)(2,1)} %broadcast_in_dim.34), calls=%async_computation.1 | async-start | bytes 786432 | tf_op jit(solution)/shard_map/all_to_all | solution.py:148
  39.9 2.4 %collective-permute-start.3 = (bf16[8,64,384]{2,1,0:T(8,128)(2,1)S(1)}, bf16[8,64,384]{2,1,0:T(8,128)(2,1)S(1)}, u32[]{:S(2)}, u32[]{:S(2)}) collective-permute-start(bf16[8,64,384]{2,1,0:T(8,128)(2,1)S(1)} %all-to-all-done.g0), channel_id=1, source_target_pairs={{0,16},{16,32},{32,48},{48,0},{64,80},{80,96},{96,112},{112,64},{1... | collective-permute-start | bytes 1179656 | tf_op jit(solution)/shard_map/ppermute | solution.py:130
  42.3 3.4 %collective-permute-start.4 = (bf16[8,64,384]{2,1,0:T(8,128)(2,1)S(1)}, bf16[8,64,384]{2,1,0:T(8,128)(2,1)S(1)}, u32[]{:S(2)}, u32[]{:S(2)}) collective-permute-start(bf16[8,64,384]{2,1,0:T(8,128)(2,1)S(1)} %all-to-all-done.g0), channel_id=1, source_target_pairs={{0,48},{16,0},{32,16},{48,32},{64,112},{80,64},{96,80},{112,96},{1... | collective-permute-start | bytes 1179656 | tf_op jit(solution)/shard_map/ppermute | solution.py:130
  45.9 6.1 %collective-permute-done.3.g1 = bf16[8,64,384]{2,1,0:T(8,128)(2,1)S(1)} collective-permute-done((bf16[8,64,384]{2,1,0:T(8,128)(2,1)S(1)}, bf16[8,64,384]{2,1,0:T(8,128)(2,1)S(1)}, u32[]{:S(2)}, u32[]{:S(2)}) %collective-permute-start.3) | collective-permute-done | bytes 393248 | tf_op jit(solution)/shard_map/ppermute | solution.py:130
  51.9 3.4 %collective-permute-done.4.g2 = bf16[8,64,384]{2,1,0:T(8,128)(2,1)S(1)} collective-permute-done((bf16[8,64,384]{2,1,0:T(8,128)(2,1)S(1)}, bf16[8,64,384]{2,1,0:T(8,128)(2,1)S(1)}, u32[]{:S(2)}, u32[]{:S(2)}) %collective-permute-start.4) | collective-permute-done | bytes 393248 | tf_op jit(solution)/shard_map/ppermute | solution.py:130
  56.8 6.8 %all-to-all-start.2 = ((bf16[8,4,64,384]{3,2,1,0:T(8,128)(2,1)}), bf16[8,4,64,384]{3,2,1,0:T(8,128)(2,1)S(1)}, u32[]{:S(2)}, u32[]{:S(2)}) async-start(bf16[8,4,64,384]{3,2,1,0:T(8,128)(2,1)} %broadcast_in_dim.40), calls=%async_computation.2 | async-start | bytes 3145728 | tf_op jit(solution)/shard_map/all_to_all | solution.py:148
  65.9 4.8 %collective-permute-start.5 = (bf16[8,64,384]{2,1,0:T(8,128)(2,1)S(1)}, bf16[8,64,384]{2,1,0:T(8,128)(2,1)S(1)}, u32[]{:S(2)}, u32[]{:S(2)}) collective-permute-start(bf16[8,64,384]{2,1,0:T(8,128)(2,1)S(1)} %collective-permute-done.3.g1), channel_id=1, source_target_pairs={{0,16},{16,32},{32,48},{48,0},{64,80},{80,96},{96,112},{112,64},{1... | collective-permute-start | bytes 1179656 | tf_op jit(solution)/shard_map/ppermute | solution.py:130
  72.7 2.5 %collective-permute-done.7.u2 = bf16[8,64,384]{2,1,0:T(8,128)(2,1)S(1)} collective-permute-done((bf16[8,64,384]{2,1,0:T(8,128)(2,1)S(1)}, bf16[8,64,384]{2,1,0:T(8,128)(2,1)S(1)}, u32[]{:S(2)}, u32[]{:S(2)}) %collective-permute-start.7) | collective-permute-done | bytes 393248 | tf_op jit(solution)/shard_map/ppermute | solution.py:130
  77.8 2.5 %collective-permute-done.5.g3 = bf16[8,64,384]{2,1,0:T(8,128)(2,1)S(1)} collective-permute-done((bf16[8,64,384]{2,1,0:T(8,128)(2,1)S(1)}, bf16[8,64,384]{2,1,0:T(8,128)(2,1)S(1)}, u32[]{:S(2)}, u32[]{:S(2)}) %collective-permute-start.5) | collective-permute-done | bytes 393248 | tf_op jit(solution)/shard_map/ppermute | solution.py:130
  81.0 4.4 %shard_map.68.gate_in = f32[384,384]{1,0:T(8,128)} custom-call(s32[2]{0:T(128)} %pad_add_fusion.place, bf16[768,2048]{1,0:T(8,128)(2,1)} %all-gather.2.cloned.1.call-done.rows_ref, bf16[8,64,384]{2,1,0:T(8,128)(2,1)} %copy-done.1, bf16[8,64,384]{2,1,0:T(8,128)(2,1)} %copy-done.3, bf16[8,64,384]{2,1,0:T(8,128)(2,1)} %copy-done.4, bf16[8,64,384]{2,1,0:T(8,128)(2,1)} %copy-done.6), custom_call_target="tpu_custom_call" | custom-call | flops 603979776 | bytes 10000000 | tf_op jit(solution)/shard_map/pallas_call | solution.py:115
  86.2 6.7 %shard_map.69 = (f32[384,384]{1,0:T(8,128)}, bf16[2048,384]{1,0:T(8,128)(2,1)}) custom-call(s32[2]{0:T(128)} %pad_add_fusion.place, bf16[768,2048]{1,0:T(8,128)(2,1)} %all-gather.2.cloned.1.call-done.rows_ref, bf16[8,64,384]{2,1,0:T(8,128)(2,1)} %copy-done.2, bf16[8,64,384]{2,1,0:T(8,128)(2,1)} %copy-done.7, bf16[8,64,384]{2,1,0:T(8,128)(2,1)} %copy-done.5, ...), custom_call_target="tpu_custom_call" | custom-call | flops 1207959552 | bytes 10000000 | tf_op jit(solution)/shard_map/pallas_call | solution.py:115
  93.0 8.5 %all-to-all-done.2 = bf16[8,4,64,384]{3,2,1,0:T(8,128)(2,1)S(1)} async-done(((bf16[8,4,64,384]{3,2,1,0:T(8,128)(2,1)}), bf16[8,4,64,384]{3,2,1,0:T(8,128)(2,1)S(1)}, u32[]{:S(2)}, u32[]{:S(2)}) %all-to-all-start.2) | async-done | bytes 1572896 | tf_op jit(solution)/shard_map/all_to_all | solution.py:148
  102.7 6.6 %shard_map.70 = (bf16[8,384,128]{2,1,0:T(8,128)(2,1)}, bf16[8,384,128]{2,1,0:T(8,128)(2,1)}) custom-call(s32[2]{0:T(128)} %pad_add_fusion.place, bf16[768,2048]{1,0:T(8,128)(2,1)} %all-gather.2.cloned.1.call-done.rows_ref, bf16[8,2,128,384]{3,2,1,0:T(8,128)(2,1)} %bitcast.20, bf16[8,64,384]{2,1,0:T(8,128)(2,1)} %copy-done.1, bf16[8,64,384]{2,1,0:T(8,128)(2,1)} %copy-done.3, ...), custom_call_target="tpu_custom_call" | custom-call | flops 1811939328 | bytes 10000000 | tf_op jit(solution)/shard_map/pallas_call | solution.py:115
  111.2 2.5 %collective-permute-done.9 = bf16[8,384,128]{2,1,0:T(8,128)(2,1)S(1)} collective-permute-done((bf16[8,384,128]{2,1,0:T(8,128)(2,1)}, bf16[8,384,128]{2,1,0:T(8,128)(2,1)S(1)}, u32[]{:S(2)}, u32[]{:S(2)}) %collective-permute-start.9) | collective-permute-done | bytes 786464 | tf_op jit(solution)/shard_map/ppermute | solution.py:140
  116.0 7.0 %all-to-all-start.3 = ((bf16[8,384,128]{2,1,0:T(8,128)(2,1)}), bf16[8,384,128]{2,1,0:T(8,128)(2,1)S(1)}, u32[]{:S(2)}, u32[]{:S(2)}) async-start(bf16[8,384,128]{2,1,0:T(8,128)(2,1)} %add_convert_fusion), calls=%async_computation.3 | async-start | bytes 1572864 | tf_op jit(solution)/shard_map/all_to_all | solution.py:219
  123.0 16.1 %reduce-scatter.2.cloned.1.call-done = bf16[256,384]{1,0:T(8,128)(2,1)} async-done(((bf16[2048,384]{1,0:T(8,128)(2,1)}), bf16[256,384]{1,0:T(8,128)(2,1)}) %reduce-scatter.2.cloned.1.call-update) | async-done | bytes 196624 | tf_op jit(solution)/shard_map/reduce_scatter | solution.py:221
  139.9 2.8 %collective-permute-start.10 = (bf16[2,64,384]{2,1,0:T(8,128)(2,1)S(1)}, bf16[2,64,384]{2,1,0:T(8,128)(2,1)S(1)}, u32[]{:S(2)}, u32[]{:S(2)}) collective-permute-start(bf16[2,64,384]{2,1,0:T(8,128)(2,1)S(1)} %pad_maximum_fusion.1), channel_id=1, source_target_pairs={{0,16},{16,0},{32,48},{48,32},{64,80},{80,64},{96,112},{112,96},{1... | collective-permute-start | bytes 294920 | tf_op jit(solution)/shard_map/ppermute | solution.py:135
  142.8 3.7 %collective-permute-done.10 = bf16[2,64,384]{2,1,0:T(8,128)(2,1)S(1)} collective-permute-done((bf16[2,64,384]{2,1,0:T(8,128)(2,1)S(1)}, bf16[2,64,384]{2,1,0:T(8,128)(2,1)S(1)}, u32[]{:S(2)}, u32[]{:S(2)}) %collective-permute-start.10) | collective-permute-done | bytes 98336 | tf_op jit(solution)/shard_map/ppermute | solution.py:135
  147.3 2.5 %collective-permute-start.11 = (bf16[64,384]{1,0:T(8,128)(2,1)S(1)}, bf16[64,384]{1,0:T(8,128)(2,1)S(1)}, u32[]{:S(2)}, u32[]{:S(2)}) collective-permute-start(bf16[64,384]{1,0:T(8,128)(2,1)S(1)} %fusion.2), channel_id=1, source_target_pairs={{0,48},{16,32},{32,16},{48,0},{64,112},{80,96},{96,80},{112,64},{1... | collective-permute-start | bytes 147464 | tf_op jit(solution)/shard_map/ppermute | solution.py:135
  150.6 3.9 %collective-permute-done.11 = bf16[64,384]{1,0:T(8,128)(2,1)S(1)} collective-permute-done((bf16[64,384]{1,0:T(8,128)(2,1)S(1)}, bf16[64,384]{1,0:T(8,128)(2,1)S(1)}, u32[]{:S(2)}, u32[]{:S(2)}) %collective-permute-start.11) | collective-permute-done | bytes 49184 | tf_op jit(solution)/shard_map/ppermute | solution.py:135
  (53 shorter events, 25.6 us)
Async XLA Ops:
  7.2 13.6 %copy-start.9 = (bf16[64,384]{1,0:T(8,128)(2,1)S(1)}, bf16[64,384]{1,0:T(8,128)(2,1)}, u32[]{:S(2)}) copy-start(bf16[64,384]{1,0:T(8,128)(2,1)} %param.9) | copy-start | bytes 147460
  7.2 28.3 %copy-start.8 = (bf16[64,384]{1,0:T(8,128)(2,1)S(1)}, bf16[64,384]{1,0:T(8,128)(2,1)}, u32[]{:S(2)}) copy-start(bf16[64,384]{1,0:T(8,128)(2,1)} %param.8) | copy-start | bytes 147460
  7.2 73.1 %all-gather.2.cloned.1.call-start = ((), (), s32[]{:S(2)}) async-start(), calls=%async_computation.5 | async-start | bytes 3342336 | tf_op jit(solution)/shard_map/all_gather | solution.py:167
  10.5 25.0 %all-to-all-start = ((bf16[8,64,384]{2,1,0:T(8,128)(2,1)}), bf16[8,64,384]{2,1,0:T(8,128)(2,1)S(1)}, u32[]{:S(2)}, u32[]{:S(2)}) async-start(bf16[8,64,384]{2,1,0:T(8,128)(2,1)} %broadcast_in_dim.16), calls=%async_computation | async-start | bytes 786432 | tf_op jit(solution)/shard_map/all_to_all | solution.py:148
  20.8 19.1 %collective-permute-start = (bf16[64,384]{1,0:T(8,128)(2,1)S(1)}, bf16[64,384]{1,0:T(8,128)(2,1)S(1)}, u32[]{:S(2)}, u32[]{:S(2)}) collective-permute-start(bf16[64,384]{1,0:T(8,128)(2,1)S(1)} %copy-done.9), channel_id=1, source_target_pairs={{0,16},{16,32},{32,48},{48,0},{64,80},{80,96},{96,112},{112,64},{1... | collective-permute-start | bytes 147464 | tf_op jit(solution)/shard_map/ppermute | solution.py:130
  23.2 22.6 %collective-permute-start.1 = (bf16[64,384]{1,0:T(8,128)(2,1)S(1)}, bf16[64,384]{1,0:T(8,128)(2,1)S(1)}, u32[]{:S(2)}, u32[]{:S(2)}) collective-permute-start(bf16[64,384]{1,0:T(8,128)(2,1)S(1)} %copy-done.9), channel_id=1, source_target_pairs={{0,48},{16,0},{32,16},{48,32},{64,112},{80,64},{96,80},{112,96},{1... | collective-permute-start | bytes 147464 | tf_op jit(solution)/shard_map/ppermute | solution.py:130
  26.7 19.2 %collective-permute-start.2 = (bf16[64,384]{1,0:T(8,128)(2,1)S(1)}, bf16[64,384]{1,0:T(8,128)(2,1)S(1)}, u32[]{:S(2)}, u32[]{:S(2)}) collective-permute-start(bf16[64,384]{1,0:T(8,128)(2,1)S(1)} %copy-done.9), channel_id=1, source_target_pairs={{0,32},{16,48},{32,0},{48,16},{64,96},{80,112},{96,64},{112,80},{1... | collective-permute-start | bytes 147464 | tf_op jit(solution)/shard_map/ppermute | solution.py:130
  35.5 21.3 %copy-start.1 = (bf16[8,64,384]{2,1,0:T(8,128)(2,1)}, bf16[8,64,384]{2,1,0:T(8,128)(2,1)S(1)}, u32[]{:S(2)}) copy-start(bf16[8,64,384]{2,1,0:T(8,128)(2,1)S(1)} %all-to-all-done.g0) | copy-start | bytes 1179652
  36.3 19.0 %all-to-all-start.1 = ((bf16[8,64,384]{2,1,0:T(8,128)(2,1)}), bf16[8,64,384]{2,1,0:T(8,128)(2,1)S(1)}, u32[]{:S(2)}, u32[]{:S(2)}) async-start(bf16[8,64,384]{2,1,0:T(8,128)(2,1)} %broadcast_in_dim.34), calls=%async_computation.1 | async-start | bytes 786432 | tf_op jit(solution)/shard_map/all_to_all | solution.py:148
  39.9 12.0 %collective-permute-start.3 = (bf16[8,64,384]{2,1,0:T(8,128)(2,1)S(1)}, bf16[8,64,384]{2,1,0:T(8,128)(2,1)S(1)}, u32[]{:S(2)}, u32[]{:S(2)}) collective-permute-start(bf16[8,64,384]{2,1,0:T(8,128)(2,1)S(1)} %all-to-all-done.g0), channel_id=1, source_target_pairs={{0,16},{16,32},{32,48},{48,0},{64,80},{80,96},{96,112},{112,64},{1... | collective-permute-start | bytes 1179656 | tf_op jit(solution)/shard_map/ppermute | solution.py:130
  42.3 12.9 %collective-permute-start.4 = (bf16[8,64,384]{2,1,0:T(8,128)(2,1)S(1)}, bf16[8,64,384]{2,1,0:T(8,128)(2,1)S(1)}, u32[]{:S(2)}, u32[]{:S(2)}) collective-permute-start(bf16[8,64,384]{2,1,0:T(8,128)(2,1)S(1)} %all-to-all-done.g0), channel_id=1, source_target_pairs={{0,48},{16,0},{32,16},{48,32},{64,112},{80,64},{96,80},{112,96},{1... | collective-permute-start | bytes 1179656 | tf_op jit(solution)/shard_map/ppermute | solution.py:130
  51.9 14.0 %copy-start.3 = (bf16[8,64,384]{2,1,0:T(8,128)(2,1)}, bf16[8,64,384]{2,1,0:T(8,128)(2,1)S(1)}, u32[]{:S(2)}) copy-start(bf16[8,64,384]{2,1,0:T(8,128)(2,1)S(1)} %collective-permute-done.3.g1) | copy-start | bytes 1179652
  55.3 15.5 %copy-start.2 = (bf16[8,64,384]{2,1,0:T(8,128)(2,1)}, bf16[8,64,384]{2,1,0:T(8,128)(2,1)S(1)}, u32[]{:S(2)}) copy-start(bf16[8,64,384]{2,1,0:T(8,128)(2,1)S(1)} %all-to-all-done.1.u0) | copy-start | bytes 1179652
  56.8 44.7 %all-to-all-start.2 = ((bf16[8,4,64,384]{3,2,1,0:T(8,128)(2,1)}), bf16[8,4,64,384]{3,2,1,0:T(8,128)(2,1)S(1)}, u32[]{:S(2)}, u32[]{:S(2)}) async-start(bf16[8,4,64,384]{3,2,1,0:T(8,128)(2,1)} %broadcast_in_dim.40), calls=%async_computation.2 | async-start | bytes 3145728 | tf_op jit(solution)/shard_map/all_to_all | solution.py:148
  63.6 75.5 %reduce-scatter.2.cloned.1.call-start = ((), (), s32[]{:S(2)}) async-start(), calls=%async_computation.6 | async-start | bytes 1769472 | tf_op jit(solution)/shard_map/reduce_scatter | solution.py:221
  63.7 11.6 %collective-permute-start.7 = (bf16[8,64,384]{2,1,0:T(8,128)(2,1)S(1)}, bf16[8,64,384]{2,1,0:T(8,128)(2,1)S(1)}, u32[]{:S(2)}, u32[]{:S(2)}) collective-permute-start(bf16[8,64,384]{2,1,0:T(8,128)(2,1)S(1)} %all-to-all-done.1.u0), channel_id=1, source_target_pairs={{0,48},{16,0},{32,16},{48,32},{64,112},{80,64},{96,80},{112,96},{1... | collective-permute-start | bytes 1179656 | tf_op jit(solution)/shard_map/ppermute | solution.py:130
  65.9 14.4 %collective-permute-start.5 = (bf16[8,64,384]{2,1,0:T(8,128)(2,1)S(1)}, bf16[8,64,384]{2,1,0:T(8,128)(2,1)S(1)}, u32[]{:S(2)}, u32[]{:S(2)}) collective-permute-start(bf16[8,64,384]{2,1,0:T(8,128)(2,1)S(1)} %collective-permute-done.3.g1), channel_id=1, source_target_pairs={{0,16},{16,32},{32,48},{48,0},{64,80},{80,96},{96,112},{112,64},{1... | collective-permute-start | bytes 1179656 | tf_op jit(solution)/shard_map/ppermute | solution.py:130
  70.8 14.7 %collective-permute-start.6 = (bf16[8,64,384]{2,1,0:T(8,128)(2,1)S(1)}, bf16[8,64,384]{2,1,0:T(8,128)(2,1)S(1)}, u32[]{:S(2)}, u32[]{:S(2)}) collective-permute-start(bf16[8,64,384]{2,1,0:T(8,128)(2,1)S(1)} %all-to-all-done.1.u0), channel_id=1, source_target_pairs={{0,16},{16,32},{32,48},{48,0},{64,80},{80,96},{96,112},{112,64},{1... | collective-permute-start | bytes 1179656 | tf_op jit(solution)/shard_map/ppermute | solution.py:130
  75.2 10.2 %copy-start.5 = (bf16[8,64,384]{2,1,0:T(8,128)(2,1)}, bf16[8,64,384]{2,1,0:T(8,128)(2,1)S(1)}, u32[]{:S(2)}) copy-start(bf16[8,64,384]{2,1,0:T(8,128)(2,1)S(1)} %collective-permute-done.7.u2) | copy-start | bytes 1179652
  75.2 11.0 %collective-permute-start.8 = (bf16[8,64,384]{2,1,0:T(8,128)(2,1)S(1)}, bf16[8,64,384]{2,1,0:T(8,128)(2,1)}, u32[]{:S(2)}, u32[]{:S(2)}) collective-permute-start(bf16[8,64,384]{2,1,0:T(8,128)(2,1)S(1)} %collective-permute-done.7.u2), channel_id=1, source_target_pairs={{0,48},{16,0},{32,16},{48,32},{64,112},{80,64},{96,80},{112,96},{1... | collective-permute-start | bytes 1179656 | tf_op jit(solution)/shard_map/ppermute | solution.py:130
  109.3 4.4 %collective-permute-start.9 = (bf16[8,384,128]{2,1,0:T(8,128)(2,1)}, bf16[8,384,128]{2,1,0:T(8,128)(2,1)S(1)}, u32[]{:S(2)}, u32[]{:S(2)}) collective-permute-start(bf16[8,384,128]{2,1,0:T(8,128)(2,1)} %get-tuple-element.26), channel_id=1, source_target_pairs={{0,1},{1,0},{2,3},{3,2},{4,5},{5,4},{6,7},{7,6},{8,9},{9,8},{10,11... | collective-permute-start | bytes 2359304 | tf_op jit(solution)/shard_map/ppermute | solution.py:140
  116.0 33.9 %all-to-all-start.3 = ((bf16[8,384,128]{2,1,0:T(8,128)(2,1)}), bf16[8,384,128]{2,1,0:T(8,128)(2,1)S(1)}, u32[]{:S(2)}, u32[]{:S(2)}) async-start(bf16[8,384,128]{2,1,0:T(8,128)(2,1)} %add_convert_fusion), calls=%async_computation.3 | async-start | bytes 1572864 | tf_op jit(solution)/shard_map/all_to_all | solution.py:219
  139.9 6.5 %collective-permute-start.10 = (bf16[2,64,384]{2,1,0:T(8,128)(2,1)S(1)}, bf16[2,64,384]{2,1,0:T(8,128)(2,1)S(1)}, u32[]{:S(2)}, u32[]{:S(2)}) collective-permute-start(bf16[2,64,384]{2,1,0:T(8,128)(2,1)S(1)} %pad_maximum_fusion.1), channel_id=1, source_target_pairs={{0,16},{16,0},{32,48},{48,32},{64,80},{80,64},{96,112},{112,96},{1... | collective-permute-start | bytes 294920 | tf_op jit(solution)/shard_map/ppermute | solution.py:135
  147.3 7.2 %collective-permute-start.11 = (bf16[64,384]{1,0:T(8,128)(2,1)S(1)}, bf16[64,384]{1,0:T(8,128)(2,1)S(1)}, u32[]{:S(2)}, u32[]{:S(2)}) collective-permute-start(bf16[64,384]{1,0:T(8,128)(2,1)S(1)} %fusion.2), channel_id=1, source_target_pairs={{0,48},{16,32},{32,16},{48,0},{64,112},{80,96},{96,80},{112,64},{1... | collective-permute-start | bytes 147464 | tf_op jit(solution)/shard_map/ppermute | solution.py:135
  (4 other events, 4.2 us)
Sparse Core Ops, SparseCore 0:
  10.6 52.2 all-gather.1
  93.1 45.9 reduce-scatter.1

commit v6 on v5

--- a/solution.py
+++ b/solution.py
@@ -12,7 +12,6 @@
 N_Y = 8
 N_CORE = 2
 Z_GROUPS = [[z * N_X + x for z in range(N_Z)] for x in range(N_X)]
-X_GROUPS = [[z * N_X + x for x in range(N_X)] for z in range(N_Z)]
 Y_GROUPS = [[y * N_CORE + c for y in range(N_Y)] for c in range(N_CORE)]
 
 
@@ -130,11 +129,6 @@
     return lax.ppermute(value, "fsdp", pairs)
 
 
-def swap_x(value, flip):
-    pairs = [(z * N_X + x, z * N_X + (x ^ flip)) for z in range(N_Z) for x in range(N_X)]
-    return lax.ppermute(value, "fsdp", pairs)
-
-
 def send_core(value):
     pairs = [(i, i ^ 1) for i in range(N_Y * N_CORE)]
     return lax.ppermute(value, "mp", pairs)
@@ -216,17 +210,15 @@
         6 * rows * n_feat * cols,
     )
     pair_sum = add(mine, send_core(other)).astype(jnp.bfloat16)
-    summed = lax.all_to_all(pair_sum, "mp", 0, 0, axis_index_groups=Y_GROUPS)
-
-    down_z = lax.psum_scatter(
-        down_partial, "fsdp", scatter_dimension=0, axis_index_groups=Z_GROUPS, tiled=True
-    ).reshape(N_X, depth, cols)
-    block = lambda flip: lax.dynamic_index_in_dim(down_z, me_x ^ flip, 0, False)
-    received = swap_x(jnp.stack([block(1), block(2)]), 1)
-    passed = swap_x(add(block(3), received[1]).astype(jnp.bfloat16), 3)
-    down_sum = add(block(0), received[0]) + passed.astype(jnp.float32)
-    grad_down = (down_sum * factor).astype(jnp.bfloat16)
-    input_grad = summed.astype(jnp.float32).sum(0).astype(jnp.bfloat16)
+    input_grad = lax.psum_scatter(
+        pair_sum.reshape(N_Y * rows, width),
+        "mp",
+        scatter_dimension=0,
+        axis_index_groups=Y_GROUPS,
+        tiled=True,
+    )
+    down_blocks = lax.all_to_all(down_partial.reshape(n_fsdp, depth, cols), "fsdp", 0, 0)
+    grad_down = (down_blocks.astype(jnp.float32).sum(0) * factor).astype(jnp.bfloat16)
     return (input_grad, grad_down)
 
 

time: 164 us -> 171 us (1.043)
  waiting for transfers between devices: 55.4 us -> 68.3 us
  starting transfers between devices: 60.9 us -> 58.7 us
  other arithmetic: 7.5 us -> 5.39 us
    all_to_all x1, waiting for transfers between devices: 0.01 us -> 24 us  [on_device(): lax.all_to_all(down_partial.reshape(n_fsdp, depth, cols), 'fsdp', 0, 0)]
    ppermute x2 -> x0, waiting for transfers between devices: 7.55 us -> none  [swap_x(): return lax.ppermute(value, 'fsdp', pairs)]
    ppermute x2 -> x0, starting transfers between devices: 5.36 us -> none  [swap_x(): return lax.ppermute(value, 'fsdp', pairs)]
    ppermute x9, waiting for transfers between devices: 15.3 us -> 11.2 us  [send_x(): return lax.ppermute(value, 'fsdp', pairs)]
    ppermute x9, starting transfers between devices: 25.9 us -> 29 us  [send_x(): return lax.ppermute(value, 'fsdp', pairs)]
  transfers between devices with their start and end apart: 18 -> 16, of which waited for: 11 -> 10; matrix products, arithmetic and copies ran while one was open for 5% -> 4% of each run, Pallas kernels for 11% -> 10%
where the time goes in v6:
time: 171 us
  waiting for transfers between devices  68.3 us (40%)
  starting transfers between devices  58.7 us (34%)
  Pallas kernels  17.7 us (10%)
  between operations  14.4 us (8%)
  local copies, waits for them, and re-layouts  6.02 us (4%)
  other arithmetic  5.39 us (3%)
    ppermute x9, starting transfers between devices, send_x(): return lax.ppermute(value, 'fsdp', pairs)  29 us
    all_to_all x1, waiting for transfers between devices, on_device(): lax.all_to_all(down_partial.reshape(n_fsdp, depth, cols), 'fsdp', 0, 0)  24 us
    all_to_all x3, starting transfers between devices, gather_z(): return lax.all_to_all(copies, 'fsdp', 0, 0, axis_index_groups=Z_GROUPS)  20.6 us
    pallas_call x3, Pallas kernels, call_kernel(): pl.pallas_call(kernel, out_shape=out_shapes, in_specs=in_specs, out_specs...  17.7 us
    reduce_scatter x1, waiting for transfers between devices, on_device(): lax.psum_scatter(pair_sum.reshape(N_Y * rows, width), 'mp', scatter_dimen...  16.5 us
    all_to_all x3, waiting for transfers between devices, gather_z(): return lax.all_to_all(copies, 'fsdp', 0, 0, axis_index_groups=Z_GROUPS)  14 us
    ppermute x9, waiting for transfers between devices, send_x(): return lax.ppermute(value, 'fsdp', pairs)  11.2 us
    all_to_all x1, starting transfers between devices, on_device(): lax.all_to_all(down_partial.reshape(n_fsdp, depth, cols), 'fsdp', 0, 0)  7.15 us
  transfers between devices with their start and end apart: 16, of which 10 were waited for; matrix products, arithmetic and copies ran while one was open for 4% of the time, Pallas kernels for 10%

profile of v6, /device:TPU:6, one launch (start us, length us, event | category | flops | bytes accessed | tf_op | source)
XLA Modules:
  0.0 170.5 jit_solution(15139844653728217667)
XLA Ops:
  10.5 10.3 %all-to-all-start = ((bf16[8,64,384]{2,1,0:T(8,128)(2,1)}), bf16[8,64,384]{2,1,0:T(8,128)(2,1)S(1)}, u32[]{:S(2)}, u32[]{:S(2)}) async-start(bf16[8,64,384]{2,1,0:T(8,128)(2,1)} %broadcast_in_dim.16), calls=%async_computation | async-start | bytes 786432 | tf_op jit(solution)/shard_map/all_to_all | solution.py:142
  20.8 2.4 %collective-permute-start = (bf16[64,384]{1,0:T(8,128)(2,1)S(1)}, bf16[64,384]{1,0:T(8,128)(2,1)S(1)}, u32[]{:S(2)}, u32[]{:S(2)}) collective-permute-start(bf16[64,384]{1,0:T(8,128)(2,1)S(1)} %copy-done.9), channel_id=1, source_target_pairs={{0,16},{16,32},{32,48},{48,0},{64,80},{80,96},{96,112},{112,64},{1... | collective-permute-start | bytes 147464 | tf_op jit(solution)/shard_map/ppermute | solution.py:129
  23.2 4.3 %collective-permute-start.2 = (bf16[64,384]{1,0:T(8,128)(2,1)S(1)}, bf16[64,384]{1,0:T(8,128)(2,1)S(1)}, u32[]{:S(2)}, u32[]{:S(2)}) collective-permute-start(bf16[64,384]{1,0:T(8,128)(2,1)S(1)} %copy-done.9), channel_id=1, source_target_pairs={{0,32},{16,48},{32,0},{48,16},{64,96},{80,112},{96,64},{112,80},{1... | collective-permute-start | bytes 147464 | tf_op jit(solution)/shard_map/ppermute | solution.py:129
  27.5 1.9 %collective-permute-start.1 = (bf16[64,384]{1,0:T(8,128)(2,1)S(1)}, bf16[64,384]{1,0:T(8,128)(2,1)S(1)}, u32[]{:S(2)}, u32[]{:S(2)}) collective-permute-start(bf16[64,384]{1,0:T(8,128)(2,1)S(1)} %copy-done.9), channel_id=1, source_target_pairs={{0,48},{16,0},{32,16},{48,32},{64,112},{80,64},{96,80},{112,96},{1... | collective-permute-start | bytes 147464 | tf_op jit(solution)/shard_map/ppermute | solution.py:129
  29.5 6.0 %all-to-all-done.g0 = bf16[8,64,384]{2,1,0:T(8,128)(2,1)S(1)} async-done(((bf16[8,64,384]{2,1,0:T(8,128)(2,1)}), bf16[8,64,384]{2,1,0:T(8,128)(2,1)S(1)}, u32[]{:S(2)}, u32[]{:S(2)}) %all-to-all-start) | async-done | bytes 393248 | tf_op jit(solution)/shard_map/all_to_all | solution.py:142
  36.3 3.5 %all-to-all-start.1 = ((bf16[8,64,384]{2,1,0:T(8,128)(2,1)}), bf16[8,64,384]{2,1,0:T(8,128)(2,1)S(1)}, u32[]{:S(2)}, u32[]{:S(2)}) async-start(bf16[8,64,384]{2,1,0:T(8,128)(2,1)} %broadcast_in_dim.34), calls=%async_computation.1 | async-start | bytes 786432 | tf_op jit(solution)/shard_map/all_to_all | solution.py:142
  39.9 2.7 %collective-permute-start.4 = (bf16[8,64,384]{2,1,0:T(8,128)(2,1)S(1)}, bf16[8,64,384]{2,1,0:T(8,128)(2,1)S(1)}, u32[]{:S(2)}, u32[]{:S(2)}) collective-permute-start(bf16[8,64,384]{2,1,0:T(8,128)(2,1)S(1)} %all-to-all-done.g0), channel_id=1, source_target_pairs={{0,48},{16,0},{32,16},{48,32},{64,112},{80,64},{96,80},{112,96},{1... | collective-permute-start | bytes 1179656 | tf_op jit(solution)/shard_map/ppermute | solution.py:129
  42.7 4.3 %collective-permute-start.3 = (bf16[8,64,384]{2,1,0:T(8,128)(2,1)S(1)}, bf16[8,64,384]{2,1,0:T(8,128)(2,1)S(1)}, u32[]{:S(2)}, u32[]{:S(2)}) collective-permute-start(bf16[8,64,384]{2,1,0:T(8,128)(2,1)S(1)} %all-to-all-done.g0), channel_id=1, source_target_pairs={{0,16},{16,32},{32,48},{48,0},{64,80},{80,96},{96,112},{112,64},{1... | collective-permute-start | bytes 1179656 | tf_op jit(solution)/shard_map/ppermute | solution.py:129
  47.1 6.1 %collective-permute-done.4.g2 = bf16[8,64,384]{2,1,0:T(8,128)(2,1)S(1)} collective-permute-done((bf16[8,64,384]{2,1,0:T(8,128)(2,1)S(1)}, bf16[8,64,384]{2,1,0:T(8,128)(2,1)S(1)}, u32[]{:S(2)}, u32[]{:S(2)}) %collective-permute-start.4) | collective-permute-done | bytes 393248 | tf_op jit(solution)/shard_map/ppermute | solution.py:129
  55.9 6.8 %all-to-all-start.2 = ((bf16[8,4,64,384]{3,2,1,0:T(8,128)(2,1)}), bf16[8,4,64,384]{3,2,1,0:T(8,128)(2,1)S(1)}, u32[]{:S(2)}, u32[]{:S(2)}) async-start(bf16[8,4,64,384]{3,2,1,0:T(8,128)(2,1)} %broadcast_in_dim.40), calls=%async_computation.2 | async-start | bytes 3145728 | tf_op jit(solution)/shard_map/all_to_all | solution.py:142
  62.7 2.4 %collective-permute-start.7 = (bf16[8,64,384]{2,1,0:T(8,128)(2,1)S(1)}, bf16[8,64,384]{2,1,0:T(8,128)(2,1)S(1)}, u32[]{:S(2)}, u32[]{:S(2)}) collective-permute-start(bf16[8,64,384]{2,1,0:T(8,128)(2,1)S(1)} %all-to-all-done.1.u0), channel_id=1, source_target_pairs={{0,48},{16,0},{32,16},{48,32},{64,112},{80,64},{96,80},{112,96},{1... | collective-permute-start | bytes 1179656 | tf_op jit(solution)/shard_map/ppermute | solution.py:129
  65.2 5.0 %collective-permute-start.5 = (bf16[8,64,384]{2,1,0:T(8,128)(2,1)S(1)}, bf16[8,64,384]{2,1,0:T(8,128)(2,1)S(1)}, u32[]{:S(2)}, u32[]{:S(2)}) collective-permute-start(bf16[8,64,384]{2,1,0:T(8,128)(2,1)S(1)} %collective-permute-done.3.g1), channel_id=1, source_target_pairs={{0,16},{16,32},{32,48},{48,0},{64,80},{80,96},{96,112},{112,64},{1... | collective-permute-start | bytes 1179656 | tf_op jit(solution)/shard_map/ppermute | solution.py:129
  70.2 3.9 %collective-permute-start.6 = (bf16[8,64,384]{2,1,0:T(8,128)(2,1)S(1)}, bf16[8,64,384]{2,1,0:T(8,128)(2,1)S(1)}, u32[]{:S(2)}, u32[]{:S(2)}) collective-permute-start(bf16[8,64,384]{2,1,0:T(8,128)(2,1)S(1)} %all-to-all-done.1.u0), channel_id=1, source_target_pairs={{0,16},{16,32},{32,48},{48,0},{64,80},{80,96},{96,112},{112,64},{1... | collective-permute-start | bytes 1179656 | tf_op jit(solution)/shard_map/ppermute | solution.py:129
  77.4 2.3 %collective-permute-done.5.g3 = bf16[8,64,384]{2,1,0:T(8,128)(2,1)S(1)} collective-permute-done((bf16[8,64,384]{2,1,0:T(8,128)(2,1)S(1)}, bf16[8,64,384]{2,1,0:T(8,128)(2,1)S(1)}, u32[]{:S(2)}, u32[]{:S(2)}) %collective-permute-start.5) | collective-permute-done | bytes 393248 | tf_op jit(solution)/shard_map/ppermute | solution.py:129
  80.5 4.4 %shard_map.68.gate_in = f32[384,384]{1,0:T(8,128)} custom-call(s32[2]{0:T(128)} %pad_add_fusion.place, bf16[768,2048]{1,0:T(8,128)(2,1)} %all-gather.2.cloned.1.call-done.rows_ref, bf16[8,64,384]{2,1,0:T(8,128)(2,1)} %copy-done.1, bf16[8,64,384]{2,1,0:T(8,128)(2,1)} %copy-done.4, bf16[8,64,384]{2,1,0:T(8,128)(2,1)} %copy-done.3, bf16[8,64,384]{2,1,0:T(8,128)(2,1)} %copy-done.6), custom_call_target="tpu_custom_call" | custom-call | flops 603979776 | bytes 10000000 | tf_op jit(solution)/shard_map/pallas_call | solution.py:114
  85.8 6.7 %shard_map.69 = (f32[384,384]{1,0:T(8,128)}, bf16[2048,384]{1,0:T(8,128)(2,1)}) custom-call(s32[2]{0:T(128)} %pad_add_fusion.place, bf16[768,2048]{1,0:T(8,128)(2,1)} %all-gather.2.cloned.1.call-done.rows_ref, bf16[8,64,384]{2,1,0:T(8,128)(2,1)} %copy-done.2, bf16[8,64,384]{2,1,0:T(8,128)(2,1)} %copy-done.7, bf16[8,64,384]{2,1,0:T(8,128)(2,1)} %copy-done.5, ...), custom_call_target="tpu_custom_call" | custom-call | flops 1207959552 | bytes 10000000 | tf_op jit(solution)/shard_map/pallas_call | solution.py:114
  92.6 8.0 %all-to-all-done.2 = bf16[8,4,64,384]{3,2,1,0:T(8,128)(2,1)S(1)} async-done(((bf16[8,4,64,384]{3,2,1,0:T(8,128)(2,1)}), bf16[8,4,64,384]{3,2,1,0:T(8,128)(2,1)S(1)}, u32[]{:S(2)}, u32[]{:S(2)}) %all-to-all-start.2) | async-done | bytes 1572896 | tf_op jit(solution)/shard_map/all_to_all | solution.py:142
  101.8 7.2 %all-to-all-start.3 = ((bf16[32,64,384]{2,1,0:T(8,128)(2,1)}), bf16[32,64,384]{2,1,0:T(8,128)(2,1)S(1)}, u32[]{:S(2)}, u32[]{:S(2)}) async-start(bf16[32,64,384]{2,1,0:T(8,128)(2,1)} %bitcast.15), calls=%async_computation.4 | async-start | bytes 3145728 | tf_op jit(solution)/shard_map/all_to_all | solution.py:220
  109.0 6.6 %shard_map.70 = (bf16[8,384,128]{2,1,0:T(8,128)(2,1)}, bf16[8,384,128]{2,1,0:T(8,128)(2,1)}) custom-call(s32[2]{0:T(128)} %pad_add_fusion.place, bf16[768,2048]{1,0:T(8,128)(2,1)} %all-gather.2.cloned.1.call-done.rows_ref, bf16[8,2,128,384]{3,2,1,0:T(8,128)(2,1)} %bitcast.13, bf16[8,64,384]{2,1,0:T(8,128)(2,1)} %copy-done.1, bf16[8,64,384]{2,1,0:T(8,128)(2,1)} %copy-done.4, ...), custom_call_target="tpu_custom_call" | custom-call | flops 1811939328 | bytes 10000000 | tf_op jit(solution)/shard_map/pallas_call | solution.py:114
  115.6 1.9 %collective-permute-start.9 = (bf16[8,384,128]{2,1,0:T(8,128)(2,1)}, bf16[8,384,128]{2,1,0:T(8,128)(2,1)S(1)}, u32[]{:S(2)}, u32[]{:S(2)}) collective-permute-start(bf16[8,384,128]{2,1,0:T(8,128)(2,1)} %get-tuple-element.26), channel_id=1, source_target_pairs={{0,1},{1,0},{2,3},{3,2},{4,5},{5,4},{6,7},{7,6},{8,9},{9,8},{10,11... | collective-permute-start | bytes 2359304 | tf_op jit(solution)/shard_map/ppermute | solution.py:134
  117.5 2.5 %collective-permute-done.9 = bf16[8,384,128]{2,1,0:T(8,128)(2,1)S(1)} collective-permute-done((bf16[8,384,128]{2,1,0:T(8,128)(2,1)}, bf16[8,384,128]{2,1,0:T(8,128)(2,1)S(1)}, u32[]{:S(2)}, u32[]{:S(2)}) %collective-permute-start.9) | collective-permute-done | bytes 786464 | tf_op jit(solution)/shard_map/ppermute | solution.py:134
  120.0 2.3 %add_convert_fusion = bf16[8,384,128]{2,1,0:T(8,128)(2,1)} fusion(bf16[8,384,128]{2,1,0:T(8,128)(2,1)S(1)} %collective-permute-done.9, bf16[8,384,128]{2,1,0:T(8,128)(2,1)} %get-tuple-element.25), kind=kLoop, calls=%fused_computation.1 | loop fusion | flops 1572864 | bytes 2359296 | tf_op jit(solution)/shard_map/convert_element_type | solution.py:212
  122.3 24.0 %all-to-all-done.3 = bf16[32,64,384]{2,1,0:T(8,128)(2,1)S(1)} async-done(((bf16[32,64,384]{2,1,0:T(8,128)(2,1)}), bf16[32,64,384]{2,1,0:T(8,128)(2,1)S(1)}, u32[]{:S(2)}, u32[]{:S(2)}) %all-to-all-start.3) | async-done | bytes 1572896 | tf_op jit(solution)/shard_map/all_to_all | solution.py:220
  147.2 16.5 %reduce-scatter.2.cloned.1.call-done = bf16[384,128]{1,0:T(8,128)(2,1)} async-done(((bf16[3072,128]{1,0:T(8,128)(2,1)}), bf16[384,128]{1,0:T(8,128)(2,1)}) %reduce-scatter.2.cloned.1.call-update) | async-done | bytes 98320 | tf_op jit(solution)/shard_map/reduce_scatter | solution.py:213
  (46 shorter events, 14.0 us)
Async XLA Ops:
  7.2 13.6 %copy-start.9 = (bf16[64,384]{1,0:T(8,128)(2,1)S(1)}, bf16[64,384]{1,0:T(8,128)(2,1)}, u32[]{:S(2)}) copy-start(bf16[64,384]{1,0:T(8,128)(2,1)} %param.9) | copy-start | bytes 147460
  7.2 28.3 %copy-start.8 = (bf16[64,384]{1,0:T(8,128)(2,1)S(1)}, bf16[64,384]{1,0:T(8,128)(2,1)}, u32[]{:S(2)}) copy-start(bf16[64,384]{1,0:T(8,128)(2,1)} %param.8) | copy-start | bytes 147460
  7.2 72.6 %all-gather.2.cloned.1.call-start = ((), (), s32[]{:S(2)}) async-start(), calls=%async_computation.5 | async-start | bytes 3342336 | tf_op jit(solution)/shard_map/all_gather | solution.py:161
  10.5 25.0 %all-to-all-start = ((bf16[8,64,384]{2,1,0:T(8,128)(2,1)}), bf16[8,64,384]{2,1,0:T(8,128)(2,1)S(1)}, u32[]{:S(2)}, u32[]{:S(2)}) async-start(bf16[8,64,384]{2,1,0:T(8,128)(2,1)} %broadcast_in_dim.16), calls=%async_computation | async-start | bytes 786432 | tf_op jit(solution)/shard_map/all_to_all | solution.py:142
  20.8 19.1 %collective-permute-start = (bf16[64,384]{1,0:T(8,128)(2,1)S(1)}, bf16[64,384]{1,0:T(8,128)(2,1)S(1)}, u32[]{:S(2)}, u32[]{:S(2)}) collective-permute-start(bf16[64,384]{1,0:T(8,128)(2,1)S(1)} %copy-done.9), channel_id=1, source_target_pairs={{0,16},{16,32},{32,48},{48,0},{64,80},{80,96},{96,112},{112,64},{1... | collective-permute-start | bytes 147464 | tf_op jit(solution)/shard_map/ppermute | solution.py:129
  23.2 23.8 %collective-permute-start.2 = (bf16[64,384]{1,0:T(8,128)(2,1)S(1)}, bf16[64,384]{1,0:T(8,128)(2,1)S(1)}, u32[]{:S(2)}, u32[]{:S(2)}) collective-permute-start(bf16[64,384]{1,0:T(8,128)(2,1)S(1)} %copy-done.9), channel_id=1, source_target_pairs={{0,32},{16,48},{32,0},{48,16},{64,96},{80,112},{96,64},{112,80},{1... | collective-permute-start | bytes 147464 | tf_op jit(solution)/shard_map/ppermute | solution.py:129
  27.5 19.5 %collective-permute-start.1 = (bf16[64,384]{1,0:T(8,128)(2,1)S(1)}, bf16[64,384]{1,0:T(8,128)(2,1)S(1)}, u32[]{:S(2)}, u32[]{:S(2)}) collective-permute-start(bf16[64,384]{1,0:T(8,128)(2,1)S(1)} %copy-done.9), channel_id=1, source_target_pairs={{0,48},{16,0},{32,16},{48,32},{64,112},{80,64},{96,80},{112,96},{1... | collective-permute-start | bytes 147464 | tf_op jit(solution)/shard_map/ppermute | solution.py:129
  35.5 20.4 %copy-start.1 = (bf16[8,64,384]{2,1,0:T(8,128)(2,1)}, bf16[8,64,384]{2,1,0:T(8,128)(2,1)S(1)}, u32[]{:S(2)}) copy-start(bf16[8,64,384]{2,1,0:T(8,128)(2,1)S(1)} %all-to-all-done.g0) | copy-start | bytes 1179652
  36.3 18.1 %all-to-all-start.1 = ((bf16[8,64,384]{2,1,0:T(8,128)(2,1)}), bf16[8,64,384]{2,1,0:T(8,128)(2,1)S(1)}, u32[]{:S(2)}, u32[]{:S(2)}) async-start(bf16[8,64,384]{2,1,0:T(8,128)(2,1)} %broadcast_in_dim.34), calls=%async_computation.1 | async-start | bytes 786432 | tf_op jit(solution)/shard_map/all_to_all | solution.py:142
  39.9 13.2 %collective-permute-start.4 = (bf16[8,64,384]{2,1,0:T(8,128)(2,1)S(1)}, bf16[8,64,384]{2,1,0:T(8,128)(2,1)S(1)}, u32[]{:S(2)}, u32[]{:S(2)}) collective-permute-start(bf16[8,64,384]{2,1,0:T(8,128)(2,1)S(1)} %all-to-all-done.g0), channel_id=1, source_target_pairs={{0,48},{16,0},{32,16},{48,32},{64,112},{80,64},{96,80},{112,96},{1... | collective-permute-start | bytes 1179656 | tf_op jit(solution)/shard_map/ppermute | solution.py:129
  42.7 11.7 %collective-permute-start.3 = (bf16[8,64,384]{2,1,0:T(8,128)(2,1)S(1)}, bf16[8,64,384]{2,1,0:T(8,128)(2,1)S(1)}, u32[]{:S(2)}, u32[]{:S(2)}) collective-permute-start(bf16[8,64,384]{2,1,0:T(8,128)(2,1)S(1)} %all-to-all-done.g0), channel_id=1, source_target_pairs={{0,16},{16,32},{32,48},{48,0},{64,80},{80,96},{96,112},{112,64},{1... | collective-permute-start | bytes 1179656 | tf_op jit(solution)/shard_map/ppermute | solution.py:129
  53.1 2.8 %copy-start.3 = (bf16[8,64,384]{2,1,0:T(8,128)(2,1)}, bf16[8,64,384]{2,1,0:T(8,128)(2,1)S(1)}, u32[]{:S(2)}) copy-start(bf16[8,64,384]{2,1,0:T(8,128)(2,1)S(1)} %collective-permute-done.4.g2) | copy-start | bytes 1179652
  54.4 10.8 %copy-start.4 = (bf16[8,64,384]{2,1,0:T(8,128)(2,1)}, bf16[8,64,384]{2,1,0:T(8,128)(2,1)S(1)}, u32[]{:S(2)}) copy-start(bf16[8,64,384]{2,1,0:T(8,128)(2,1)S(1)} %collective-permute-done.3.g1) | copy-start | bytes 1179652
  54.4 15.8 %copy-start.2 = (bf16[8,64,384]{2,1,0:T(8,128)(2,1)}, bf16[8,64,384]{2,1,0:T(8,128)(2,1)S(1)}, u32[]{:S(2)}) copy-start(bf16[8,64,384]{2,1,0:T(8,128)(2,1)S(1)} %all-to-all-done.1.u0) | copy-start | bytes 1179652
  55.9 44.7 %all-to-all-start.2 = ((bf16[8,4,64,384]{3,2,1,0:T(8,128)(2,1)}), bf16[8,4,64,384]{3,2,1,0:T(8,128)(2,1)S(1)}, u32[]{:S(2)}, u32[]{:S(2)}) async-start(bf16[8,4,64,384]{3,2,1,0:T(8,128)(2,1)} %broadcast_in_dim.40), calls=%async_computation.2 | async-start | bytes 3145728 | tf_op jit(solution)/shard_map/all_to_all | solution.py:142
  62.7 12.1 %collective-permute-start.7 = (bf16[8,64,384]{2,1,0:T(8,128)(2,1)S(1)}, bf16[8,64,384]{2,1,0:T(8,128)(2,1)S(1)}, u32[]{:S(2)}, u32[]{:S(2)}) collective-permute-start(bf16[8,64,384]{2,1,0:T(8,128)(2,1)S(1)} %all-to-all-done.1.u0), channel_id=1, source_target_pairs={{0,48},{16,0},{32,16},{48,32},{64,112},{80,64},{96,80},{112,96},{1... | collective-permute-start | bytes 1179656 | tf_op jit(solution)/shard_map/ppermute | solution.py:129
  65.2 14.6 %collective-permute-start.5 = (bf16[8,64,384]{2,1,0:T(8,128)(2,1)S(1)}, bf16[8,64,384]{2,1,0:T(8,128)(2,1)S(1)}, u32[]{:S(2)}, u32[]{:S(2)}) collective-permute-start(bf16[8,64,384]{2,1,0:T(8,128)(2,1)S(1)} %collective-permute-done.3.g1), channel_id=1, source_target_pairs={{0,16},{16,32},{32,48},{48,0},{64,80},{80,96},{96,112},{112,64},{1... | collective-permute-start | bytes 1179656 | tf_op jit(solution)/shard_map/ppermute | solution.py:129
  70.2 14.7 %collective-permute-start.6 = (bf16[8,64,384]{2,1,0:T(8,128)(2,1)S(1)}, bf16[8,64,384]{2,1,0:T(8,128)(2,1)S(1)}, u32[]{:S(2)}, u32[]{:S(2)}) collective-permute-start(bf16[8,64,384]{2,1,0:T(8,128)(2,1)S(1)} %all-to-all-done.1.u0), channel_id=1, source_target_pairs={{0,16},{16,32},{32,48},{48,0},{64,80},{80,96},{96,112},{112,64},{1... | collective-permute-start | bytes 1179656 | tf_op jit(solution)/shard_map/ppermute | solution.py:129
  74.8 10.1 %copy-start.5 = (bf16[8,64,384]{2,1,0:T(8,128)(2,1)}, bf16[8,64,384]{2,1,0:T(8,128)(2,1)S(1)}, u32[]{:S(2)}) copy-start(bf16[8,64,384]{2,1,0:T(8,128)(2,1)S(1)} %collective-permute-done.7.u2) | copy-start | bytes 1179652
  74.8 11.0 %collective-permute-start.8 = (bf16[8,64,384]{2,1,0:T(8,128)(2,1)S(1)}, bf16[8,64,384]{2,1,0:T(8,128)(2,1)}, u32[]{:S(2)}, u32[]{:S(2)}) collective-permute-start(bf16[8,64,384]{2,1,0:T(8,128)(2,1)S(1)} %collective-permute-done.7.u2), channel_id=1, source_target_pairs={{0,48},{16,0},{32,16},{48,32},{64,112},{80,64},{96,80},{112,96},{1... | collective-permute-start | bytes 1179656 | tf_op jit(solution)/shard_map/ppermute | solution.py:129
  100.6 1.2 copy-start
  101.8 44.5 %all-to-all-start.3 = ((bf16[32,64,384]{2,1,0:T(8,128)(2,1)}), bf16[32,64,384]{2,1,0:T(8,128)(2,1)S(1)}, u32[]{:S(2)}, u32[]{:S(2)}) async-start(bf16[32,64,384]{2,1,0:T(8,128)(2,1)} %bitcast.15), calls=%async_computation.4 | async-start | bytes 3145728 | tf_op jit(solution)/shard_map/all_to_all | solution.py:220
  108.9 54.7 %reduce-scatter.2.cloned.1.call-start = ((), (), s32[]{:S(2)}) async-start(), calls=%async_computation.6 | async-start | bytes 884736 | tf_op jit(solution)/shard_map/reduce_scatter | solution.py:213
  115.6 4.4 %collective-permute-start.9 = (bf16[8,384,128]{2,1,0:T(8,128)(2,1)}, bf16[8,384,128]{2,1,0:T(8,128)(2,1)S(1)}, u32[]{:S(2)}, u32[]{:S(2)}) collective-permute-start(bf16[8,384,128]{2,1,0:T(8,128)(2,1)} %get-tuple-element.26), channel_id=1, source_target_pairs={{0,1},{1,0},{2,3},{3,2},{4,5},{5,4},{6,7},{7,6},{8,9},{9,8},{10,11... | collective-permute-start | bytes 2359304 | tf_op jit(solution)/shard_map/ppermute | solution.py:134
  (2 other events, 1.7 us)
Sparse Core Ops, SparseCore 0:
  10.6 52.2 all-gather.1
  122.4 41.2 reduce-scatter.1

commit v7 on v5

--- a/solution.py
+++ b/solution.py
@@ -67,7 +67,12 @@
     up_out[...] = up_value
     hidden = (silu * up_value).astype(jnp.bfloat16)
     cot_copy.wait()
-    partial_out[...] = dot(cot[...], hidden, ((0,), (0,))).astype(jnp.bfloat16)
+    partial_value = dot(cot[...], hidden, ((0,), (0,))).astype(jnp.bfloat16)
+    depth = n_feat // (N_Z * N_X)
+    for z in range(N_Z):
+        for x in range(N_X):
+            row = (z * N_X + x) * depth
+            partial_out[x, z] = partial_value[row : row + depth]
 
 
 def backward_kernel(
@@ -130,8 +135,8 @@
     return lax.ppermute(value, "fsdp", pairs)
 
 
-def swap_x(value, flip):
-    pairs = [(z * N_X + x, z * N_X + (x ^ flip)) for z in range(N_Z) for x in range(N_X)]
+def swap_z(value, flip):
+    pairs = [(z * N_X + x, (z ^ flip) * N_X + x) for z in range(N_Z) for x in range(N_X)]
     return lax.ppermute(value, "fsdp", pairs)
 
 
@@ -159,6 +164,7 @@
     n_feat = depth * n_fsdp
     factor = 1.0 / math.sqrt(rows * n_fsdp)
     me_x = lax.axis_index("fsdp") % N_X
+    me_z = lax.axis_index("fsdp") // N_X
     core = lax.axis_index("mp") % N_CORE
 
     gate_copies = copies_of(gate_weight)
@@ -202,7 +208,7 @@
         forward_kernel,
         5,
         (place, both) + blocks[4:] + (gate_value,),
-        (value, jax.ShapeDtypeStruct((n_feat, cols), jnp.bfloat16)),
+        (value, jax.ShapeDtypeStruct((N_X, N_Z, depth, cols), jnp.bfloat16)),
         [row_block, row_block, full, sems((2,)), sems((N_X,))],
         4 * rows * n_feat * cols,
     )
@@ -218,13 +224,19 @@
     pair_sum = add(mine, send_core(other)).astype(jnp.bfloat16)
     summed = lax.all_to_all(pair_sum, "mp", 0, 0, axis_index_groups=Y_GROUPS)
 
-    down_z = lax.psum_scatter(
-        down_partial, "fsdp", scatter_dimension=0, axis_index_groups=Z_GROUPS, tiled=True
-    ).reshape(N_X, depth, cols)
-    block = lambda flip: lax.dynamic_index_in_dim(down_z, me_x ^ flip, 0, False)
-    received = swap_x(jnp.stack([block(1), block(2)]), 1)
-    passed = swap_x(add(block(3), received[1]).astype(jnp.bfloat16), 3)
-    down_sum = add(block(0), received[0]) + passed.astype(jnp.float32)
+    down_x = lax.psum_scatter(
+        down_partial.reshape(n_feat, cols),
+        "fsdp",
+        scatter_dimension=0,
+        axis_index_groups=X_GROUPS,
+        tiled=True,
+    ).reshape(N_Z, depth, cols)
+    block = lambda flip: lax.dynamic_index_in_dim(down_x, me_z ^ flip, 0, False)
+    got = swap_z(jnp.stack([block(1 ^ flip) for flip in (0, 2, 6, 4)]), 1)
+    mine_0, mine_2, mine_6, mine_4 = (add(block(f), got[i]) for i, f in enumerate((0, 2, 6, 4)))
+    got = swap_z(jnp.stack([mine_2, mine_4]).astype(jnp.bfloat16), 2)
+    got_last = swap_z((mine_6 + got[1].astype(jnp.float32)).astype(jnp.bfloat16), 6)
+    down_sum = mine_0 + got[0].astype(jnp.float32) + got_last.astype(jnp.float32)
     grad_down = (down_sum * factor).astype(jnp.bfloat16)
     input_grad = summed.astype(jnp.float32).sum(0).astype(jnp.bfloat16)
     return (input_grad, grad_down)

time: 164 us -> 162 us (0.988)
  waiting for transfers between devices: 55.4 us -> 42.7 us
  starting transfers between devices: 60.9 us -> 70.1 us
    reduce_scatter x1, waiting for transfers between devices: 16.1 us -> 2.35 us  [on_device(): lax.psum_scatter(down_partial.reshape(n_feat, cols), 'fsdp', scatter_dime...]
    ppermute x2 -> x3, starting transfers between devices: 5.36 us -> 14.6 us  [swap_z(): return lax.ppermute(value, 'fsdp', pairs)]
    ppermute x2 -> x3, waiting for transfers between devices: 7.55 us -> 8.7 us  [swap_z(): return lax.ppermute(value, 'fsdp', pairs)]
  transfers between devices with their start and end apart: 18 -> 19, of which waited for: 11 -> 12; matrix products, arithmetic and copies ran while one was open for 5% -> 5% of each run, Pallas kernels for 11% -> 11%
where the time goes in v7:
time: 162 us; the launch traced here: 160 us
  starting transfers between devices  70.1 us (43%)
  waiting for transfers between devices  42.7 us (26%)
  Pallas kernels  17.7 us (11%)
  between operations  14.5 us (9%)
  other arithmetic  8.48 us (5%)
  local copies, waits for them, and re-layouts  6.84 us (4%)
    ppermute x9, starting transfers between devices, send_x(): return lax.ppermute(value, 'fsdp', pairs)  25.9 us
    all_to_all x3, starting transfers between devices, gather_z(): return lax.all_to_all(copies, 'fsdp', 0, 0, axis_index_groups=Z_GROUPS)  20.6 us
    pallas_call x3, Pallas kernels, call_kernel(): pl.pallas_call(kernel, out_shape=out_shapes, in_specs=in_specs, out_specs...  17.7 us
    ppermute x9, waiting for transfers between devices, send_x(): return lax.ppermute(value, 'fsdp', pairs)  15.2 us
    ppermute x3, starting transfers between devices, swap_z(): return lax.ppermute(value, 'fsdp', pairs)  14.6 us
    all_to_all x3, waiting for transfers between devices, gather_z(): return lax.all_to_all(copies, 'fsdp', 0, 0, axis_index_groups=Z_GROUPS)  14 us
    ppermute x3, waiting for transfers between devices, swap_z(): return lax.ppermute(value, 'fsdp', pairs)  8.7 us
    all_to_all x1, starting transfers between devices, on_device(): summed = lax.all_to_all(pair_sum, 'mp', 0, 0, axis_index_groups=Y_GROUPS)  7.02 us
  transfers between devices with their start and end apart: 19, of which 12 were waited for; matrix products, arithmetic and copies ran while one was open for 5% of the time, Pallas kernels for 11%

profile of v7, /device:TPU:6, one launch (start us, length us, event | category | flops | bytes accessed | tf_op | source)
XLA Modules:
  0.0 160.3 jit_solution(10572575716810667300)
XLA Ops:
  10.5 10.3 %all-to-all-start = ((bf16[8,64,384]{2,1,0:T(8,128)(2,1)}), bf16[8,64,384]{2,1,0:T(8,128)(2,1)S(1)}, u32[]{:S(2)}, u32[]{:S(2)}) async-start(bf16[8,64,384]{2,1,0:T(8,128)(2,1)} %broadcast_in_dim.16), calls=%async_computation | async-start | bytes 786432 | tf_op jit(solution)/shard_map/all_to_all | solution.py:153
  23.2 3.5 %collective-permute-start.1 = (bf16[64,384]{1,0:T(8,128)(2,1)S(1)}, bf16[64,384]{1,0:T(8,128)(2,1)S(1)}, u32[]{:S(2)}, u32[]{:S(2)}) collective-permute-start(bf16[64,384]{1,0:T(8,128)(2,1)S(1)} %copy-done.9), channel_id=1, source_target_pairs={{0,48},{16,0},{32,16},{48,32},{64,112},{80,64},{96,80},{112,96},{1... | collective-permute-start | bytes 147464 | tf_op jit(solution)/shard_map/ppermute | solution.py:135
  26.6 3.3 %collective-permute-start.2 = (bf16[64,384]{1,0:T(8,128)(2,1)S(1)}, bf16[64,384]{1,0:T(8,128)(2,1)S(1)}, u32[]{:S(2)}, u32[]{:S(2)}) collective-permute-start(bf16[64,384]{1,0:T(8,128)(2,1)S(1)} %copy-done.9), channel_id=1, source_target_pairs={{0,32},{16,48},{32,0},{48,16},{64,96},{80,112},{96,64},{112,80},{1... | collective-permute-start | bytes 147464 | tf_op jit(solution)/shard_map/ppermute | solution.py:135
  30.0 5.5 %all-to-all-done.g0 = bf16[8,64,384]{2,1,0:T(8,128)(2,1)S(1)} async-done(((bf16[8,64,384]{2,1,0:T(8,128)(2,1)}), bf16[8,64,384]{2,1,0:T(8,128)(2,1)S(1)}, u32[]{:S(2)}, u32[]{:S(2)}) %all-to-all-start) | async-done | bytes 393248 | tf_op jit(solution)/shard_map/all_to_all | solution.py:153
  36.3 3.5 %all-to-all-start.1 = ((bf16[8,64,384]{2,1,0:T(8,128)(2,1)}), bf16[8,64,384]{2,1,0:T(8,128)(2,1)S(1)}, u32[]{:S(2)}, u32[]{:S(2)}) async-start(bf16[8,64,384]{2,1,0:T(8,128)(2,1)} %broadcast_in_dim.34), calls=%async_computation.1 | async-start | bytes 786432 | tf_op jit(solution)/shard_map/all_to_all | solution.py:153
  39.9 2.4 %collective-permute-start.3 = (bf16[8,64,384]{2,1,0:T(8,128)(2,1)S(1)}, bf16[8,64,384]{2,1,0:T(8,128)(2,1)S(1)}, u32[]{:S(2)}, u32[]{:S(2)}) collective-permute-start(bf16[8,64,384]{2,1,0:T(8,128)(2,1)S(1)} %all-to-all-done.g0), channel_id=1, source_target_pairs={{0,16},{16,32},{32,48},{48,0},{64,80},{80,96},{96,112},{112,64},{1... | collective-permute-start | bytes 1179656 | tf_op jit(solution)/shard_map/ppermute | solution.py:135
  42.3 3.4 %collective-permute-start.4 = (bf16[8,64,384]{2,1,0:T(8,128)(2,1)S(1)}, bf16[8,64,384]{2,1,0:T(8,128)(2,1)S(1)}, u32[]{:S(2)}, u32[]{:S(2)}) collective-permute-start(bf16[8,64,384]{2,1,0:T(8,128)(2,1)S(1)} %all-to-all-done.g0), channel_id=1, source_target_pairs={{0,48},{16,0},{32,16},{48,32},{64,112},{80,64},{96,80},{112,96},{1... | collective-permute-start | bytes 1179656 | tf_op jit(solution)/shard_map/ppermute | solution.py:135
  45.9 6.1 %collective-permute-done.3.g1 = bf16[8,64,384]{2,1,0:T(8,128)(2,1)S(1)} collective-permute-done((bf16[8,64,384]{2,1,0:T(8,128)(2,1)S(1)}, bf16[8,64,384]{2,1,0:T(8,128)(2,1)S(1)}, u32[]{:S(2)}, u32[]{:S(2)}) %collective-permute-start.3) | collective-permute-done | bytes 393248 | tf_op jit(solution)/shard_map/ppermute | solution.py:135
  51.9 3.4 %collective-permute-done.4.g2 = bf16[8,64,384]{2,1,0:T(8,128)(2,1)S(1)} collective-permute-done((bf16[8,64,384]{2,1,0:T(8,128)(2,1)S(1)}, bf16[8,64,384]{2,1,0:T(8,128)(2,1)S(1)}, u32[]{:S(2)}, u32[]{:S(2)}) %collective-permute-start.4) | collective-permute-done | bytes 393248 | tf_op jit(solution)/shard_map/ppermute | solution.py:135
  56.7 6.8 %all-to-all-start.2 = ((bf16[8,4,64,384]{3,2,1,0:T(8,128)(2,1)}), bf16[8,4,64,384]{3,2,1,0:T(8,128)(2,1)S(1)}, u32[]{:S(2)}, u32[]{:S(2)}) async-start(bf16[8,4,64,384]{3,2,1,0:T(8,128)(2,1)} %broadcast_in_dim.40), calls=%async_computation.2 | async-start | bytes 3145728 | tf_op jit(solution)/shard_map/all_to_all | solution.py:153
  65.8 4.8 %collective-permute-start.5 = (bf16[8,64,384]{2,1,0:T(8,128)(2,1)S(1)}, bf16[8,64,384]{2,1,0:T(8,128)(2,1)S(1)}, u32[]{:S(2)}, u32[]{:S(2)}) collective-permute-start(bf16[8,64,384]{2,1,0:T(8,128)(2,1)S(1)} %collective-permute-done.3.g1), channel_id=1, source_target_pairs={{0,16},{16,32},{32,48},{48,0},{64,80},{80,96},{96,112},{112,64},{1... | collective-permute-start | bytes 1179656 | tf_op jit(solution)/shard_map/ppermute | solution.py:135
  72.6 2.6 %collective-permute-done.7.u2 = bf16[8,64,384]{2,1,0:T(8,128)(2,1)S(1)} collective-permute-done((bf16[8,64,384]{2,1,0:T(8,128)(2,1)S(1)}, bf16[8,64,384]{2,1,0:T(8,128)(2,1)S(1)}, u32[]{:S(2)}, u32[]{:S(2)}) %collective-permute-start.7) | collective-permute-done | bytes 393248 | tf_op jit(solution)/shard_map/ppermute | solution.py:135
  77.8 2.5 %collective-permute-done.5.g3 = bf16[8,64,384]{2,1,0:T(8,128)(2,1)S(1)} collective-permute-done((bf16[8,64,384]{2,1,0:T(8,128)(2,1)S(1)}, bf16[8,64,384]{2,1,0:T(8,128)(2,1)S(1)}, u32[]{:S(2)}, u32[]{:S(2)}) %collective-permute-start.5) | collective-permute-done | bytes 393248 | tf_op jit(solution)/shard_map/ppermute | solution.py:135
  81.0 4.4 %shard_map.68.gate_in = f32[384,384]{1,0:T(8,128)} custom-call(s32[2]{0:T(128)} %pad_add_fusion.place, bf16[768,2048]{1,0:T(8,128)(2,1)} %all-gather.2.cloned.1.call-done.rows_ref, bf16[8,64,384]{2,1,0:T(8,128)(2,1)} %copy-done.1, bf16[8,64,384]{2,1,0:T(8,128)(2,1)} %copy-done.3, bf16[8,64,384]{2,1,0:T(8,128)(2,1)} %copy-done.4, bf16[8,64,384]{2,1,0:T(8,128)(2,1)} %copy-done.6), custom_call_target="tpu_custom_call" | custom-call | flops 603979776 | bytes 10000000 | tf_op jit(solution)/shard_map/pallas_call | solution.py:120
  86.2 6.7 %shard_map.69 = (f32[384,384]{1,0:T(8,128)}, bf16[4,8,64,384]{3,2,1,0:T(8,128)(2,1)}) custom-call(s32[2]{0:T(128)} %pad_add_fusion.place, bf16[768,2048]{1,0:T(8,128)(2,1)} %all-gather.2.cloned.1.call-done.rows_ref, bf16[8,64,384]{2,1,0:T(8,128)(2,1)} %copy-done.2, bf16[8,64,384]{2,1,0:T(8,128)(2,1)} %copy-done.7, bf16[8,64,384]{2,1,0:T(8,128)(2,1)} %copy-done.5, ...), custom_call_target="tpu_custom_call" | custom-call | flops 1207959552 | bytes 10000000 | tf_op jit(solution)/shard_map/pallas_call | solution.py:120
  92.9 8.5 %all-to-all-done.2 = bf16[8,4,64,384]{3,2,1,0:T(8,128)(2,1)S(1)} async-done(((bf16[8,4,64,384]{3,2,1,0:T(8,128)(2,1)}), bf16[8,4,64,384]{3,2,1,0:T(8,128)(2,1)S(1)}, u32[]{:S(2)}, u32[]{:S(2)}) %all-to-all-start.2) | async-done | bytes 1572896 | tf_op jit(solution)/shard_map/all_to_all | solution.py:153
  102.6 6.6 %shard_map.70 = (bf16[8,384,128]{2,1,0:T(8,128)(2,1)}, bf16[8,384,128]{2,1,0:T(8,128)(2,1)}) custom-call(s32[2]{0:T(128)} %pad_add_fusion.place, bf16[768,2048]{1,0:T(8,128)(2,1)} %all-gather.2.cloned.1.call-done.rows_ref, bf16[8,2,128,384]{3,2,1,0:T(8,128)(2,1)} %bitcast.21, bf16[8,64,384]{2,1,0:T(8,128)(2,1)} %copy-done.1, bf16[8,64,384]{2,1,0:T(8,128)(2,1)} %copy-done.3, ...), custom_call_target="tpu_custom_call" | custom-call | flops 1811939328 | bytes 10000000 | tf_op jit(solution)/shard_map/pallas_call | solution.py:120
  111.2 2.5 %collective-permute-done.9 = bf16[8,384,128]{2,1,0:T(8,128)(2,1)S(1)} collective-permute-done((bf16[8,384,128]{2,1,0:T(8,128)(2,1)}, bf16[8,384,128]{2,1,0:T(8,128)(2,1)S(1)}, u32[]{:S(2)}, u32[]{:S(2)}) %collective-permute-start.9) | collective-permute-done | bytes 786464 | tf_op jit(solution)/shard_map/ppermute | solution.py:145
  115.9 7.0 %all-to-all-start.3 = ((bf16[8,384,128]{2,1,0:T(8,128)(2,1)}), bf16[8,384,128]{2,1,0:T(8,128)(2,1)S(1)}, u32[]{:S(2)}, u32[]{:S(2)}) async-start(bf16[8,384,128]{2,1,0:T(8,128)(2,1)} %add_convert_fusion), calls=%async_computation.3 | async-start | bytes 1572864 | tf_op jit(solution)/shard_map/all_to_all | solution.py:225
  126.2 3.1 %collective-permute-start.10 = (bf16[4,64,384]{2,1,0:T(8,128)(2,1)S(1)}, bf16[4,64,384]{2,1,0:T(8,128)(2,1)S(1)}, u32[]{:S(2)}, u32[]{:S(2)}) collective-permute-start(bf16[4,64,384]{2,1,0:T(8,128)(2,1)S(1)} %pad_maximum_fusion.1), channel_id=1, source_target_pairs={{0,64},{16,80},{32,96},{48,112},{64,0},{80,16},{96,32},{112,48},{1... | collective-permute-start | bytes 589832 | tf_op jit(solution)/shard_map/ppermute | solution.py:140
  129.4 4.7 %collective-permute-done.10 = bf16[4,64,384]{2,1,0:T(8,128)(2,1)S(1)} collective-permute-done((bf16[4,64,384]{2,1,0:T(8,128)(2,1)S(1)}, bf16[4,64,384]{2,1,0:T(8,128)(2,1)S(1)}, u32[]{:S(2)}, u32[]{:S(2)}) %collective-permute-start.10) | collective-permute-done | bytes 196640 | tf_op jit(solution)/shard_map/ppermute | solution.py:140
  134.9 4.7 %collective-permute-start.11 = (bf16[2,64,384]{2,1,0:T(8,128)(2,1)S(1)}, bf16[2,64,384]{2,1,0:T(8,128)(2,1)S(1)}, u32[]{:S(2)}, u32[]{:S(2)}) collective-permute-start(bf16[2,64,384]{2,1,0:T(8,128)(2,1)S(1)} %pad_maximum_fusion.2), channel_id=1, source_target_pairs={{0,128},{16,144},{32,160},{48,176},{64,192},{80,208},{96,224},{112... | collective-permute-start | bytes 294920 | tf_op jit(solution)/shard_map/ppermute | solution.py:140
  139.6 2.7 %collective-permute-done.11 = bf16[2,64,384]{2,1,0:T(8,128)(2,1)S(1)} collective-permute-done((bf16[2,64,384]{2,1,0:T(8,128)(2,1)S(1)}, bf16[2,64,384]{2,1,0:T(8,128)(2,1)S(1)}, u32[]{:S(2)}, u32[]{:S(2)}) %collective-permute-start.11) | collective-permute-done | bytes 98336 | tf_op jit(solution)/shard_map/ppermute | solution.py:140
  143.2 6.7 %collective-permute-start.12 = (bf16[64,384]{1,0:T(8,128)(2,1)S(1)}, bf16[64,384]{1,0:T(8,128)(2,1)S(1)}, u32[]{:S(2)}, u32[]{:S(2)}) collective-permute-start(bf16[64,384]{1,0:T(8,128)(2,1)S(1)} %fusion.2), channel_id=1, source_target_pairs={{0,384},{16,400},{32,416},{48,432},{64,448},{80,464},{96,480},{112... | collective-permute-start | bytes 147464 | tf_op jit(solution)/shard_map/ppermute | solution.py:140
  (57 shorter events, 30.2 us)
Async XLA Ops:
  7.2 13.6 %copy-start.9 = (bf16[64,384]{1,0:T(8,128)(2,1)S(1)}, bf16[64,384]{1,0:T(8,128)(2,1)}, u32[]{:S(2)}) copy-start(bf16[64,384]{1,0:T(8,128)(2,1)} %param.9) | copy-start | bytes 147460
  7.2 28.3 %copy-start.8 = (bf16[64,384]{1,0:T(8,128)(2,1)S(1)}, bf16[64,384]{1,0:T(8,128)(2,1)}, u32[]{:S(2)}) copy-start(bf16[64,384]{1,0:T(8,128)(2,1)} %param.8) | copy-start | bytes 147460
  7.2 73.1 %all-gather.2.cloned.1.call-start = ((), (), s32[]{:S(2)}) async-start(), calls=%async_computation.5 | async-start | bytes 3342336 | tf_op jit(solution)/shard_map/all_gather | solution.py:173
  10.5 25.0 %all-to-all-start = ((bf16[8,64,384]{2,1,0:T(8,128)(2,1)}), bf16[8,64,384]{2,1,0:T(8,128)(2,1)S(1)}, u32[]{:S(2)}, u32[]{:S(2)}) async-start(bf16[8,64,384]{2,1,0:T(8,128)(2,1)} %broadcast_in_dim.16), calls=%async_computation | async-start | bytes 786432 | tf_op jit(solution)/shard_map/all_to_all | solution.py:153
  20.8 19.1 %collective-permute-start = (bf16[64,384]{1,0:T(8,128)(2,1)S(1)}, bf16[64,384]{1,0:T(8,128)(2,1)S(1)}, u32[]{:S(2)}, u32[]{:S(2)}) collective-permute-start(bf16[64,384]{1,0:T(8,128)(2,1)S(1)} %copy-done.9), channel_id=1, source_target_pairs={{0,16},{16,32},{32,48},{48,0},{64,80},{80,96},{96,112},{112,64},{1... | collective-permute-start | bytes 147464 | tf_op jit(solution)/shard_map/ppermute | solution.py:135
  23.2 22.6 %collective-permute-start.1 = (bf16[64,384]{1,0:T(8,128)(2,1)S(1)}, bf16[64,384]{1,0:T(8,128)(2,1)S(1)}, u32[]{:S(2)}, u32[]{:S(2)}) collective-permute-start(bf16[64,384]{1,0:T(8,128)(2,1)S(1)} %copy-done.9), channel_id=1, source_target_pairs={{0,48},{16,0},{32,16},{48,32},{64,112},{80,64},{96,80},{112,96},{1... | collective-permute-start | bytes 147464 | tf_op jit(solution)/shard_map/ppermute | solution.py:135
  26.6 19.2 %collective-permute-start.2 = (bf16[64,384]{1,0:T(8,128)(2,1)S(1)}, bf16[64,384]{1,0:T(8,128)(2,1)S(1)}, u32[]{:S(2)}, u32[]{:S(2)}) collective-permute-start(bf16[64,384]{1,0:T(8,128)(2,1)S(1)} %copy-done.9), channel_id=1, source_target_pairs={{0,32},{16,48},{32,0},{48,16},{64,96},{80,112},{96,64},{112,80},{1... | collective-permute-start | bytes 147464 | tf_op jit(solution)/shard_map/ppermute | solution.py:135
  35.5 21.2 %copy-start.1 = (bf16[8,64,384]{2,1,0:T(8,128)(2,1)}, bf16[8,64,384]{2,1,0:T(8,128)(2,1)S(1)}, u32[]{:S(2)}) copy-start(bf16[8,64,384]{2,1,0:T(8,128)(2,1)S(1)} %all-to-all-done.g0) | copy-start | bytes 1179652
  36.3 19.0 %all-to-all-start.1 = ((bf16[8,64,384]{2,1,0:T(8,128)(2,1)}), bf16[8,64,384]{2,1,0:T(8,128)(2,1)S(1)}, u32[]{:S(2)}, u32[]{:S(2)}) async-start(bf16[8,64,384]{2,1,0:T(8,128)(2,1)} %broadcast_in_dim.34), calls=%async_computation.1 | async-start | bytes 786432 | tf_op jit(solution)/shard_map/all_to_all | solution.py:153
  39.9 12.0 %collective-permute-start.3 = (bf16[8,64,384]{2,1,0:T(8,128)(2,1)S(1)}, bf16[8,64,384]{2,1,0:T(8,128)(2,1)S(1)}, u32[]{:S(2)}, u32[]{:S(2)}) collective-permute-start(bf16[8,64,384]{2,1,0:T(8,128)(2,1)S(1)} %all-to-all-done.g0), channel_id=1, source_target_pairs={{0,16},{16,32},{32,48},{48,0},{64,80},{80,96},{96,112},{112,64},{1... | collective-permute-start | bytes 1179656 | tf_op jit(solution)/shard_map/ppermute | solution.py:135
  42.3 12.9 %collective-permute-start.4 = (bf16[8,64,384]{2,1,0:T(8,128)(2,1)S(1)}, bf16[8,64,384]{2,1,0:T(8,128)(2,1)S(1)}, u32[]{:S(2)}, u32[]{:S(2)}) collective-permute-start(bf16[8,64,384]{2,1,0:T(8,128)(2,1)S(1)} %all-to-all-done.g0), channel_id=1, source_target_pairs={{0,48},{16,0},{32,16},{48,32},{64,112},{80,64},{96,80},{112,96},{1... | collective-permute-start | bytes 1179656 | tf_op jit(solution)/shard_map/ppermute | solution.py:135
  51.9 13.9 %copy-start.3 = (bf16[8,64,384]{2,1,0:T(8,128)(2,1)}, bf16[8,64,384]{2,1,0:T(8,128)(2,1)S(1)}, u32[]{:S(2)}) copy-start(bf16[8,64,384]{2,1,0:T(8,128)(2,1)S(1)} %collective-permute-done.3.g1) | copy-start | bytes 1179652
  55.3 15.4 %copy-start.2 = (bf16[8,64,384]{2,1,0:T(8,128)(2,1)}, bf16[8,64,384]{2,1,0:T(8,128)(2,1)S(1)}, u32[]{:S(2)}) copy-start(bf16[8,64,384]{2,1,0:T(8,128)(2,1)S(1)} %all-to-all-done.1.u0) | copy-start | bytes 1179652
  56.7 44.7 %all-to-all-start.2 = ((bf16[8,4,64,384]{3,2,1,0:T(8,128)(2,1)}), bf16[8,4,64,384]{3,2,1,0:T(8,128)(2,1)S(1)}, u32[]{:S(2)}, u32[]{:S(2)}) async-start(bf16[8,4,64,384]{3,2,1,0:T(8,128)(2,1)} %broadcast_in_dim.40), calls=%async_computation.2 | async-start | bytes 3145728 | tf_op jit(solution)/shard_map/all_to_all | solution.py:153
  63.6 61.7 %reduce-scatter.2.cloned.1.call-start = ((), (), s32[]{:S(2)}) async-start(), calls=%async_computation.6 | async-start | bytes 1966080 | tf_op jit(solution)/shard_map/reduce_scatter | solution.py:227
  63.6 11.6 %collective-permute-start.7 = (bf16[8,64,384]{2,1,0:T(8,128)(2,1)S(1)}, bf16[8,64,384]{2,1,0:T(8,128)(2,1)S(1)}, u32[]{:S(2)}, u32[]{:S(2)}) collective-permute-start(bf16[8,64,384]{2,1,0:T(8,128)(2,1)S(1)} %all-to-all-done.1.u0), channel_id=1, source_target_pairs={{0,48},{16,0},{32,16},{48,32},{64,112},{80,64},{96,80},{112,96},{1... | collective-permute-start | bytes 1179656 | tf_op jit(solution)/shard_map/ppermute | solution.py:135
  65.8 14.4 %collective-permute-start.5 = (bf16[8,64,384]{2,1,0:T(8,128)(2,1)S(1)}, bf16[8,64,384]{2,1,0:T(8,128)(2,1)S(1)}, u32[]{:S(2)}, u32[]{:S(2)}) collective-permute-start(bf16[8,64,384]{2,1,0:T(8,128)(2,1)S(1)} %collective-permute-done.3.g1), channel_id=1, source_target_pairs={{0,16},{16,32},{32,48},{48,0},{64,80},{80,96},{96,112},{112,64},{1... | collective-permute-start | bytes 1179656 | tf_op jit(solution)/shard_map/ppermute | solution.py:135
  70.7 14.7 %collective-permute-start.6 = (bf16[8,64,384]{2,1,0:T(8,128)(2,1)S(1)}, bf16[8,64,384]{2,1,0:T(8,128)(2,1)S(1)}, u32[]{:S(2)}, u32[]{:S(2)}) collective-permute-start(bf16[8,64,384]{2,1,0:T(8,128)(2,1)S(1)} %all-to-all-done.1.u0), channel_id=1, source_target_pairs={{0,16},{16,32},{32,48},{48,0},{64,80},{80,96},{96,112},{112,64},{1... | collective-permute-start | bytes 1179656 | tf_op jit(solution)/shard_map/ppermute | solution.py:135
  75.2 11.0 %collective-permute-start.8 = (bf16[8,64,384]{2,1,0:T(8,128)(2,1)S(1)}, bf16[8,64,384]{2,1,0:T(8,128)(2,1)}, u32[]{:S(2)}, u32[]{:S(2)}) collective-permute-start(bf16[8,64,384]{2,1,0:T(8,128)(2,1)S(1)} %collective-permute-done.7.u2), channel_id=1, source_target_pairs={{0,48},{16,0},{32,16},{48,32},{64,112},{80,64},{96,80},{112,96},{1... | collective-permute-start | bytes 1179656 | tf_op jit(solution)/shard_map/ppermute | solution.py:135
  109.2 4.4 %collective-permute-start.9 = (bf16[8,384,128]{2,1,0:T(8,128)(2,1)}, bf16[8,384,128]{2,1,0:T(8,128)(2,1)S(1)}, u32[]{:S(2)}, u32[]{:S(2)}) collective-permute-start(bf16[8,384,128]{2,1,0:T(8,128)(2,1)} %get-tuple-element.26), channel_id=1, source_target_pairs={{0,1},{1,0},{2,3},{3,2},{4,5},{5,4},{6,7},{7,6},{8,9},{9,8},{10,11... | collective-permute-start | bytes 2359304 | tf_op jit(solution)/shard_map/ppermute | solution.py:145
  115.9 34.0 %all-to-all-start.3 = ((bf16[8,384,128]{2,1,0:T(8,128)(2,1)}), bf16[8,384,128]{2,1,0:T(8,128)(2,1)S(1)}, u32[]{:S(2)}, u32[]{:S(2)}) async-start(bf16[8,384,128]{2,1,0:T(8,128)(2,1)} %add_convert_fusion), calls=%async_computation.3 | async-start | bytes 1572864 | tf_op jit(solution)/shard_map/all_to_all | solution.py:225
  126.2 7.8 %collective-permute-start.10 = (bf16[4,64,384]{2,1,0:T(8,128)(2,1)S(1)}, bf16[4,64,384]{2,1,0:T(8,128)(2,1)S(1)}, u32[]{:S(2)}, u32[]{:S(2)}) collective-permute-start(bf16[4,64,384]{2,1,0:T(8,128)(2,1)S(1)} %pad_maximum_fusion.1), channel_id=1, source_target_pairs={{0,64},{16,80},{32,96},{48,112},{64,0},{80,16},{96,32},{112,48},{1... | collective-permute-start | bytes 589832 | tf_op jit(solution)/shard_map/ppermute | solution.py:140
  134.9 7.5 %collective-permute-start.11 = (bf16[2,64,384]{2,1,0:T(8,128)(2,1)S(1)}, bf16[2,64,384]{2,1,0:T(8,128)(2,1)S(1)}, u32[]{:S(2)}, u32[]{:S(2)}) collective-permute-start(bf16[2,64,384]{2,1,0:T(8,128)(2,1)S(1)} %pad_maximum_fusion.2), channel_id=1, source_target_pairs={{0,128},{16,144},{32,160},{48,176},{64,192},{80,208},{96,224},{112... | collective-permute-start | bytes 294920 | tf_op jit(solution)/shard_map/ppermute | solution.py:140
  143.2 8.8 %collective-permute-start.12 = (bf16[64,384]{1,0:T(8,128)(2,1)S(1)}, bf16[64,384]{1,0:T(8,128)(2,1)S(1)}, u32[]{:S(2)}, u32[]{:S(2)}) collective-permute-start(bf16[64,384]{1,0:T(8,128)(2,1)S(1)} %fusion.2), channel_id=1, source_target_pairs={{0,384},{16,400},{32,416},{48,432},{64,448},{80,464},{96,480},{112... | collective-permute-start | bytes 147464 | tf_op jit(solution)/shard_map/ppermute | solution.py:140
  (5 other events, 14.4 us)
Sparse Core Ops, SparseCore 0:
  10.6 52.2 all-gather.1
  93.0 32.1 reduce-scatter.1

commit v8 on v7

--- a/solution.py
+++ b/solution.py
@@ -33,39 +33,31 @@
     return copies
 
 
-def gate_kernel(place, rows_ref, g0, g1, g2, g3, gate_out, tok, gate_full, row_sem, gate_sems):
-    count, n_feat = tok.shape
-    tok_copy = pltpu.make_async_copy(rows_ref.at[pl.ds(0, count)], tok, row_sem.at[0])
-    tok_copy.start()
-    gate_copies = copy_blocks((g0, g1, g2, g3), gate_full, gate_sems, place[0])
-    tok_copy.wait()
-    for copy in gate_copies:
-        copy.wait()
-    gate_out[...] = jnp.dot(
-        tok[...], gate_full[...].reshape(n_feat, -1), preferred_element_type=jnp.float32
-    )
-
-
 def forward_kernel(
-    place, rows_ref, u0, u1, u2, u3, gate_in, up_out, partial_out,
-    tok, cot, up_full, row_sems, up_sems,
+    place, rows_ref, g0, g1, g2, g3, u0, u1, u2, u3, gate_out, up_out, partial_out,
+    tok, cot, gate_full, up_full, row_sems, gate_sems, up_sems,
 ):
     count, n_feat = tok.shape
     tok_copy = pltpu.make_async_copy(rows_ref.at[pl.ds(0, count)], tok, row_sems.at[0])
     cot_copy = pltpu.make_async_copy(rows_ref.at[pl.ds(count, count)], cot, row_sems.at[1])
     tok_copy.start()
+    gate_copies = copy_blocks((g0, g1, g2, g3), gate_full, gate_sems, place[0])
     up_copies = copy_blocks((u0, u1, u2, u3), up_full, up_sems, place[0])
     cot_copy.start()
-    gate_value = gate_in[...]
-    silu = gate_value * jax.nn.sigmoid(gate_value)
     tok_copy.wait()
+    for copy in gate_copies:
+        copy.wait()
+    gate_value = jnp.dot(
+        tok[...], gate_full[...].reshape(n_feat, -1), preferred_element_type=jnp.float32
+    )
+    gate_out[...] = gate_value
     for copy in up_copies:
         copy.wait()
     up_value = jnp.dot(
         tok[...], up_full[...].reshape(n_feat, -1), preferred_element_type=jnp.float32
     )
     up_out[...] = up_value
-    hidden = (silu * up_value).astype(jnp.bfloat16)
+    hidden = (gate_value * jax.nn.sigmoid(gate_value) * up_value).astype(jnp.bfloat16)
     cot_copy.wait()
     partial_value = dot(cot[...], hidden, ((0,), (0,))).astype(jnp.bfloat16)
     depth = n_feat // (N_Z * N_X)
@@ -196,21 +188,13 @@
     full = pltpu.VMEM((N_Z, N_CORE, 2 * depth, cols), jnp.bfloat16)
     row_block = pltpu.VMEM((rows, n_feat), jnp.bfloat16)
     sems = pltpu.SemaphoreType.DMA
-    (gate_value,) = call_kernel(
-        gate_kernel,
-        5,
-        (place, both) + blocks[:4],
-        (value,),
-        [row_block, full, sems((1,)), sems((N_X,))],
-        2 * rows * n_feat * cols,
-    )
-    up_value, down_partial = call_kernel(
+    gate_value, up_value, down_partial = call_kernel(
         forward_kernel,
-        5,
-        (place, both) + blocks[4:] + (gate_value,),
-        (value, jax.ShapeDtypeStruct((N_X, N_Z, depth, cols), jnp.bfloat16)),
-        [row_block, row_block, full, sems((2,)), sems((N_X,))],
-        4 * rows * n_feat * cols,
+        9,
+        (place, both) + blocks,
+        (value, value, jax.ShapeDtypeStruct((N_X, N_Z, depth, cols), jnp.bfloat16)),
+        [row_block, row_block, full, full, sems((2,)), sems((N_X,)), sems((N_X,))],
+        6 * rows * n_feat * cols,
     )
     half = jax.ShapeDtypeStruct((N_Y, rows, width), jnp.bfloat16)
     other, mine = call_kernel(

time: 162 us -> 162 us (level)
  waiting for transfers between devices: 42.7 us -> 47.2 us
  Pallas kernels: 17.7 us -> 14.3 us
    ppermute x9, waiting for transfers between devices: 15.2 us -> 20.4 us  [send_x(): return lax.ppermute(value, 'fsdp', pairs)]
    pallas_call x3 -> x2, Pallas kernels: 17.7 us -> 14.3 us  [call_kernel(): pl.pallas_call(kernel, out_shape=out_shapes, in_specs=in_specs, out_specs...]
  transfers between devices with their start and end apart: 19 -> 19, of which waited for: 12 -> 12; matrix products, arithmetic and copies ran while one was open for 5% -> 5% of each run, Pallas kernels for 11% -> 9%
where the time goes in v8:
time: 162 us; the launch traced here: 160 us
  starting transfers between devices  70 us (43%)
  waiting for transfers between devices  47.2 us (29%)
  between operations  14.4 us (9%)
  Pallas kernels  14.3 us (9%)
  other arithmetic  8.49 us (5%)
  local copies, waits for them, and re-layouts  6.09 us (4%)
    ppermute x9, starting transfers between devices, send_x(): return lax.ppermute(value, 'fsdp', pairs)  25.9 us
    all_to_all x3, starting transfers between devices, gather_z(): return lax.all_to_all(copies, 'fsdp', 0, 0, axis_index_groups=Z_GROUPS)  20.6 us
    ppermute x9, waiting for transfers between devices, send_x(): return lax.ppermute(value, 'fsdp', pairs)  20.4 us
    ppermute x3, starting transfers between devices, swap_z(): return lax.ppermute(value, 'fsdp', pairs)  14.5 us
    pallas_call x2, Pallas kernels, call_kernel(): pl.pallas_call(kernel, out_shape=out_shapes, in_specs=in_specs, out_specs...  14.3 us
    all_to_all x3, waiting for transfers between devices, gather_z(): return lax.all_to_all(copies, 'fsdp', 0, 0, axis_index_groups=Z_GROUPS)  13 us
    ppermute x3, waiting for transfers between devices, swap_z(): return lax.ppermute(value, 'fsdp', pairs)  8.78 us
    all_to_all x1, starting transfers between devices, on_device(): summed = lax.all_to_all(pair_sum, 'mp', 0, 0, axis_index_groups=Y_GROUPS)  7.02 us
  transfers between devices with their start and end apart: 19, of which 12 were waited for; matrix products, arithmetic and copies ran while one was open for 5% of the time, Pallas kernels for 9%

profile of v8, /device:TPU:6, one launch (start us, length us, event | category | flops | bytes accessed | tf_op | source)
XLA Modules:
  0.0 160.5 jit_solution(558042782589922615)
XLA Ops:
  10.5 10.3 %all-to-all-start = ((bf16[8,64,384]{2,1,0:T(8,128)(2,1)}), bf16[8,64,384]{2,1,0:T(8,128)(2,1)S(1)}, u32[]{:S(2)}, u32[]{:S(2)}) async-start(bf16[8,64,384]{2,1,0:T(8,128)(2,1)} %broadcast_in_dim.16), calls=%async_computation | async-start | bytes 786432 | tf_op jit(solution)/shard_map/all_to_all | solution.py:145
  23.2 3.5 %collective-permute-start.1 = (bf16[64,384]{1,0:T(8,128)(2,1)S(1)}, bf16[64,384]{1,0:T(8,128)(2,1)S(1)}, u32[]{:S(2)}, u32[]{:S(2)}) collective-permute-start(bf16[64,384]{1,0:T(8,128)(2,1)S(1)} %copy-done.9), channel_id=1, source_target_pairs={{0,48},{16,0},{32,16},{48,32},{64,112},{80,64},{96,80},{112,96},{1... | collective-permute-start | bytes 147464 | tf_op jit(solution)/shard_map/ppermute | solution.py:127
  26.6 3.3 %collective-permute-start.2 = (bf16[64,384]{1,0:T(8,128)(2,1)S(1)}, bf16[64,384]{1,0:T(8,128)(2,1)S(1)}, u32[]{:S(2)}, u32[]{:S(2)}) collective-permute-start(bf16[64,384]{1,0:T(8,128)(2,1)S(1)} %copy-done.9), channel_id=1, source_target_pairs={{0,32},{16,48},{32,0},{48,16},{64,96},{80,112},{96,64},{112,80},{1... | collective-permute-start | bytes 147464 | tf_op jit(solution)/shard_map/ppermute | solution.py:127
  30.0 5.5 %all-to-all-done.g0 = bf16[8,64,384]{2,1,0:T(8,128)(2,1)S(1)} async-done(((bf16[8,64,384]{2,1,0:T(8,128)(2,1)}), bf16[8,64,384]{2,1,0:T(8,128)(2,1)S(1)}, u32[]{:S(2)}, u32[]{:S(2)}) %all-to-all-start) | async-done | bytes 393248 | tf_op jit(solution)/shard_map/all_to_all | solution.py:145
  36.3 3.5 %all-to-all-start.1 = ((bf16[8,64,384]{2,1,0:T(8,128)(2,1)}), bf16[8,64,384]{2,1,0:T(8,128)(2,1)S(1)}, u32[]{:S(2)}, u32[]{:S(2)}) async-start(bf16[8,64,384]{2,1,0:T(8,128)(2,1)} %broadcast_in_dim.34), calls=%async_computation.1 | async-start | bytes 786432 | tf_op jit(solution)/shard_map/all_to_all | solution.py:145
  39.9 2.4 %collective-permute-start.3 = (bf16[8,64,384]{2,1,0:T(8,128)(2,1)S(1)}, bf16[8,64,384]{2,1,0:T(8,128)(2,1)S(1)}, u32[]{:S(2)}, u32[]{:S(2)}) collective-permute-start(bf16[8,64,384]{2,1,0:T(8,128)(2,1)S(1)} %all-to-all-done.g0), channel_id=1, source_target_pairs={{0,16},{16,32},{32,48},{48,0},{64,80},{80,96},{96,112},{112,64},{1... | collective-permute-start | bytes 1179656 | tf_op jit(solution)/shard_map/ppermute | solution.py:127
  42.3 3.4 %collective-permute-start.4 = (bf16[8,64,384]{2,1,0:T(8,128)(2,1)S(1)}, bf16[8,64,384]{2,1,0:T(8,128)(2,1)S(1)}, u32[]{:S(2)}, u32[]{:S(2)}) collective-permute-start(bf16[8,64,384]{2,1,0:T(8,128)(2,1)S(1)} %all-to-all-done.g0), channel_id=1, source_target_pairs={{0,48},{16,0},{32,16},{48,32},{64,112},{80,64},{96,80},{112,96},{1... | collective-permute-start | bytes 1179656 | tf_op jit(solution)/shard_map/ppermute | solution.py:127
  45.9 6.1 %collective-permute-done.3.g1 = bf16[8,64,384]{2,1,0:T(8,128)(2,1)S(1)} collective-permute-done((bf16[8,64,384]{2,1,0:T(8,128)(2,1)S(1)}, bf16[8,64,384]{2,1,0:T(8,128)(2,1)S(1)}, u32[]{:S(2)}, u32[]{:S(2)}) %collective-permute-start.3) | collective-permute-done | bytes 393248 | tf_op jit(solution)/shard_map/ppermute | solution.py:127
  51.9 3.4 %collective-permute-done.4.g2 = bf16[8,64,384]{2,1,0:T(8,128)(2,1)S(1)} collective-permute-done((bf16[8,64,384]{2,1,0:T(8,128)(2,1)S(1)}, bf16[8,64,384]{2,1,0:T(8,128)(2,1)S(1)}, u32[]{:S(2)}, u32[]{:S(2)}) %collective-permute-start.4) | collective-permute-done | bytes 393248 | tf_op jit(solution)/shard_map/ppermute | solution.py:127
  56.7 6.8 %all-to-all-start.2 = ((bf16[8,4,64,384]{3,2,1,0:T(8,128)(2,1)}), bf16[8,4,64,384]{3,2,1,0:T(8,128)(2,1)S(1)}, u32[]{:S(2)}, u32[]{:S(2)}) async-start(bf16[8,4,64,384]{3,2,1,0:T(8,128)(2,1)} %broadcast_in_dim.40), calls=%async_computation.2 | async-start | bytes 3145728 | tf_op jit(solution)/shard_map/all_to_all | solution.py:145
  65.8 4.8 %collective-permute-start.6 = (bf16[8,64,384]{2,1,0:T(8,128)(2,1)S(1)}, bf16[8,64,384]{2,1,0:T(8,128)(2,1)S(1)}, u32[]{:S(2)}, u32[]{:S(2)}) collective-permute-start(bf16[8,64,384]{2,1,0:T(8,128)(2,1)S(1)} %all-to-all-done.1.u0), channel_id=1, source_target_pairs={{0,16},{16,32},{32,48},{48,0},{64,80},{80,96},{96,112},{112,64},{1... | collective-permute-start | bytes 1179656 | tf_op jit(solution)/shard_map/ppermute | solution.py:127
  72.6 2.6 %collective-permute-done.7.u2 = bf16[8,64,384]{2,1,0:T(8,128)(2,1)S(1)} collective-permute-done((bf16[8,64,384]{2,1,0:T(8,128)(2,1)S(1)}, bf16[8,64,384]{2,1,0:T(8,128)(2,1)S(1)}, u32[]{:S(2)}, u32[]{:S(2)}) %collective-permute-start.7) | collective-permute-done | bytes 393248 | tf_op jit(solution)/shard_map/ppermute | solution.py:127
  77.8 7.0 %collective-permute-done.5.g3 = bf16[8,64,384]{2,1,0:T(8,128)(2,1)S(1)} collective-permute-done((bf16[8,64,384]{2,1,0:T(8,128)(2,1)S(1)}, bf16[8,64,384]{2,1,0:T(8,128)(2,1)S(1)}, u32[]{:S(2)}, u32[]{:S(2)}) %collective-permute-start.5) | collective-permute-done | bytes 393248 | tf_op jit(solution)/shard_map/ppermute | solution.py:127
  86.2 7.7 %shard_map.68 = (f32[384,384]{1,0:T(8,128)}, f32[384,384]{1,0:T(8,128)}, bf16[4,8,64,384]{3,2,1,0:T(8,128)(2,1)}) custom-call(s32[2]{0:T(128)} %pad_add_fusion.place, bf16[768,2048]{1,0:T(8,128)(2,1)} %all-gather.2.cloned.1.call-done.rows_ref, bf16[8,64,384]{2,1,0:T(8,128)(2,1)} %copy-done.1, bf16[8,64,384]{2,1,0:T(8,128)(2,1)} %copy-done.3, ...), custom_call_target="tpu_custom_call" | custom-call | flops 1811939328 | bytes 10000000 | tf_op jit(solution)/shard_map/pallas_call | solution.py:112
  93.9 7.5 %all-to-all-done.2 = bf16[8,4,64,384]{3,2,1,0:T(8,128)(2,1)S(1)} async-done(((bf16[8,4,64,384]{3,2,1,0:T(8,128)(2,1)}), bf16[8,4,64,384]{3,2,1,0:T(8,128)(2,1)S(1)}, u32[]{:S(2)}, u32[]{:S(2)}) %all-to-all-start.2) | async-done | bytes 1572896 | tf_op jit(solution)/shard_map/all_to_all | solution.py:145
  102.6 6.6 %shard_map.69 = (bf16[8,384,128]{2,1,0:T(8,128)(2,1)}, bf16[8,384,128]{2,1,0:T(8,128)(2,1)}) custom-call(s32[2]{0:T(128)} %pad_add_fusion.place, bf16[768,2048]{1,0:T(8,128)(2,1)} %all-gather.2.cloned.1.call-done.rows_ref, bf16[8,2,128,384]{3,2,1,0:T(8,128)(2,1)} %bitcast.21, bf16[8,64,384]{2,1,0:T(8,128)(2,1)} %copy-done.1, bf16[8,64,384]{2,1,0:T(8,128)(2,1)} %copy-done.3, ...), custom_call_target="tpu_custom_call" | custom-call | flops 1811939328 | bytes 10000000 | tf_op jit(solution)/shard_map/pallas_call | solution.py:112
  111.2 2.5 %collective-permute-done.9 = bf16[8,384,128]{2,1,0:T(8,128)(2,1)S(1)} collective-permute-done((bf16[8,384,128]{2,1,0:T(8,128)(2,1)}, bf16[8,384,128]{2,1,0:T(8,128)(2,1)S(1)}, u32[]{:S(2)}, u32[]{:S(2)}) %collective-permute-start.9) | collective-permute-done | bytes 786464 | tf_op jit(solution)/shard_map/ppermute | solution.py:137
  115.9 7.0 %all-to-all-start.3 = ((bf16[8,384,128]{2,1,0:T(8,128)(2,1)}), bf16[8,384,128]{2,1,0:T(8,128)(2,1)S(1)}, u32[]{:S(2)}, u32[]{:S(2)}) async-start(bf16[8,384,128]{2,1,0:T(8,128)(2,1)} %add_convert_fusion), calls=%async_computation.3 | async-start | bytes 1572864 | tf_op jit(solution)/shard_map/all_to_all | solution.py:209
  122.9 2.5 %reduce-scatter.2.cloned.1.call-done = bf16[512,384]{1,0:T(8,128)(2,1)} async-done(((bf16[2048,384]{1,0:T(8,128)(2,1)}), bf16[512,384]{1,0:T(8,128)(2,1)}) %reduce-scatter.2.cloned.1.call-update) | async-done | bytes 393232 | tf_op jit(solution)/shard_map/reduce_scatter | solution.py:211
  126.4 3.1 %collective-permute-start.10 = (bf16[4,64,384]{2,1,0:T(8,128)(2,1)S(1)}, bf16[4,64,384]{2,1,0:T(8,128)(2,1)S(1)}, u32[]{:S(2)}, u32[]{:S(2)}) collective-permute-start(bf16[4,64,384]{2,1,0:T(8,128)(2,1)S(1)} %pad_maximum_fusion.1), channel_id=1, source_target_pairs={{0,64},{16,80},{32,96},{48,112},{64,0},{80,16},{96,32},{112,48},{1... | collective-permute-start | bytes 589832 | tf_op jit(solution)/shard_map/ppermute | solution.py:132
  129.5 4.7 %collective-permute-done.10 = bf16[4,64,384]{2,1,0:T(8,128)(2,1)S(1)} collective-permute-done((bf16[4,64,384]{2,1,0:T(8,128)(2,1)S(1)}, bf16[4,64,384]{2,1,0:T(8,128)(2,1)S(1)}, u32[]{:S(2)}, u32[]{:S(2)}) %collective-permute-start.10) | collective-permute-done | bytes 196640 | tf_op jit(solution)/shard_map/ppermute | solution.py:132
  135.1 4.7 %collective-permute-start.11 = (bf16[2,64,384]{2,1,0:T(8,128)(2,1)S(1)}, bf16[2,64,384]{2,1,0:T(8,128)(2,1)S(1)}, u32[]{:S(2)}, u32[]{:S(2)}) collective-permute-start(bf16[2,64,384]{2,1,0:T(8,128)(2,1)S(1)} %pad_maximum_fusion.2), channel_id=1, source_target_pairs={{0,128},{16,144},{32,160},{48,176},{64,192},{80,208},{96,224},{112... | collective-permute-start | bytes 294920 | tf_op jit(solution)/shard_map/ppermute | solution.py:132
  139.8 2.8 %collective-permute-done.11 = bf16[2,64,384]{2,1,0:T(8,128)(2,1)S(1)} collective-permute-done((bf16[2,64,384]{2,1,0:T(8,128)(2,1)S(1)}, bf16[2,64,384]{2,1,0:T(8,128)(2,1)S(1)}, u32[]{:S(2)}, u32[]{:S(2)}) %collective-permute-start.11) | collective-permute-done | bytes 98336 | tf_op jit(solution)/shard_map/ppermute | solution.py:132
  143.4 6.7 %collective-permute-start.12 = (bf16[64,384]{1,0:T(8,128)(2,1)S(1)}, bf16[64,384]{1,0:T(8,128)(2,1)S(1)}, u32[]{:S(2)}, u32[]{:S(2)}) collective-permute-start(bf16[64,384]{1,0:T(8,128)(2,1)S(1)} %fusion.2), channel_id=1, source_target_pairs={{0,384},{16,400},{32,416},{48,432},{64,448},{80,464},{96,480},{112... | collective-permute-start | bytes 147464 | tf_op jit(solution)/shard_map/ppermute | solution.py:132
  (56 shorter events, 27.7 us)
Async XLA Ops:
  7.2 13.6 %copy-start.9 = (bf16[64,384]{1,0:T(8,128)(2,1)S(1)}, bf16[64,384]{1,0:T(8,128)(2,1)}, u32[]{:S(2)}) copy-start(bf16[64,384]{1,0:T(8,128)(2,1)} %param.9) | copy-start | bytes 147460
  7.2 28.3 %copy-start.8 = (bf16[64,384]{1,0:T(8,128)(2,1)S(1)}, bf16[64,384]{1,0:T(8,128)(2,1)}, u32[]{:S(2)}) copy-start(bf16[64,384]{1,0:T(8,128)(2,1)} %param.8) | copy-start | bytes 147460
  7.2 79.0 %all-gather.2.cloned.1.call-start = ((), (), s32[]{:S(2)}) async-start(), calls=%async_computation.5 | async-start | bytes 3342336 | tf_op jit(solution)/shard_map/all_gather | solution.py:165
  10.5 25.0 %all-to-all-start = ((bf16[8,64,384]{2,1,0:T(8,128)(2,1)}), bf16[8,64,384]{2,1,0:T(8,128)(2,1)S(1)}, u32[]{:S(2)}, u32[]{:S(2)}) async-start(bf16[8,64,384]{2,1,0:T(8,128)(2,1)} %broadcast_in_dim.16), calls=%async_computation | async-start | bytes 786432 | tf_op jit(solution)/shard_map/all_to_all | solution.py:145
  20.8 19.1 %collective-permute-start = (bf16[64,384]{1,0:T(8,128)(2,1)S(1)}, bf16[64,384]{1,0:T(8,128)(2,1)S(1)}, u32[]{:S(2)}, u32[]{:S(2)}) collective-permute-start(bf16[64,384]{1,0:T(8,128)(2,1)S(1)} %copy-done.9), channel_id=1, source_target_pairs={{0,16},{16,32},{32,48},{48,0},{64,80},{80,96},{96,112},{112,64},{1... | collective-permute-start | bytes 147464 | tf_op jit(solution)/shard_map/ppermute | solution.py:127
  23.2 22.6 %collective-permute-start.1 = (bf16[64,384]{1,0:T(8,128)(2,1)S(1)}, bf16[64,384]{1,0:T(8,128)(2,1)S(1)}, u32[]{:S(2)}, u32[]{:S(2)}) collective-permute-start(bf16[64,384]{1,0:T(8,128)(2,1)S(1)} %copy-done.9), channel_id=1, source_target_pairs={{0,48},{16,0},{32,16},{48,32},{64,112},{80,64},{96,80},{112,96},{1... | collective-permute-start | bytes 147464 | tf_op jit(solution)/shard_map/ppermute | solution.py:127
  26.6 19.2 %collective-permute-start.2 = (bf16[64,384]{1,0:T(8,128)(2,1)S(1)}, bf16[64,384]{1,0:T(8,128)(2,1)S(1)}, u32[]{:S(2)}, u32[]{:S(2)}) collective-permute-start(bf16[64,384]{1,0:T(8,128)(2,1)S(1)} %copy-done.9), channel_id=1, source_target_pairs={{0,32},{16,48},{32,0},{48,16},{64,96},{80,112},{96,64},{112,80},{1... | collective-permute-start | bytes 147464 | tf_op jit(solution)/shard_map/ppermute | solution.py:127
  35.5 21.2 %copy-start.1 = (bf16[8,64,384]{2,1,0:T(8,128)(2,1)}, bf16[8,64,384]{2,1,0:T(8,128)(2,1)S(1)}, u32[]{:S(2)}) copy-start(bf16[8,64,384]{2,1,0:T(8,128)(2,1)S(1)} %all-to-all-done.g0) | copy-start | bytes 1179652
  36.3 19.0 %all-to-all-start.1 = ((bf16[8,64,384]{2,1,0:T(8,128)(2,1)}), bf16[8,64,384]{2,1,0:T(8,128)(2,1)S(1)}, u32[]{:S(2)}, u32[]{:S(2)}) async-start(bf16[8,64,384]{2,1,0:T(8,128)(2,1)} %broadcast_in_dim.34), calls=%async_computation.1 | async-start | bytes 786432 | tf_op jit(solution)/shard_map/all_to_all | solution.py:145
  39.9 12.0 %collective-permute-start.3 = (bf16[8,64,384]{2,1,0:T(8,128)(2,1)S(1)}, bf16[8,64,384]{2,1,0:T(8,128)(2,1)S(1)}, u32[]{:S(2)}, u32[]{:S(2)}) collective-permute-start(bf16[8,64,384]{2,1,0:T(8,128)(2,1)S(1)} %all-to-all-done.g0), channel_id=1, source_target_pairs={{0,16},{16,32},{32,48},{48,0},{64,80},{80,96},{96,112},{112,64},{1... | collective-permute-start | bytes 1179656 | tf_op jit(solution)/shard_map/ppermute | solution.py:127
  42.3 12.9 %collective-permute-start.4 = (bf16[8,64,384]{2,1,0:T(8,128)(2,1)S(1)}, bf16[8,64,384]{2,1,0:T(8,128)(2,1)S(1)}, u32[]{:S(2)}, u32[]{:S(2)}) collective-permute-start(bf16[8,64,384]{2,1,0:T(8,128)(2,1)S(1)} %all-to-all-done.g0), channel_id=1, source_target_pairs={{0,48},{16,0},{32,16},{48,32},{64,112},{80,64},{96,80},{112,96},{1... | collective-permute-start | bytes 1179656 | tf_op jit(solution)/shard_map/ppermute | solution.py:127
  51.9 18.8 %copy-start.3 = (bf16[8,64,384]{2,1,0:T(8,128)(2,1)}, bf16[8,64,384]{2,1,0:T(8,128)(2,1)S(1)}, u32[]{:S(2)}) copy-start(bf16[8,64,384]{2,1,0:T(8,128)(2,1)S(1)} %collective-permute-done.3.g1) | copy-start | bytes 1179652
  56.7 44.7 %all-to-all-start.2 = ((bf16[8,4,64,384]{3,2,1,0:T(8,128)(2,1)}), bf16[8,4,64,384]{3,2,1,0:T(8,128)(2,1)S(1)}, u32[]{:S(2)}, u32[]{:S(2)}) async-start(bf16[8,4,64,384]{3,2,1,0:T(8,128)(2,1)} %broadcast_in_dim.40), calls=%async_computation.2 | async-start | bytes 3145728 | tf_op jit(solution)/shard_map/all_to_all | solution.py:145
  63.6 61.9 %reduce-scatter.2.cloned.1.call-start = ((), (), s32[]{:S(2)}) async-start(), calls=%async_computation.6 | async-start | bytes 1966080 | tf_op jit(solution)/shard_map/reduce_scatter | solution.py:211
  63.6 11.6 %collective-permute-start.7 = (bf16[8,64,384]{2,1,0:T(8,128)(2,1)S(1)}, bf16[8,64,384]{2,1,0:T(8,128)(2,1)S(1)}, u32[]{:S(2)}, u32[]{:S(2)}) collective-permute-start(bf16[8,64,384]{2,1,0:T(8,128)(2,1)S(1)} %all-to-all-done.1.u0), channel_id=1, source_target_pairs={{0,48},{16,0},{32,16},{48,32},{64,112},{80,64},{96,80},{112,96},{1... | collective-permute-start | bytes 1179656 | tf_op jit(solution)/shard_map/ppermute | solution.py:127
  65.8 19.0 %collective-permute-start.6 = (bf16[8,64,384]{2,1,0:T(8,128)(2,1)S(1)}, bf16[8,64,384]{2,1,0:T(8,128)(2,1)S(1)}, u32[]{:S(2)}, u32[]{:S(2)}) collective-permute-start(bf16[8,64,384]{2,1,0:T(8,128)(2,1)S(1)} %all-to-all-done.1.u0), channel_id=1, source_target_pairs={{0,16},{16,32},{32,48},{48,0},{64,80},{80,96},{96,112},{112,64},{1... | collective-permute-start | bytes 1179656 | tf_op jit(solution)/shard_map/ppermute | solution.py:127
  70.7 14.1 %collective-permute-start.5 = (bf16[8,64,384]{2,1,0:T(8,128)(2,1)S(1)}, bf16[8,64,384]{2,1,0:T(8,128)(2,1)S(1)}, u32[]{:S(2)}, u32[]{:S(2)}) collective-permute-start(bf16[8,64,384]{2,1,0:T(8,128)(2,1)S(1)} %collective-permute-done.3.g1), channel_id=1, source_target_pairs={{0,16},{16,32},{32,48},{48,0},{64,80},{80,96},{96,112},{112,64},{1... | collective-permute-start | bytes 1179656 | tf_op jit(solution)/shard_map/ppermute | solution.py:127
  75.2 11.0 %copy-start.5 = (bf16[8,64,384]{2,1,0:T(8,128)(2,1)}, bf16[8,64,384]{2,1,0:T(8,128)(2,1)S(1)}, u32[]{:S(2)}) copy-start(bf16[8,64,384]{2,1,0:T(8,128)(2,1)S(1)} %collective-permute-done.7.u2) | copy-start | bytes 1179652
  75.2 11.0 %collective-permute-start.8 = (bf16[8,64,384]{2,1,0:T(8,128)(2,1)S(1)}, bf16[8,64,384]{2,1,0:T(8,128)(2,1)}, u32[]{:S(2)}, u32[]{:S(2)}) collective-permute-start(bf16[8,64,384]{2,1,0:T(8,128)(2,1)S(1)} %collective-permute-done.7.u2), channel_id=1, source_target_pairs={{0,48},{16,0},{32,16},{48,32},{64,112},{80,64},{96,80},{112,96},{1... | collective-permute-start | bytes 1179656 | tf_op jit(solution)/shard_map/ppermute | solution.py:127
  109.2 4.4 %collective-permute-start.9 = (bf16[8,384,128]{2,1,0:T(8,128)(2,1)}, bf16[8,384,128]{2,1,0:T(8,128)(2,1)S(1)}, u32[]{:S(2)}, u32[]{:S(2)}) collective-permute-start(bf16[8,384,128]{2,1,0:T(8,128)(2,1)} %get-tuple-element.28), channel_id=1, source_target_pairs={{0,1},{1,0},{2,3},{3,2},{4,5},{5,4},{6,7},{7,6},{8,9},{9,8},{10,11... | collective-permute-start | bytes 2359304 | tf_op jit(solution)/shard_map/ppermute | solution.py:137
  115.9 34.2 %all-to-all-start.3 = ((bf16[8,384,128]{2,1,0:T(8,128)(2,1)}), bf16[8,384,128]{2,1,0:T(8,128)(2,1)S(1)}, u32[]{:S(2)}, u32[]{:S(2)}) async-start(bf16[8,384,128]{2,1,0:T(8,128)(2,1)} %add_convert_fusion), calls=%async_computation.3 | async-start | bytes 1572864 | tf_op jit(solution)/shard_map/all_to_all | solution.py:209
  126.4 7.8 %collective-permute-start.10 = (bf16[4,64,384]{2,1,0:T(8,128)(2,1)S(1)}, bf16[4,64,384]{2,1,0:T(8,128)(2,1)S(1)}, u32[]{:S(2)}, u32[]{:S(2)}) collective-permute-start(bf16[4,64,384]{2,1,0:T(8,128)(2,1)S(1)} %pad_maximum_fusion.1), channel_id=1, source_target_pairs={{0,64},{16,80},{32,96},{48,112},{64,0},{80,16},{96,32},{112,48},{1... | collective-permute-start | bytes 589832 | tf_op jit(solution)/shard_map/ppermute | solution.py:132
  135.1 7.5 %collective-permute-start.11 = (bf16[2,64,384]{2,1,0:T(8,128)(2,1)S(1)}, bf16[2,64,384]{2,1,0:T(8,128)(2,1)S(1)}, u32[]{:S(2)}, u32[]{:S(2)}) collective-permute-start(bf16[2,64,384]{2,1,0:T(8,128)(2,1)S(1)} %pad_maximum_fusion.2), channel_id=1, source_target_pairs={{0,128},{16,144},{32,160},{48,176},{64,192},{80,208},{96,224},{112... | collective-permute-start | bytes 294920 | tf_op jit(solution)/shard_map/ppermute | solution.py:132
  143.4 8.7 %collective-permute-start.12 = (bf16[64,384]{1,0:T(8,128)(2,1)S(1)}, bf16[64,384]{1,0:T(8,128)(2,1)S(1)}, u32[]{:S(2)}, u32[]{:S(2)}) collective-permute-start(bf16[64,384]{1,0:T(8,128)(2,1)S(1)} %fusion.2), channel_id=1, source_target_pairs={{0,384},{16,400},{32,416},{48,432},{64,448},{80,464},{96,480},{112... | collective-permute-start | bytes 147464 | tf_op jit(solution)/shard_map/ppermute | solution.py:132
  (5 other events, 15.9 us)
Sparse Core Ops, SparseCore 0:
  10.6 52.2 all-gather.1
  94.0 31.3 reduce-scatter.1

commit v9 on v8

--- a/solution.py
+++ b/solution.py
@@ -12,12 +12,19 @@
 N_Y = 8
 N_CORE = 2
 Z_GROUPS = [[z * N_X + x for z in range(N_Z)] for x in range(N_X)]
-X_GROUPS = [[z * N_X + x for x in range(N_X)] for z in range(N_Z)]
+PAIR_GROUPS = [
+    [z * N_X + x for x in range(N_X)] + [(z + 1) * N_X + x for x in reversed(range(N_X))]
+    for z in range(0, N_Z, 2)
+]
 Y_GROUPS = [[y * N_CORE + c for y in range(N_Y)] for c in range(N_CORE)]
 
 
 def dot(left, right, dims):
     return lax.dot_general(left, right, (dims, ((), ())), preferred_element_type=jnp.float32)
+
+
+def pair_place(odd, x):
+    return 2 * N_X - 1 - x if odd else x
 
 
 def copy_blocks(blocks, full, sems, me_x):
@@ -64,7 +71,7 @@
     for z in range(N_Z):
         for x in range(N_X):
             row = (z * N_X + x) * depth
-            partial_out[x, z] = partial_value[row : row + depth]
+            partial_out[pair_place(z % 2, x), z // 2] = partial_value[row : row + depth]
 
 
 def backward_kernel(
@@ -192,7 +199,7 @@
         forward_kernel,
         9,
         (place, both) + blocks,
-        (value, value, jax.ShapeDtypeStruct((N_X, N_Z, depth, cols), jnp.bfloat16)),
+        (value, value, jax.ShapeDtypeStruct((2 * N_X, N_Z // 2, depth, cols), jnp.bfloat16)),
         [row_block, row_block, full, full, sems((2,)), sems((N_X,)), sems((N_X,))],
         6 * rows * n_feat * cols,
     )
@@ -208,19 +215,17 @@
     pair_sum = add(mine, send_core(other)).astype(jnp.bfloat16)
     summed = lax.all_to_all(pair_sum, "mp", 0, 0, axis_index_groups=Y_GROUPS)
 
-    down_x = lax.psum_scatter(
+    down_pair = lax.psum_scatter(
         down_partial.reshape(n_feat, cols),
         "fsdp",
         scatter_dimension=0,
-        axis_index_groups=X_GROUPS,
+        axis_index_groups=PAIR_GROUPS,
         tiled=True,
-    ).reshape(N_Z, depth, cols)
-    block = lambda flip: lax.dynamic_index_in_dim(down_x, me_z ^ flip, 0, False)
-    got = swap_z(jnp.stack([block(1 ^ flip) for flip in (0, 2, 6, 4)]), 1)
-    mine_0, mine_2, mine_6, mine_4 = (add(block(f), got[i]) for i, f in enumerate((0, 2, 6, 4)))
-    got = swap_z(jnp.stack([mine_2, mine_4]).astype(jnp.bfloat16), 2)
-    got_last = swap_z((mine_6 + got[1].astype(jnp.float32)).astype(jnp.bfloat16), 6)
-    down_sum = mine_0 + got[0].astype(jnp.float32) + got_last.astype(jnp.float32)
+    ).reshape(N_Z // 2, depth, cols)
+    block = lambda flip: lax.dynamic_index_in_dim(down_pair, (me_z // 2) ^ (flip // 2), 0, False)
+    got = swap_z(jnp.stack([block(2), block(4)]), 2)
+    got_last = swap_z(add(block(6), got[1]).astype(jnp.bfloat16), 6)
+    down_sum = add(block(0), got[0]) + got_last.astype(jnp.float32)
     grad_down = (down_sum * factor).astype(jnp.bfloat16)
     input_grad = summed.astype(jnp.float32).sum(0).astype(jnp.bfloat16)
     return (input_grad, grad_down)

time: 162 us -> 162 us (level)
  waiting for transfers between devices: 47.2 us -> 52.9 us
  starting transfers between devices: 70 us -> 65 us
    reduce_scatter x1, waiting for transfers between devices: 2.5 us -> 10.6 us  [on_device(): lax.psum_scatter(down_partial.reshape(n_feat, cols), 'fsdp', scatter_dime...]
    ppermute x3 -> x2, starting transfers between devices: 14.5 us -> 9.45 us  [swap_z(): return lax.ppermute(value, 'fsdp', pairs)]
    ppermute x3 -> x2, waiting for transfers between devices: 8.78 us -> 6.36 us  [swap_z(): return lax.ppermute(value, 'fsdp', pairs)]
  transfers between devices with their start and end apart: 19 -> 18, of which waited for: 12 -> 11; matrix products, arithmetic and copies ran while one was open for 5% -> 5% of each run, Pallas kernels for 9% -> 9%
where the time goes in v9:
time: 162 us; the launch traced here: 160 us
  starting transfers between devices  65 us (40%)
  waiting for transfers between devices  52.9 us (33%)
  between operations  14.4 us (9%)
  Pallas kernels  14.3 us (9%)
  other arithmetic  7.51 us (5%)
  local copies, waits for them, and re-layouts  6.1 us (4%)
    ppermute x9, starting transfers between devices, send_x(): return lax.ppermute(value, 'fsdp', pairs)  25.9 us
    all_to_all x3, starting transfers between devices, gather_z(): return lax.all_to_all(copies, 'fsdp', 0, 0, axis_index_groups=Z_GROUPS)  20.6 us
    ppermute x9, waiting for transfers between devices, send_x(): return lax.ppermute(value, 'fsdp', pairs)  20.4 us
    pallas_call x2, Pallas kernels, call_kernel(): pl.pallas_call(kernel, out_shape=out_shapes, in_specs=in_specs, out_specs...  14.3 us
    all_to_all x3, waiting for transfers between devices, gather_z(): return lax.all_to_all(copies, 'fsdp', 0, 0, axis_index_groups=Z_GROUPS)  13 us
    reduce_scatter x1, waiting for transfers between devices, on_device(): lax.psum_scatter(down_partial.reshape(n_feat, cols), 'fsdp', scatter_dime...  10.6 us
    ppermute x2, starting transfers between devices, swap_z(): return lax.ppermute(value, 'fsdp', pairs)  9.45 us
    all_to_all x1, starting transfers between devices, on_device(): summed = lax.all_to_all(pair_sum, 'mp', 0, 0, axis_index_groups=Y_GROUPS)  7.05 us
  transfers between devices with their start and end apart: 18, of which 11 were waited for; matrix products, arithmetic and copies ran while one was open for 5% of the time, Pallas kernels for 9%

profile of v9, /device:TPU:6, one launch (start us, length us, event | category | flops | bytes accessed | tf_op | source)
XLA Modules:
  0.0 160.2 jit_solution(12218458980537661519)
XLA Ops:
  10.5 10.3 %all-to-all-start = ((bf16[8,64,384]{2,1,0:T(8,128)(2,1)}), bf16[8,64,384]{2,1,0:T(8,128)(2,1)S(1)}, u32[]{:S(2)}, u32[]{:S(2)}) async-start(bf16[8,64,384]{2,1,0:T(8,128)(2,1)} %broadcast_in_dim.16), calls=%async_computation | async-start | bytes 786432 | tf_op jit(solution)/shard_map/all_to_all | solution.py:152
  20.8 2.4 %collective-permute-start = (bf16[64,384]{1,0:T(8,128)(2,1)S(1)}, bf16[64,384]{1,0:T(8,128)(2,1)S(1)}, u32[]{:S(2)}, u32[]{:S(2)}) collective-permute-start(bf16[64,384]{1,0:T(8,128)(2,1)S(1)} %copy-done.9), channel_id=1, source_target_pairs={{0,16},{16,32},{32,48},{48,0},{64,80},{80,96},{96,112},{112,64},{1... | collective-permute-start | bytes 147464 | tf_op jit(solution)/shard_map/ppermute | solution.py:134
  23.2 3.5 %collective-permute-start.1 = (bf16[64,384]{1,0:T(8,128)(2,1)S(1)}, bf16[64,384]{1,0:T(8,128)(2,1)S(1)}, u32[]{:S(2)}, u32[]{:S(2)}) collective-permute-start(bf16[64,384]{1,0:T(8,128)(2,1)S(1)} %copy-done.9), channel_id=1, source_target_pairs={{0,48},{16,0},{32,16},{48,32},{64,112},{80,64},{96,80},{112,96},{1... | collective-permute-start | bytes 147464 | tf_op jit(solution)/shard_map/ppermute | solution.py:134
  26.7 3.3 %collective-permute-start.2 = (bf16[64,384]{1,0:T(8,128)(2,1)S(1)}, bf16[64,384]{1,0:T(8,128)(2,1)S(1)}, u32[]{:S(2)}, u32[]{:S(2)}) collective-permute-start(bf16[64,384]{1,0:T(8,128)(2,1)S(1)} %copy-done.9), channel_id=1, source_target_pairs={{0,32},{16,48},{32,0},{48,16},{64,96},{80,112},{96,64},{112,80},{1... | collective-permute-start | bytes 147464 | tf_op jit(solution)/shard_map/ppermute | solution.py:134
  30.0 5.5 %all-to-all-done.g0 = bf16[8,64,384]{2,1,0:T(8,128)(2,1)S(1)} async-done(((bf16[8,64,384]{2,1,0:T(8,128)(2,1)}), bf16[8,64,384]{2,1,0:T(8,128)(2,1)S(1)}, u32[]{:S(2)}, u32[]{:S(2)}) %all-to-all-start) | async-done | bytes 393248 | tf_op jit(solution)/shard_map/all_to_all | solution.py:152
  36.3 3.5 %all-to-all-start.1 = ((bf16[8,64,384]{2,1,0:T(8,128)(2,1)}), bf16[8,64,384]{2,1,0:T(8,128)(2,1)S(1)}, u32[]{:S(2)}, u32[]{:S(2)}) async-start(bf16[8,64,384]{2,1,0:T(8,128)(2,1)} %broadcast_in_dim.34), calls=%async_computation.1 | async-start | bytes 786432 | tf_op jit(solution)/shard_map/all_to_all | solution.py:152
  39.9 2.4 %collective-permute-start.3 = (bf16[8,64,384]{2,1,0:T(8,128)(2,1)S(1)}, bf16[8,64,384]{2,1,0:T(8,128)(2,1)S(1)}, u32[]{:S(2)}, u32[]{:S(2)}) collective-permute-start(bf16[8,64,384]{2,1,0:T(8,128)(2,1)S(1)} %all-to-all-done.g0), channel_id=1, source_target_pairs={{0,16},{16,32},{32,48},{48,0},{64,80},{80,96},{96,112},{112,64},{1... | collective-permute-start | bytes 1179656 | tf_op jit(solution)/shard_map/ppermute | solution.py:134
  42.3 3.4 %collective-permute-start.4 = (bf16[8,64,384]{2,1,0:T(8,128)(2,1)S(1)}, bf16[8,64,384]{2,1,0:T(8,128)(2,1)S(1)}, u32[]{:S(2)}, u32[]{:S(2)}) collective-permute-start(bf16[8,64,384]{2,1,0:T(8,128)(2,1)S(1)} %all-to-all-done.g0), channel_id=1, source_target_pairs={{0,48},{16,0},{32,16},{48,32},{64,112},{80,64},{96,80},{112,96},{1... | collective-permute-start | bytes 1179656 | tf_op jit(solution)/shard_map/ppermute | solution.py:134
  45.9 6.1 %collective-permute-done.3.g1 = bf16[8,64,384]{2,1,0:T(8,128)(2,1)S(1)} collective-permute-done((bf16[8,64,384]{2,1,0:T(8,128)(2,1)S(1)}, bf16[8,64,384]{2,1,0:T(8,128)(2,1)S(1)}, u32[]{:S(2)}, u32[]{:S(2)}) %collective-permute-start.3) | collective-permute-done | bytes 393248 | tf_op jit(solution)/shard_map/ppermute | solution.py:134
  51.9 3.4 %collective-permute-done.4.g2 = bf16[8,64,384]{2,1,0:T(8,128)(2,1)S(1)} collective-permute-done((bf16[8,64,384]{2,1,0:T(8,128)(2,1)S(1)}, bf16[8,64,384]{2,1,0:T(8,128)(2,1)S(1)}, u32[]{:S(2)}, u32[]{:S(2)}) %collective-permute-start.4) | collective-permute-done | bytes 393248 | tf_op jit(solution)/shard_map/ppermute | solution.py:134
  56.8 6.8 %all-to-all-start.2 = ((bf16[8,4,64,384]{3,2,1,0:T(8,128)(2,1)}), bf16[8,4,64,384]{3,2,1,0:T(8,128)(2,1)S(1)}, u32[]{:S(2)}, u32[]{:S(2)}) async-start(bf16[8,4,64,384]{3,2,1,0:T(8,128)(2,1)} %broadcast_in_dim.40), calls=%async_computation.2 | async-start | bytes 3145728 | tf_op jit(solution)/shard_map/all_to_all | solution.py:152
  65.9 4.8 %collective-permute-start.6 = (bf16[8,64,384]{2,1,0:T(8,128)(2,1)S(1)}, bf16[8,64,384]{2,1,0:T(8,128)(2,1)S(1)}, u32[]{:S(2)}, u32[]{:S(2)}) collective-permute-start(bf16[8,64,384]{2,1,0:T(8,128)(2,1)S(1)} %all-to-all-done.1.u0), channel_id=1, source_target_pairs={{0,16},{16,32},{32,48},{48,0},{64,80},{80,96},{96,112},{112,64},{1... | collective-permute-start | bytes 1179656 | tf_op jit(solution)/shard_map/ppermute | solution.py:134
  72.7 2.5 %collective-permute-done.7.u2 = bf16[8,64,384]{2,1,0:T(8,128)(2,1)S(1)} collective-permute-done((bf16[8,64,384]{2,1,0:T(8,128)(2,1)S(1)}, bf16[8,64,384]{2,1,0:T(8,128)(2,1)S(1)}, u32[]{:S(2)}, u32[]{:S(2)}) %collective-permute-start.7) | collective-permute-done | bytes 393248 | tf_op jit(solution)/shard_map/ppermute | solution.py:134
  77.8 7.1 %collective-permute-done.5.g3 = bf16[8,64,384]{2,1,0:T(8,128)(2,1)S(1)} collective-permute-done((bf16[8,64,384]{2,1,0:T(8,128)(2,1)S(1)}, bf16[8,64,384]{2,1,0:T(8,128)(2,1)S(1)}, u32[]{:S(2)}, u32[]{:S(2)}) %collective-permute-start.5) | collective-permute-done | bytes 393248 | tf_op jit(solution)/shard_map/ppermute | solution.py:134
  86.2 7.7 %shard_map.68 = (f32[384,384]{1,0:T(8,128)}, f32[384,384]{1,0:T(8,128)}, bf16[8,4,64,384]{3,2,1,0:T(8,128)(2,1)}) custom-call(s32[2]{0:T(128)} %pad_add_fusion.place, bf16[768,2048]{1,0:T(8,128)(2,1)} %all-gather.2.cloned.1.call-done.rows_ref, bf16[8,64,384]{2,1,0:T(8,128)(2,1)} %copy-done.1, bf16[8,64,384]{2,1,0:T(8,128)(2,1)} %copy-done.3, ...), custom_call_target="tpu_custom_call" | custom-call | flops 1811939328 | bytes 10000000 | tf_op jit(solution)/shard_map/pallas_call | solution.py:119
  93.9 7.5 %all-to-all-done.2 = bf16[8,4,64,384]{3,2,1,0:T(8,128)(2,1)S(1)} async-done(((bf16[8,4,64,384]{3,2,1,0:T(8,128)(2,1)}), bf16[8,4,64,384]{3,2,1,0:T(8,128)(2,1)S(1)}, u32[]{:S(2)}, u32[]{:S(2)}) %all-to-all-start.2) | async-done | bytes 1572896 | tf_op jit(solution)/shard_map/all_to_all | solution.py:152
  102.7 6.6 %shard_map.69 = (bf16[8,384,128]{2,1,0:T(8,128)(2,1)}, bf16[8,384,128]{2,1,0:T(8,128)(2,1)}) custom-call(s32[2]{0:T(128)} %pad_add_fusion.place, bf16[768,2048]{1,0:T(8,128)(2,1)} %all-gather.2.cloned.1.call-done.rows_ref, bf16[8,2,128,384]{3,2,1,0:T(8,128)(2,1)} %bitcast.21, bf16[8,64,384]{2,1,0:T(8,128)(2,1)} %copy-done.1, bf16[8,64,384]{2,1,0:T(8,128)(2,1)} %copy-done.3, ...), custom_call_target="tpu_custom_call" | custom-call | flops 1811939328 | bytes 10000000 | tf_op jit(solution)/shard_map/pallas_call | solution.py:119
  111.2 2.5 %collective-permute-done.9 = bf16[8,384,128]{2,1,0:T(8,128)(2,1)S(1)} collective-permute-done((bf16[8,384,128]{2,1,0:T(8,128)(2,1)}, bf16[8,384,128]{2,1,0:T(8,128)(2,1)S(1)}, u32[]{:S(2)}, u32[]{:S(2)}) %collective-permute-start.9) | collective-permute-done | bytes 786464 | tf_op jit(solution)/shard_map/ppermute | solution.py:144
  116.0 7.0 %all-to-all-start.3 = ((bf16[8,384,128]{2,1,0:T(8,128)(2,1)}), bf16[8,384,128]{2,1,0:T(8,128)(2,1)S(1)}, u32[]{:S(2)}, u32[]{:S(2)}) async-start(bf16[8,384,128]{2,1,0:T(8,128)(2,1)} %add_convert_fusion), calls=%async_computation.3 | async-start | bytes 1572864 | tf_op jit(solution)/shard_map/all_to_all | solution.py:216
  123.0 10.6 %reduce-scatter.2.cloned.1.call-done = bf16[256,384]{1,0:T(8,128)(2,1)} async-done(((bf16[2048,384]{1,0:T(8,128)(2,1)}), bf16[256,384]{1,0:T(8,128)(2,1)}) %reduce-scatter.2.cloned.1.call-update) | async-done | bytes 196624 | tf_op jit(solution)/shard_map/reduce_scatter | solution.py:218
  134.5 4.7 %collective-permute-start.10 = (bf16[2,64,384]{2,1,0:T(8,128)(2,1)S(1)}, bf16[2,64,384]{2,1,0:T(8,128)(2,1)S(1)}, u32[]{:S(2)}, u32[]{:S(2)}) collective-permute-start(bf16[2,64,384]{2,1,0:T(8,128)(2,1)S(1)} %pad_maximum_fusion.1), channel_id=1, source_target_pairs={{0,128},{16,144},{32,160},{48,176},{64,192},{80,208},{96,224},{112... | collective-permute-start | bytes 294920 | tf_op jit(solution)/shard_map/ppermute | solution.py:139
  139.3 3.7 %collective-permute-done.10 = bf16[2,64,384]{2,1,0:T(8,128)(2,1)S(1)} collective-permute-done((bf16[2,64,384]{2,1,0:T(8,128)(2,1)S(1)}, bf16[2,64,384]{2,1,0:T(8,128)(2,1)S(1)}, u32[]{:S(2)}, u32[]{:S(2)}) %collective-permute-start.10) | collective-permute-done | bytes 98336 | tf_op jit(solution)/shard_map/ppermute | solution.py:139
  143.8 4.7 %collective-permute-start.11 = (bf16[64,384]{1,0:T(8,128)(2,1)S(1)}, bf16[64,384]{1,0:T(8,128)(2,1)S(1)}, u32[]{:S(2)}, u32[]{:S(2)}) collective-permute-start(bf16[64,384]{1,0:T(8,128)(2,1)S(1)} %fusion.2), channel_id=1, source_target_pairs={{0,384},{16,400},{32,416},{48,432},{64,448},{80,464},{96,480},{112... | collective-permute-start | bytes 147464 | tf_op jit(solution)/shard_map/ppermute | solution.py:139
  149.3 2.6 %collective-permute-done.11 = bf16[64,384]{1,0:T(8,128)(2,1)S(1)} collective-permute-done((bf16[64,384]{1,0:T(8,128)(2,1)S(1)}, bf16[64,384]{1,0:T(8,128)(2,1)S(1)}, u32[]{:S(2)}, u32[]{:S(2)}) %collective-permute-start.11) | collective-permute-done | bytes 49184 | tf_op jit(solution)/shard_map/ppermute | solution.py:139
  (52 shorter events, 23.1 us)
Async XLA Ops:
  7.2 13.6 %copy-start.9 = (bf16[64,384]{1,0:T(8,128)(2,1)S(1)}, bf16[64,384]{1,0:T(8,128)(2,1)}, u32[]{:S(2)}) copy-start(bf16[64,384]{1,0:T(8,128)(2,1)} %param.9) | copy-start | bytes 147460
  7.2 28.3 %copy-start.8 = (bf16[64,384]{1,0:T(8,128)(2,1)S(1)}, bf16[64,384]{1,0:T(8,128)(2,1)}, u32[]{:S(2)}) copy-start(bf16[64,384]{1,0:T(8,128)(2,1)} %param.8) | copy-start | bytes 147460
  7.2 79.0 %all-gather.2.cloned.1.call-start = ((), (), s32[]{:S(2)}) async-start(), calls=%async_computation.5 | async-start | bytes 3342336 | tf_op jit(solution)/shard_map/all_gather | solution.py:172
  10.5 25.0 %all-to-all-start = ((bf16[8,64,384]{2,1,0:T(8,128)(2,1)}), bf16[8,64,384]{2,1,0:T(8,128)(2,1)S(1)}, u32[]{:S(2)}, u32[]{:S(2)}) async-start(bf16[8,64,384]{2,1,0:T(8,128)(2,1)} %broadcast_in_dim.16), calls=%async_computation | async-start | bytes 786432 | tf_op jit(solution)/shard_map/all_to_all | solution.py:152
  20.8 19.1 %collective-permute-start = (bf16[64,384]{1,0:T(8,128)(2,1)S(1)}, bf16[64,384]{1,0:T(8,128)(2,1)S(1)}, u32[]{:S(2)}, u32[]{:S(2)}) collective-permute-start(bf16[64,384]{1,0:T(8,128)(2,1)S(1)} %copy-done.9), channel_id=1, source_target_pairs={{0,16},{16,32},{32,48},{48,0},{64,80},{80,96},{96,112},{112,64},{1... | collective-permute-start | bytes 147464 | tf_op jit(solution)/shard_map/ppermute | solution.py:134
  23.2 22.6 %collective-permute-start.1 = (bf16[64,384]{1,0:T(8,128)(2,1)S(1)}, bf16[64,384]{1,0:T(8,128)(2,1)S(1)}, u32[]{:S(2)}, u32[]{:S(2)}) collective-permute-start(bf16[64,384]{1,0:T(8,128)(2,1)S(1)} %copy-done.9), channel_id=1, source_target_pairs={{0,48},{16,0},{32,16},{48,32},{64,112},{80,64},{96,80},{112,96},{1... | collective-permute-start | bytes 147464 | tf_op jit(solution)/shard_map/ppermute | solution.py:134
  26.7 19.2 %collective-permute-start.2 = (bf16[64,384]{1,0:T(8,128)(2,1)S(1)}, bf16[64,384]{1,0:T(8,128)(2,1)S(1)}, u32[]{:S(2)}, u32[]{:S(2)}) collective-permute-start(bf16[64,384]{1,0:T(8,128)(2,1)S(1)} %copy-done.9), channel_id=1, source_target_pairs={{0,32},{16,48},{32,0},{48,16},{64,96},{80,112},{96,64},{112,80},{1... | collective-permute-start | bytes 147464 | tf_op jit(solution)/shard_map/ppermute | solution.py:134
  35.5 21.3 %copy-start.1 = (bf16[8,64,384]{2,1,0:T(8,128)(2,1)}, bf16[8,64,384]{2,1,0:T(8,128)(2,1)S(1)}, u32[]{:S(2)}) copy-start(bf16[8,64,384]{2,1,0:T(8,128)(2,1)S(1)} %all-to-all-done.g0) | copy-start | bytes 1179652
  36.3 19.0 %all-to-all-start.1 = ((bf16[8,64,384]{2,1,0:T(8,128)(2,1)}), bf16[8,64,384]{2,1,0:T(8,128)(2,1)S(1)}, u32[]{:S(2)}, u32[]{:S(2)}) async-start(bf16[8,64,384]{2,1,0:T(8,128)(2,1)} %broadcast_in_dim.34), calls=%async_computation.1 | async-start | bytes 786432 | tf_op jit(solution)/shard_map/all_to_all | solution.py:152
  39.9 12.0 %collective-permute-start.3 = (bf16[8,64,384]{2,1,0:T(8,128)(2,1)S(1)}, bf16[8,64,384]{2,1,0:T(8,128)(2,1)S(1)}, u32[]{:S(2)}, u32[]{:S(2)}) collective-permute-start(bf16[8,64,384]{2,1,0:T(8,128)(2,1)S(1)} %all-to-all-done.g0), channel_id=1, source_target_pairs={{0,16},{16,32},{32,48},{48,0},{64,80},{80,96},{96,112},{112,64},{1... | collective-permute-start | bytes 1179656 | tf_op jit(solution)/shard_map/ppermute | solution.py:134
  42.3 12.9 %collective-permute-start.4 = (bf16[8,64,384]{2,1,0:T(8,128)(2,1)S(1)}, bf16[8,64,384]{2,1,0:T(8,128)(2,1)S(1)}, u32[]{:S(2)}, u32[]{:S(2)}) collective-permute-start(bf16[8,64,384]{2,1,0:T(8,128)(2,1)S(1)} %all-to-all-done.g0), channel_id=1, source_target_pairs={{0,48},{16,0},{32,16},{48,32},{64,112},{80,64},{96,80},{112,96},{1... | collective-permute-start | bytes 1179656 | tf_op jit(solution)/shard_map/ppermute | solution.py:134
  51.9 18.8 %copy-start.3 = (bf16[8,64,384]{2,1,0:T(8,128)(2,1)}, bf16[8,64,384]{2,1,0:T(8,128)(2,1)S(1)}, u32[]{:S(2)}) copy-start(bf16[8,64,384]{2,1,0:T(8,128)(2,1)S(1)} %collective-permute-done.3.g1) | copy-start | bytes 1179652
  55.3 10.6 %copy-start.2 = (bf16[8,64,384]{2,1,0:T(8,128)(2,1)}, bf16[8,64,384]{2,1,0:T(8,128)(2,1)S(1)}, u32[]{:S(2)}) copy-start(bf16[8,64,384]{2,1,0:T(8,128)(2,1)S(1)} %all-to-all-done.1.u0) | copy-start | bytes 1179652
  56.8 44.7 %all-to-all-start.2 = ((bf16[8,4,64,384]{3,2,1,0:T(8,128)(2,1)}), bf16[8,4,64,384]{3,2,1,0:T(8,128)(2,1)S(1)}, u32[]{:S(2)}, u32[]{:S(2)}) async-start(bf16[8,4,64,384]{3,2,1,0:T(8,128)(2,1)} %broadcast_in_dim.40), calls=%async_computation.2 | async-start | bytes 3145728 | tf_op jit(solution)/shard_map/all_to_all | solution.py:152
  63.6 70.0 %reduce-scatter.2.cloned.1.call-start = ((), (), s32[]{:S(2)}) async-start(), calls=%async_computation.6 | async-start | bytes 1769472 | tf_op jit(solution)/shard_map/reduce_scatter | solution.py:218
  63.7 11.6 %collective-permute-start.7 = (bf16[8,64,384]{2,1,0:T(8,128)(2,1)S(1)}, bf16[8,64,384]{2,1,0:T(8,128)(2,1)S(1)}, u32[]{:S(2)}, u32[]{:S(2)}) collective-permute-start(bf16[8,64,384]{2,1,0:T(8,128)(2,1)S(1)} %all-to-all-done.1.u0), channel_id=1, source_target_pairs={{0,48},{16,0},{32,16},{48,32},{64,112},{80,64},{96,80},{112,96},{1... | collective-permute-start | bytes 1179656 | tf_op jit(solution)/shard_map/ppermute | solution.py:134
  65.9 19.0 %collective-permute-start.6 = (bf16[8,64,384]{2,1,0:T(8,128)(2,1)S(1)}, bf16[8,64,384]{2,1,0:T(8,128)(2,1)S(1)}, u32[]{:S(2)}, u32[]{:S(2)}) collective-permute-start(bf16[8,64,384]{2,1,0:T(8,128)(2,1)S(1)} %all-to-all-done.1.u0), channel_id=1, source_target_pairs={{0,16},{16,32},{32,48},{48,0},{64,80},{80,96},{96,112},{112,64},{1... | collective-permute-start | bytes 1179656 | tf_op jit(solution)/shard_map/ppermute | solution.py:134
  70.8 14.1 %collective-permute-start.5 = (bf16[8,64,384]{2,1,0:T(8,128)(2,1)S(1)}, bf16[8,64,384]{2,1,0:T(8,128)(2,1)S(1)}, u32[]{:S(2)}, u32[]{:S(2)}) collective-permute-start(bf16[8,64,384]{2,1,0:T(8,128)(2,1)S(1)} %collective-permute-done.3.g1), channel_id=1, source_target_pairs={{0,16},{16,32},{32,48},{48,0},{64,80},{80,96},{96,112},{112,64},{1... | collective-permute-start | bytes 1179656 | tf_op jit(solution)/shard_map/ppermute | solution.py:134
  75.2 11.0 %copy-start.5 = (bf16[8,64,384]{2,1,0:T(8,128)(2,1)}, bf16[8,64,384]{2,1,0:T(8,128)(2,1)S(1)}, u32[]{:S(2)}) copy-start(bf16[8,64,384]{2,1,0:T(8,128)(2,1)S(1)} %collective-permute-done.7.u2) | copy-start | bytes 1179652
  75.2 11.0 %collective-permute-start.8 = (bf16[8,64,384]{2,1,0:T(8,128)(2,1)S(1)}, bf16[8,64,384]{2,1,0:T(8,128)(2,1)}, u32[]{:S(2)}, u32[]{:S(2)}) collective-permute-start(bf16[8,64,384]{2,1,0:T(8,128)(2,1)S(1)} %collective-permute-done.7.u2), channel_id=1, source_target_pairs={{0,48},{16,0},{32,16},{48,32},{64,112},{80,64},{96,80},{112,96},{1... | collective-permute-start | bytes 1179656 | tf_op jit(solution)/shard_map/ppermute | solution.py:134
  109.3 4.4 %collective-permute-start.9 = (bf16[8,384,128]{2,1,0:T(8,128)(2,1)}, bf16[8,384,128]{2,1,0:T(8,128)(2,1)S(1)}, u32[]{:S(2)}, u32[]{:S(2)}) collective-permute-start(bf16[8,384,128]{2,1,0:T(8,128)(2,1)} %get-tuple-element.28), channel_id=1, source_target_pairs={{0,1},{1,0},{2,3},{3,2},{4,5},{5,4},{6,7},{7,6},{8,9},{9,8},{10,11... | collective-permute-start | bytes 2359304 | tf_op jit(solution)/shard_map/ppermute | solution.py:144
  116.0 32.6 %all-to-all-start.3 = ((bf16[8,384,128]{2,1,0:T(8,128)(2,1)}), bf16[8,384,128]{2,1,0:T(8,128)(2,1)S(1)}, u32[]{:S(2)}, u32[]{:S(2)}) async-start(bf16[8,384,128]{2,1,0:T(8,128)(2,1)} %add_convert_fusion), calls=%async_computation.3 | async-start | bytes 1572864 | tf_op jit(solution)/shard_map/all_to_all | solution.py:216
  134.5 8.5 %collective-permute-start.10 = (bf16[2,64,384]{2,1,0:T(8,128)(2,1)S(1)}, bf16[2,64,384]{2,1,0:T(8,128)(2,1)S(1)}, u32[]{:S(2)}, u32[]{:S(2)}) collective-permute-start(bf16[2,64,384]{2,1,0:T(8,128)(2,1)S(1)} %pad_maximum_fusion.1), channel_id=1, source_target_pairs={{0,128},{16,144},{32,160},{48,176},{64,192},{80,208},{96,224},{112... | collective-permute-start | bytes 294920 | tf_op jit(solution)/shard_map/ppermute | solution.py:139
  143.8 8.1 %collective-permute-start.11 = (bf16[64,384]{1,0:T(8,128)(2,1)S(1)}, bf16[64,384]{1,0:T(8,128)(2,1)S(1)}, u32[]{:S(2)}, u32[]{:S(2)}) collective-permute-start(bf16[64,384]{1,0:T(8,128)(2,1)S(1)} %fusion.2), channel_id=1, source_target_pairs={{0,384},{16,400},{32,416},{48,432},{64,448},{80,464},{96,480},{112... | collective-permute-start | bytes 147464 | tf_op jit(solution)/shard_map/ppermute | solution.py:139
  (4 other events, 5.5 us)
Sparse Core Ops, SparseCore 0:
  10.6 52.2 all-gather.1
  94.1 39.5 reduce-scatter.1

commit v10 on v9

--- a/solution.py
+++ b/solution.py
@@ -64,7 +64,7 @@
         tok[...], up_full[...].reshape(n_feat, -1), preferred_element_type=jnp.float32
     )
     up_out[...] = up_value
-    hidden = (gate_value * jax.nn.sigmoid(gate_value) * up_value).astype(jnp.bfloat16)
+    hidden = (gate_value * sigmoid(gate_value) * up_value).astype(jnp.bfloat16)
     cot_copy.wait()
     partial_value = dot(cot[...], hidden, ((0,), (0,))).astype(jnp.bfloat16)
     depth = n_feat // (N_Z * N_X)
@@ -88,7 +88,7 @@
     gate_copies = copy_blocks((g0, g1, g2, g3), gate_full, gate_sems, me_x)
     up_copies = copy_blocks((u0, u1, u2, u3), up_full, up_sems, me_x)
     gate_value, up_value = gate_in[...], up_in[...]
-    sigmoid_gate = jax.nn.sigmoid(gate_value)
+    sigmoid_gate = sigmoid(gate_value)
     cot_copy.wait()
     down_copy.wait()
     hidden_grad = jnp.dot(
@@ -127,6 +127,10 @@
     )(*operands)
 
 
+def sigmoid(value):
+    return 1.0 / (1.0 + jnp.exp(-value))
+
+
 def send_x(value, step):
     pairs = [
         (z * N_X + x, z * N_X + (x + step) % N_X) for z in range(N_Z) for x in range(N_X)

time: 162 us -> 162 us (level)
  no operation moved by 1% of the time
where the time goes in v10:
time: 162 us; the launch traced here: 160 us
  starting transfers between devices  64.9 us (40%)
  waiting for transfers between devices  52.6 us (32%)
  Pallas kernels  14.7 us (9%)
  between operations  14.4 us (9%)
  other arithmetic  7.51 us (5%)
  local copies, waits for them, and re-layouts  6.1 us (4%)
    ppermute x9, starting transfers between devices, send_x(): return lax.ppermute(value, 'fsdp', pairs)  25.9 us
    all_to_all x3, starting transfers between devices, gather_z(): return lax.all_to_all(copies, 'fsdp', 0, 0, axis_index_groups=Z_GROUPS)  20.6 us
    ppermute x9, waiting for transfers between devices, send_x(): return lax.ppermute(value, 'fsdp', pairs)  20.4 us
    pallas_call x2, Pallas kernels, call_kernel(): pl.pallas_call(kernel, out_shape=out_shapes, in_specs=in_specs, out_specs...  14.7 us
    all_to_all x3, waiting for transfers between devices, gather_z(): return lax.all_to_all(copies, 'fsdp', 0, 0, axis_index_groups=Z_GROUPS)  13 us
    reduce_scatter x1, waiting for transfers between devices, on_device(): lax.psum_scatter(down_partial.reshape(n_feat, cols), 'fsdp', scatter_dime...  10.3 us
    ppermute x2, starting transfers between devices, swap_z(): return lax.ppermute(value, 'fsdp', pairs)  9.38 us
    all_to_all x1, starting transfers between devices, on_device(): summed = lax.all_to_all(pair_sum, 'mp', 0, 0, axis_index_groups=Y_GROUPS)  7.04 us
  transfers between devices with their start and end apart: 18, of which 11 were waited for; matrix products, arithmetic and copies ran while one was open for 5% of the time, Pallas kernels for 9%

profile of v10, /device:TPU:6, one launch (start us, length us, event | category | flops | bytes accessed | tf_op | source)
XLA Modules:
  0.0 160.3 jit_solution(3237203625656701853)
XLA Ops:
  10.5 10.3 %all-to-all-start = ((bf16[8,64,384]{2,1,0:T(8,128)(2,1)}), bf16[8,64,384]{2,1,0:T(8,128)(2,1)S(1)}, u32[]{:S(2)}, u32[]{:S(2)}) async-start(bf16[8,64,384]{2,1,0:T(8,128)(2,1)} %broadcast_in_dim.16), calls=%async_computation | async-start | bytes 786432 | tf_op jit(solution)/shard_map/all_to_all | solution.py:156
  20.8 2.4 %collective-permute-start = (bf16[64,384]{1,0:T(8,128)(2,1)S(1)}, bf16[64,384]{1,0:T(8,128)(2,1)S(1)}, u32[]{:S(2)}, u32[]{:S(2)}) collective-permute-start(bf16[64,384]{1,0:T(8,128)(2,1)S(1)} %copy-done.9), channel_id=1, source_target_pairs={{0,16},{16,32},{32,48},{48,0},{64,80},{80,96},{96,112},{112,64},{1... | collective-permute-start | bytes 147464 | tf_op jit(solution)/shard_map/ppermute | solution.py:138
  23.2 3.5 %collective-permute-start.1 = (bf16[64,384]{1,0:T(8,128)(2,1)S(1)}, bf16[64,384]{1,0:T(8,128)(2,1)S(1)}, u32[]{:S(2)}, u32[]{:S(2)}) collective-permute-start(bf16[64,384]{1,0:T(8,128)(2,1)S(1)} %copy-done.9), channel_id=1, source_target_pairs={{0,48},{16,0},{32,16},{48,32},{64,112},{80,64},{96,80},{112,96},{1... | collective-permute-start | bytes 147464 | tf_op jit(solution)/shard_map/ppermute | solution.py:138
  26.7 3.3 %collective-permute-start.2 = (bf16[64,384]{1,0:T(8,128)(2,1)S(1)}, bf16[64,384]{1,0:T(8,128)(2,1)S(1)}, u32[]{:S(2)}, u32[]{:S(2)}) collective-permute-start(bf16[64,384]{1,0:T(8,128)(2,1)S(1)} %copy-done.9), channel_id=1, source_target_pairs={{0,32},{16,48},{32,0},{48,16},{64,96},{80,112},{96,64},{112,80},{1... | collective-permute-start | bytes 147464 | tf_op jit(solution)/shard_map/ppermute | solution.py:138
  30.0 5.5 %all-to-all-done.g0 = bf16[8,64,384]{2,1,0:T(8,128)(2,1)S(1)} async-done(((bf16[8,64,384]{2,1,0:T(8,128)(2,1)}), bf16[8,64,384]{2,1,0:T(8,128)(2,1)S(1)}, u32[]{:S(2)}, u32[]{:S(2)}) %all-to-all-start) | async-done | bytes 393248 | tf_op jit(solution)/shard_map/all_to_all | solution.py:156
  36.3 3.5 %all-to-all-start.1 = ((bf16[8,64,384]{2,1,0:T(8,128)(2,1)}), bf16[8,64,384]{2,1,0:T(8,128)(2,1)S(1)}, u32[]{:S(2)}, u32[]{:S(2)}) async-start(bf16[8,64,384]{2,1,0:T(8,128)(2,1)} %broadcast_in_dim.34), calls=%async_computation.1 | async-start | bytes 786432 | tf_op jit(solution)/shard_map/all_to_all | solution.py:156
  39.9 2.4 %collective-permute-start.3 = (bf16[8,64,384]{2,1,0:T(8,128)(2,1)S(1)}, bf16[8,64,384]{2,1,0:T(8,128)(2,1)S(1)}, u32[]{:S(2)}, u32[]{:S(2)}) collective-permute-start(bf16[8,64,384]{2,1,0:T(8,128)(2,1)S(1)} %all-to-all-done.g0), channel_id=1, source_target_pairs={{0,16},{16,32},{32,48},{48,0},{64,80},{80,96},{96,112},{112,64},{1... | collective-permute-start | bytes 1179656 | tf_op jit(solution)/shard_map/ppermute | solution.py:138
  42.3 3.4 %collective-permute-start.4 = (bf16[8,64,384]{2,1,0:T(8,128)(2,1)S(1)}, bf16[8,64,384]{2,1,0:T(8,128)(2,1)S(1)}, u32[]{:S(2)}, u32[]{:S(2)}) collective-permute-start(bf16[8,64,384]{2,1,0:T(8,128)(2,1)S(1)} %all-to-all-done.g0), channel_id=1, source_target_pairs={{0,48},{16,0},{32,16},{48,32},{64,112},{80,64},{96,80},{112,96},{1... | collective-permute-start | bytes 1179656 | tf_op jit(solution)/shard_map/ppermute | solution.py:138
  45.9 6.1 %collective-permute-done.3.g1 = bf16[8,64,384]{2,1,0:T(8,128)(2,1)S(1)} collective-permute-done((bf16[8,64,384]{2,1,0:T(8,128)(2,1)S(1)}, bf16[8,64,384]{2,1,0:T(8,128)(2,1)S(1)}, u32[]{:S(2)}, u32[]{:S(2)}) %collective-permute-start.3) | collective-permute-done | bytes 393248 | tf_op jit(solution)/shard_map/ppermute | solution.py:138
  51.9 3.4 %collective-permute-done.4.g2 = bf16[8,64,384]{2,1,0:T(8,128)(2,1)S(1)} collective-permute-done((bf16[8,64,384]{2,1,0:T(8,128)(2,1)S(1)}, bf16[8,64,384]{2,1,0:T(8,128)(2,1)S(1)}, u32[]{:S(2)}, u32[]{:S(2)}) %collective-permute-start.4) | collective-permute-done | bytes 393248 | tf_op jit(solution)/shard_map/ppermute | solution.py:138
  56.8 6.8 %all-to-all-start.2 = ((bf16[8,4,64,384]{3,2,1,0:T(8,128)(2,1)}), bf16[8,4,64,384]{3,2,1,0:T(8,128)(2,1)S(1)}, u32[]{:S(2)}, u32[]{:S(2)}) async-start(bf16[8,4,64,384]{3,2,1,0:T(8,128)(2,1)} %broadcast_in_dim.40), calls=%async_computation.2 | async-start | bytes 3145728 | tf_op jit(solution)/shard_map/all_to_all | solution.py:156
  65.9 4.8 %collective-permute-start.6 = (bf16[8,64,384]{2,1,0:T(8,128)(2,1)S(1)}, bf16[8,64,384]{2,1,0:T(8,128)(2,1)S(1)}, u32[]{:S(2)}, u32[]{:S(2)}) collective-permute-start(bf16[8,64,384]{2,1,0:T(8,128)(2,1)S(1)} %all-to-all-done.1.u0), channel_id=1, source_target_pairs={{0,16},{16,32},{32,48},{48,0},{64,80},{80,96},{96,112},{112,64},{1... | collective-permute-start | bytes 1179656 | tf_op jit(solution)/shard_map/ppermute | solution.py:138
  72.7 2.5 %collective-permute-done.7.u2 = bf16[8,64,384]{2,1,0:T(8,128)(2,1)S(1)} collective-permute-done((bf16[8,64,384]{2,1,0:T(8,128)(2,1)S(1)}, bf16[8,64,384]{2,1,0:T(8,128)(2,1)S(1)}, u32[]{:S(2)}, u32[]{:S(2)}) %collective-permute-start.7) | collective-permute-done | bytes 393248 | tf_op jit(solution)/shard_map/ppermute | solution.py:138
  77.8 7.1 %collective-permute-done.5.g3 = bf16[8,64,384]{2,1,0:T(8,128)(2,1)S(1)} collective-permute-done((bf16[8,64,384]{2,1,0:T(8,128)(2,1)S(1)}, bf16[8,64,384]{2,1,0:T(8,128)(2,1)S(1)}, u32[]{:S(2)}, u32[]{:S(2)}) %collective-permute-start.5) | collective-permute-done | bytes 393248 | tf_op jit(solution)/shard_map/ppermute | solution.py:138
  86.2 7.7 %shard_map.68 = (f32[384,384]{1,0:T(8,128)}, f32[384,384]{1,0:T(8,128)}, bf16[8,4,64,384]{3,2,1,0:T(8,128)(2,1)}) custom-call(s32[2]{0:T(128)} %pad_add_fusion.place, bf16[768,2048]{1,0:T(8,128)(2,1)} %all-gather.2.cloned.1.call-done.rows_ref, bf16[8,64,384]{2,1,0:T(8,128)(2,1)} %copy-done.1, bf16[8,64,384]{2,1,0:T(8,128)(2,1)} %copy-done.3, ...), custom_call_target="tpu_custom_call" | custom-call | flops 1811939328 | bytes 10000000 | tf_op jit(solution)/shard_map/pallas_call | solution.py:119
  94.0 7.5 %all-to-all-done.2 = bf16[8,4,64,384]{3,2,1,0:T(8,128)(2,1)S(1)} async-done(((bf16[8,4,64,384]{3,2,1,0:T(8,128)(2,1)}), bf16[8,4,64,384]{3,2,1,0:T(8,128)(2,1)S(1)}, u32[]{:S(2)}, u32[]{:S(2)}) %all-to-all-start.2) | async-done | bytes 1572896 | tf_op jit(solution)/shard_map/all_to_all | solution.py:156
  102.7 7.0 %shard_map.69 = (bf16[8,384,128]{2,1,0:T(8,128)(2,1)}, bf16[8,384,128]{2,1,0:T(8,128)(2,1)}) custom-call(s32[2]{0:T(128)} %pad_add_fusion.place, bf16[768,2048]{1,0:T(8,128)(2,1)} %all-gather.2.cloned.1.call-done.rows_ref, bf16[8,2,128,384]{3,2,1,0:T(8,128)(2,1)} %bitcast.21, bf16[8,64,384]{2,1,0:T(8,128)(2,1)} %copy-done.1, bf16[8,64,384]{2,1,0:T(8,128)(2,1)} %copy-done.3, ...), custom_call_target="tpu_custom_call" | custom-call | flops 1811939328 | bytes 10000000 | tf_op jit(solution)/shard_map/pallas_call | solution.py:119
  111.7 2.5 %collective-permute-done.9 = bf16[8,384,128]{2,1,0:T(8,128)(2,1)S(1)} collective-permute-done((bf16[8,384,128]{2,1,0:T(8,128)(2,1)}, bf16[8,384,128]{2,1,0:T(8,128)(2,1)S(1)}, u32[]{:S(2)}, u32[]{:S(2)}) %collective-permute-start.9) | collective-permute-done | bytes 786464 | tf_op jit(solution)/shard_map/ppermute | solution.py:148
  116.4 7.0 %all-to-all-start.3 = ((bf16[8,384,128]{2,1,0:T(8,128)(2,1)}), bf16[8,384,128]{2,1,0:T(8,128)(2,1)S(1)}, u32[]{:S(2)}, u32[]{:S(2)}) async-start(bf16[8,384,128]{2,1,0:T(8,128)(2,1)} %add_convert_fusion), calls=%async_computation.3 | async-start | bytes 1572864 | tf_op jit(solution)/shard_map/all_to_all | solution.py:220
  123.4 10.3 %reduce-scatter.2.cloned.1.call-done = bf16[256,384]{1,0:T(8,128)(2,1)} async-done(((bf16[2048,384]{1,0:T(8,128)(2,1)}), bf16[256,384]{1,0:T(8,128)(2,1)}) %reduce-scatter.2.cloned.1.call-update) | async-done | bytes 196624 | tf_op jit(solution)/shard_map/reduce_scatter | solution.py:222
  134.6 4.7 %collective-permute-start.10 = (bf16[2,64,384]{2,1,0:T(8,128)(2,1)S(1)}, bf16[2,64,384]{2,1,0:T(8,128)(2,1)S(1)}, u32[]{:S(2)}, u32[]{:S(2)}) collective-permute-start(bf16[2,64,384]{2,1,0:T(8,128)(2,1)S(1)} %pad_maximum_fusion.1), channel_id=1, source_target_pairs={{0,128},{16,144},{32,160},{48,176},{64,192},{80,208},{96,224},{112... | collective-permute-start | bytes 294920 | tf_op jit(solution)/shard_map/ppermute | solution.py:143
  139.3 3.8 %collective-permute-done.10 = bf16[2,64,384]{2,1,0:T(8,128)(2,1)S(1)} collective-permute-done((bf16[2,64,384]{2,1,0:T(8,128)(2,1)S(1)}, bf16[2,64,384]{2,1,0:T(8,128)(2,1)S(1)}, u32[]{:S(2)}, u32[]{:S(2)}) %collective-permute-start.10) | collective-permute-done | bytes 98336 | tf_op jit(solution)/shard_map/ppermute | solution.py:143
  143.8 4.7 %collective-permute-start.11 = (bf16[64,384]{1,0:T(8,128)(2,1)S(1)}, bf16[64,384]{1,0:T(8,128)(2,1)S(1)}, u32[]{:S(2)}, u32[]{:S(2)}) collective-permute-start(bf16[64,384]{1,0:T(8,128)(2,1)S(1)} %fusion.2), channel_id=1, source_target_pairs={{0,384},{16,400},{32,416},{48,432},{64,448},{80,464},{96,480},{112... | collective-permute-start | bytes 147464 | tf_op jit(solution)/shard_map/ppermute | solution.py:143
  149.3 2.7 %collective-permute-done.11 = bf16[64,384]{1,0:T(8,128)(2,1)S(1)} collective-permute-done((bf16[64,384]{1,0:T(8,128)(2,1)S(1)}, bf16[64,384]{1,0:T(8,128)(2,1)S(1)}, u32[]{:S(2)}, u32[]{:S(2)}) %collective-permute-start.11) | collective-permute-done | bytes 49184 | tf_op jit(solution)/shard_map/ppermute | solution.py:143
  (52 shorter events, 23.1 us)
Async XLA Ops:
  7.2 13.6 %copy-start.9 = (bf16[64,384]{1,0:T(8,128)(2,1)S(1)}, bf16[64,384]{1,0:T(8,128)(2,1)}, u32[]{:S(2)}) copy-start(bf16[64,384]{1,0:T(8,128)(2,1)} %param.9) | copy-start | bytes 147460
  7.2 28.3 %copy-start.8 = (bf16[64,384]{1,0:T(8,128)(2,1)S(1)}, bf16[64,384]{1,0:T(8,128)(2,1)}, u32[]{:S(2)}) copy-start(bf16[64,384]{1,0:T(8,128)(2,1)} %param.8) | copy-start | bytes 147460
  7.2 79.0 %all-gather.2.cloned.1.call-start = ((), (), s32[]{:S(2)}) async-start(), calls=%async_computation.5 | async-start | bytes 3342336 | tf_op jit(solution)/shard_map/all_gather | solution.py:176
  10.5 25.0 %all-to-all-start = ((bf16[8,64,384]{2,1,0:T(8,128)(2,1)}), bf16[8,64,384]{2,1,0:T(8,128)(2,1)S(1)}, u32[]{:S(2)}, u32[]{:S(2)}) async-start(bf16[8,64,384]{2,1,0:T(8,128)(2,1)} %broadcast_in_dim.16), calls=%async_computation | async-start | bytes 786432 | tf_op jit(solution)/shard_map/all_to_all | solution.py:156
  20.8 19.1 %collective-permute-start = (bf16[64,384]{1,0:T(8,128)(2,1)S(1)}, bf16[64,384]{1,0:T(8,128)(2,1)S(1)}, u32[]{:S(2)}, u32[]{:S(2)}) collective-permute-start(bf16[64,384]{1,0:T(8,128)(2,1)S(1)} %copy-done.9), channel_id=1, source_target_pairs={{0,16},{16,32},{32,48},{48,0},{64,80},{80,96},{96,112},{112,64},{1... | collective-permute-start | bytes 147464 | tf_op jit(solution)/shard_map/ppermute | solution.py:138
  23.2 22.6 %collective-permute-start.1 = (bf16[64,384]{1,0:T(8,128)(2,1)S(1)}, bf16[64,384]{1,0:T(8,128)(2,1)S(1)}, u32[]{:S(2)}, u32[]{:S(2)}) collective-permute-start(bf16[64,384]{1,0:T(8,128)(2,1)S(1)} %copy-done.9), channel_id=1, source_target_pairs={{0,48},{16,0},{32,16},{48,32},{64,112},{80,64},{96,80},{112,96},{1... | collective-permute-start | bytes 147464 | tf_op jit(solution)/shard_map/ppermute | solution.py:138
  26.7 19.2 %collective-permute-start.2 = (bf16[64,384]{1,0:T(8,128)(2,1)S(1)}, bf16[64,384]{1,0:T(8,128)(2,1)S(1)}, u32[]{:S(2)}, u32[]{:S(2)}) collective-permute-start(bf16[64,384]{1,0:T(8,128)(2,1)S(1)} %copy-done.9), channel_id=1, source_target_pairs={{0,32},{16,48},{32,0},{48,16},{64,96},{80,112},{96,64},{112,80},{1... | collective-permute-start | bytes 147464 | tf_op jit(solution)/shard_map/ppermute | solution.py:138
  35.5 21.3 %copy-start.1 = (bf16[8,64,384]{2,1,0:T(8,128)(2,1)}, bf16[8,64,384]{2,1,0:T(8,128)(2,1)S(1)}, u32[]{:S(2)}) copy-start(bf16[8,64,384]{2,1,0:T(8,128)(2,1)S(1)} %all-to-all-done.g0) | copy-start | bytes 1179652
  36.3 19.0 %all-to-all-start.1 = ((bf16[8,64,384]{2,1,0:T(8,128)(2,1)}), bf16[8,64,384]{2,1,0:T(8,128)(2,1)S(1)}, u32[]{:S(2)}, u32[]{:S(2)}) async-start(bf16[8,64,384]{2,1,0:T(8,128)(2,1)} %broadcast_in_dim.34), calls=%async_computation.1 | async-start | bytes 786432 | tf_op jit(solution)/shard_map/all_to_all | solution.py:156
  39.9 12.0 %collective-permute-start.3 = (bf16[8,64,384]{2,1,0:T(8,128)(2,1)S(1)}, bf16[8,64,384]{2,1,0:T(8,128)(2,1)S(1)}, u32[]{:S(2)}, u32[]{:S(2)}) collective-permute-start(bf16[8,64,384]{2,1,0:T(8,128)(2,1)S(1)} %all-to-all-done.g0), channel_id=1, source_target_pairs={{0,16},{16,32},{32,48},{48,0},{64,80},{80,96},{96,112},{112,64},{1... | collective-permute-start | bytes 1179656 | tf_op jit(solution)/shard_map/ppermute | solution.py:138
  42.3 12.9 %collective-permute-start.4 = (bf16[8,64,384]{2,1,0:T(8,128)(2,1)S(1)}, bf16[8,64,384]{2,1,0:T(8,128)(2,1)S(1)}, u32[]{:S(2)}, u32[]{:S(2)}) collective-permute-start(bf16[8,64,384]{2,1,0:T(8,128)(2,1)S(1)} %all-to-all-done.g0), channel_id=1, source_target_pairs={{0,48},{16,0},{32,16},{48,32},{64,112},{80,64},{96,80},{112,96},{1... | collective-permute-start | bytes 1179656 | tf_op jit(solution)/shard_map/ppermute | solution.py:138
  51.9 18.8 %copy-start.3 = (bf16[8,64,384]{2,1,0:T(8,128)(2,1)}, bf16[8,64,384]{2,1,0:T(8,128)(2,1)S(1)}, u32[]{:S(2)}) copy-start(bf16[8,64,384]{2,1,0:T(8,128)(2,1)S(1)} %collective-permute-done.3.g1) | copy-start | bytes 1179652
  55.3 10.6 %copy-start.2 = (bf16[8,64,384]{2,1,0:T(8,128)(2,1)}, bf16[8,64,384]{2,1,0:T(8,128)(2,1)S(1)}, u32[]{:S(2)}) copy-start(bf16[8,64,384]{2,1,0:T(8,128)(2,1)S(1)} %all-to-all-done.1.u0) | copy-start | bytes 1179652
  56.8 44.7 %all-to-all-start.2 = ((bf16[8,4,64,384]{3,2,1,0:T(8,128)(2,1)}), bf16[8,4,64,384]{3,2,1,0:T(8,128)(2,1)S(1)}, u32[]{:S(2)}, u32[]{:S(2)}) async-start(bf16[8,4,64,384]{3,2,1,0:T(8,128)(2,1)} %broadcast_in_dim.40), calls=%async_computation.2 | async-start | bytes 3145728 | tf_op jit(solution)/shard_map/all_to_all | solution.py:156
  63.6 70.1 %reduce-scatter.2.cloned.1.call-start = ((), (), s32[]{:S(2)}) async-start(), calls=%async_computation.6 | async-start | bytes 1769472 | tf_op jit(solution)/shard_map/reduce_scatter | solution.py:222
  63.7 11.6 %collective-permute-start.7 = (bf16[8,64,384]{2,1,0:T(8,128)(2,1)S(1)}, bf16[8,64,384]{2,1,0:T(8,128)(2,1)S(1)}, u32[]{:S(2)}, u32[]{:S(2)}) collective-permute-start(bf16[8,64,384]{2,1,0:T(8,128)(2,1)S(1)} %all-to-all-done.1.u0), channel_id=1, source_target_pairs={{0,48},{16,0},{32,16},{48,32},{64,112},{80,64},{96,80},{112,96},{1... | collective-permute-start | bytes 1179656 | tf_op jit(solution)/shard_map/ppermute | solution.py:138
  65.9 19.0 %collective-permute-start.6 = (bf16[8,64,384]{2,1,0:T(8,128)(2,1)S(1)}, bf16[8,64,384]{2,1,0:T(8,128)(2,1)S(1)}, u32[]{:S(2)}, u32[]{:S(2)}) collective-permute-start(bf16[8,64,384]{2,1,0:T(8,128)(2,1)S(1)} %all-to-all-done.1.u0), channel_id=1, source_target_pairs={{0,16},{16,32},{32,48},{48,0},{64,80},{80,96},{96,112},{112,64},{1... | collective-permute-start | bytes 1179656 | tf_op jit(solution)/shard_map/ppermute | solution.py:138
  70.8 14.1 %collective-permute-start.5 = (bf16[8,64,384]{2,1,0:T(8,128)(2,1)S(1)}, bf16[8,64,384]{2,1,0:T(8,128)(2,1)S(1)}, u32[]{:S(2)}, u32[]{:S(2)}) collective-permute-start(bf16[8,64,384]{2,1,0:T(8,128)(2,1)S(1)} %collective-permute-done.3.g1), channel_id=1, source_target_pairs={{0,16},{16,32},{32,48},{48,0},{64,80},{80,96},{96,112},{112,64},{1... | collective-permute-start | bytes 1179656 | tf_op jit(solution)/shard_map/ppermute | solution.py:138
  75.2 11.0 %copy-start.5 = (bf16[8,64,384]{2,1,0:T(8,128)(2,1)}, bf16[8,64,384]{2,1,0:T(8,128)(2,1)S(1)}, u32[]{:S(2)}) copy-start(bf16[8,64,384]{2,1,0:T(8,128)(2,1)S(1)} %collective-permute-done.7.u2) | copy-start | bytes 1179652
  75.2 11.0 %collective-permute-start.8 = (bf16[8,64,384]{2,1,0:T(8,128)(2,1)S(1)}, bf16[8,64,384]{2,1,0:T(8,128)(2,1)}, u32[]{:S(2)}, u32[]{:S(2)}) collective-permute-start(bf16[8,64,384]{2,1,0:T(8,128)(2,1)S(1)} %collective-permute-done.7.u2), channel_id=1, source_target_pairs={{0,48},{16,0},{32,16},{48,32},{64,112},{80,64},{96,80},{112,96},{1... | collective-permute-start | bytes 1179656 | tf_op jit(solution)/shard_map/ppermute | solution.py:138
  109.7 4.4 %collective-permute-start.9 = (bf16[8,384,128]{2,1,0:T(8,128)(2,1)}, bf16[8,384,128]{2,1,0:T(8,128)(2,1)S(1)}, u32[]{:S(2)}, u32[]{:S(2)}) collective-permute-start(bf16[8,384,128]{2,1,0:T(8,128)(2,1)} %get-tuple-element.28), channel_id=1, source_target_pairs={{0,1},{1,0},{2,3},{3,2},{4,5},{5,4},{6,7},{7,6},{8,9},{9,8},{10,11... | collective-permute-start | bytes 2359304 | tf_op jit(solution)/shard_map/ppermute | solution.py:148
  116.4 32.1 %all-to-all-start.3 = ((bf16[8,384,128]{2,1,0:T(8,128)(2,1)}), bf16[8,384,128]{2,1,0:T(8,128)(2,1)S(1)}, u32[]{:S(2)}, u32[]{:S(2)}) async-start(bf16[8,384,128]{2,1,0:T(8,128)(2,1)} %add_convert_fusion), calls=%async_computation.3 | async-start | bytes 1572864 | tf_op jit(solution)/shard_map/all_to_all | solution.py:220
  134.6 8.5 %collective-permute-start.10 = (bf16[2,64,384]{2,1,0:T(8,128)(2,1)S(1)}, bf16[2,64,384]{2,1,0:T(8,128)(2,1)S(1)}, u32[]{:S(2)}, u32[]{:S(2)}) collective-permute-start(bf16[2,64,384]{2,1,0:T(8,128)(2,1)S(1)} %pad_maximum_fusion.1), channel_id=1, source_target_pairs={{0,128},{16,144},{32,160},{48,176},{64,192},{80,208},{96,224},{112... | collective-permute-start | bytes 294920 | tf_op jit(solution)/shard_map/ppermute | solution.py:143
  143.8 8.1 %collective-permute-start.11 = (bf16[64,384]{1,0:T(8,128)(2,1)S(1)}, bf16[64,384]{1,0:T(8,128)(2,1)S(1)}, u32[]{:S(2)}, u32[]{:S(2)}) collective-permute-start(bf16[64,384]{1,0:T(8,128)(2,1)S(1)} %fusion.2), channel_id=1, source_target_pairs={{0,384},{16,400},{32,416},{48,432},{64,448},{80,464},{96,480},{112... | collective-permute-start | bytes 147464 | tf_op jit(solution)/shard_map/ppermute | solution.py:143
  (4 other events, 5.5 us)
Sparse Core Ops, SparseCore 0:
  10.6 52.2 all-gather.1
  94.1 39.5 reduce-scatter.1

commit v11 on v10

--- a/solution.py
+++ b/solution.py
@@ -228,8 +228,10 @@
     ).reshape(N_Z // 2, depth, cols)
     block = lambda flip: lax.dynamic_index_in_dim(down_pair, (me_z // 2) ^ (flip // 2), 0, False)
     got = swap_z(jnp.stack([block(2), block(4)]), 2)
-    got_last = swap_z(add(block(6), got[1]).astype(jnp.bfloat16), 6)
-    down_sum = add(block(0), got[0]) + got_last.astype(jnp.float32)
+    kept, passed = lax.optimization_barrier(
+        (add(block(0), got[0]), add(block(6), got[1]).astype(jnp.bfloat16))
+    )
+    down_sum = kept + swap_z(passed, 6).astype(jnp.float32)
     grad_down = (down_sum * factor).astype(jnp.bfloat16)
     input_grad = summed.astype(jnp.float32).sum(0).astype(jnp.bfloat16)
     return (input_grad, grad_down)

time: 162 us -> 161 us (level)
  no operation moved by 1% of the time
where the time goes in v11:
time: 161 us; the launch traced here: 160 us
  starting transfers between devices  64.7 us (40%)
  waiting for transfers between devices  52.8 us (33%)
  Pallas kernels  14.7 us (9%)
  between operations  14.4 us (9%)
  other arithmetic  6.75 us (4%)
  local copies, waits for them, and re-layouts  6.12 us (4%)
    ppermute x9, starting transfers between devices, send_x(): return lax.ppermute(value, 'fsdp', pairs)  25.9 us
    all_to_all x3, starting transfers between devices, gather_z(): return lax.all_to_all(copies, 'fsdp', 0, 0, axis_index_groups=Z_GROUPS)  20.6 us
    ppermute x9, waiting for transfers between devices, send_x(): return lax.ppermute(value, 'fsdp', pairs)  20.4 us
    pallas_call x2, Pallas kernels, call_kernel(): pl.pallas_call(kernel, out_shape=out_shapes, in_specs=in_specs, out_specs...  14.7 us
    all_to_all x3, waiting for transfers between devices, gather_z(): return lax.all_to_all(copies, 'fsdp', 0, 0, axis_index_groups=Z_GROUPS)  13 us
    reduce_scatter x1, waiting for transfers between devices, on_device(): lax.psum_scatter(down_partial.reshape(n_feat, cols), 'fsdp', scatter_dime...  10.3 us
    ppermute x2, starting transfers between devices, swap_z(): return lax.ppermute(value, 'fsdp', pairs)  9.2 us
    all_to_all x1, starting transfers between devices, on_device(): summed = lax.all_to_all(pair_sum, 'mp', 0, 0, axis_index_groups=Y_GROUPS)  7.03 us
  transfers between devices with their start and end apart: 18, of which 11 were waited for; matrix products, arithmetic and copies ran while one was open for 5% of the time, Pallas kernels for 9%

profile of v11, /device:TPU:6, one launch (start us, length us, event | category | flops | bytes accessed | tf_op | source)
XLA Modules:
  0.0 159.5 jit_solution(698386116532137812)
XLA Ops:
  10.5 10.3 %all-to-all-start = ((bf16[8,64,384]{2,1,0:T(8,128)(2,1)}), bf16[8,64,384]{2,1,0:T(8,128)(2,1)S(1)}, u32[]{:S(2)}, u32[]{:S(2)}) async-start(bf16[8,64,384]{2,1,0:T(8,128)(2,1)} %broadcast_in_dim.16), calls=%async_computation | async-start | bytes 786432 | tf_op jit(solution)/shard_map/all_to_all | solution.py:156
  20.8 2.4 %collective-permute-start = (bf16[64,384]{1,0:T(8,128)(2,1)S(1)}, bf16[64,384]{1,0:T(8,128)(2,1)S(1)}, u32[]{:S(2)}, u32[]{:S(2)}) collective-permute-start(bf16[64,384]{1,0:T(8,128)(2,1)S(1)} %copy-done.9), channel_id=1, source_target_pairs={{0,16},{16,32},{32,48},{48,0},{64,80},{80,96},{96,112},{112,64},{1... | collective-permute-start | bytes 147464 | tf_op jit(solution)/shard_map/ppermute | solution.py:138
  23.2 3.5 %collective-permute-start.1 = (bf16[64,384]{1,0:T(8,128)(2,1)S(1)}, bf16[64,384]{1,0:T(8,128)(2,1)S(1)}, u32[]{:S(2)}, u32[]{:S(2)}) collective-permute-start(bf16[64,384]{1,0:T(8,128)(2,1)S(1)} %copy-done.9), channel_id=1, source_target_pairs={{0,48},{16,0},{32,16},{48,32},{64,112},{80,64},{96,80},{112,96},{1... | collective-permute-start | bytes 147464 | tf_op jit(solution)/shard_map/ppermute | solution.py:138
  26.7 3.3 %collective-permute-start.2 = (bf16[64,384]{1,0:T(8,128)(2,1)S(1)}, bf16[64,384]{1,0:T(8,128)(2,1)S(1)}, u32[]{:S(2)}, u32[]{:S(2)}) collective-permute-start(bf16[64,384]{1,0:T(8,128)(2,1)S(1)} %copy-done.9), channel_id=1, source_target_pairs={{0,32},{16,48},{32,0},{48,16},{64,96},{80,112},{96,64},{112,80},{1... | collective-permute-start | bytes 147464 | tf_op jit(solution)/shard_map/ppermute | solution.py:138
  30.0 5.5 %all-to-all-done.g0 = bf16[8,64,384]{2,1,0:T(8,128)(2,1)S(1)} async-done(((bf16[8,64,384]{2,1,0:T(8,128)(2,1)}), bf16[8,64,384]{2,1,0:T(8,128)(2,1)S(1)}, u32[]{:S(2)}, u32[]{:S(2)}) %all-to-all-start) | async-done | bytes 393248 | tf_op jit(solution)/shard_map/all_to_all | solution.py:156
  36.3 3.5 %all-to-all-start.1 = ((bf16[8,64,384]{2,1,0:T(8,128)(2,1)}), bf16[8,64,384]{2,1,0:T(8,128)(2,1)S(1)}, u32[]{:S(2)}, u32[]{:S(2)}) async-start(bf16[8,64,384]{2,1,0:T(8,128)(2,1)} %broadcast_in_dim.34), calls=%async_computation.1 | async-start | bytes 786432 | tf_op jit(solution)/shard_map/all_to_all | solution.py:156
  39.9 2.4 %collective-permute-start.3 = (bf16[8,64,384]{2,1,0:T(8,128)(2,1)S(1)}, bf16[8,64,384]{2,1,0:T(8,128)(2,1)S(1)}, u32[]{:S(2)}, u32[]{:S(2)}) collective-permute-start(bf16[8,64,384]{2,1,0:T(8,128)(2,1)S(1)} %all-to-all-done.g0), channel_id=1, source_target_pairs={{0,16},{16,32},{32,48},{48,0},{64,80},{80,96},{96,112},{112,64},{1... | collective-permute-start | bytes 1179656 | tf_op jit(solution)/shard_map/ppermute | solution.py:138
  42.4 3.4 %collective-permute-start.4 = (bf16[8,64,384]{2,1,0:T(8,128)(2,1)S(1)}, bf16[8,64,384]{2,1,0:T(8,128)(2,1)S(1)}, u32[]{:S(2)}, u32[]{:S(2)}) collective-permute-start(bf16[8,64,384]{2,1,0:T(8,128)(2,1)S(1)} %all-to-all-done.g0), channel_id=1, source_target_pairs={{0,48},{16,0},{32,16},{48,32},{64,112},{80,64},{96,80},{112,96},{1... | collective-permute-start | bytes 1179656 | tf_op jit(solution)/shard_map/ppermute | solution.py:138
  45.9 6.1 %collective-permute-done.3.g1 = bf16[8,64,384]{2,1,0:T(8,128)(2,1)S(1)} collective-permute-done((bf16[8,64,384]{2,1,0:T(8,128)(2,1)S(1)}, bf16[8,64,384]{2,1,0:T(8,128)(2,1)S(1)}, u32[]{:S(2)}, u32[]{:S(2)}) %collective-permute-start.3) | collective-permute-done | bytes 393248 | tf_op jit(solution)/shard_map/ppermute | solution.py:138
  51.9 3.4 %collective-permute-done.4.g2 = bf16[8,64,384]{2,1,0:T(8,128)(2,1)S(1)} collective-permute-done((bf16[8,64,384]{2,1,0:T(8,128)(2,1)S(1)}, bf16[8,64,384]{2,1,0:T(8,128)(2,1)S(1)}, u32[]{:S(2)}, u32[]{:S(2)}) %collective-permute-start.4) | collective-permute-done | bytes 393248 | tf_op jit(solution)/shard_map/ppermute | solution.py:138
  56.8 6.8 %all-to-all-start.2 = ((bf16[8,4,64,384]{3,2,1,0:T(8,128)(2,1)}), bf16[8,4,64,384]{3,2,1,0:T(8,128)(2,1)S(1)}, u32[]{:S(2)}, u32[]{:S(2)}) async-start(bf16[8,4,64,384]{3,2,1,0:T(8,128)(2,1)} %broadcast_in_dim.40), calls=%async_computation.2 | async-start | bytes 3145728 | tf_op jit(solution)/shard_map/all_to_all | solution.py:156
  65.9 4.8 %collective-permute-start.6 = (bf16[8,64,384]{2,1,0:T(8,128)(2,1)S(1)}, bf16[8,64,384]{2,1,0:T(8,128)(2,1)S(1)}, u32[]{:S(2)}, u32[]{:S(2)}) collective-permute-start(bf16[8,64,384]{2,1,0:T(8,128)(2,1)S(1)} %all-to-all-done.1.u0), channel_id=1, source_target_pairs={{0,16},{16,32},{32,48},{48,0},{64,80},{80,96},{96,112},{112,64},{1... | collective-permute-start | bytes 1179656 | tf_op jit(solution)/shard_map/ppermute | solution.py:138
  72.7 2.5 %collective-permute-done.7.u2 = bf16[8,64,384]{2,1,0:T(8,128)(2,1)S(1)} collective-permute-done((bf16[8,64,384]{2,1,0:T(8,128)(2,1)S(1)}, bf16[8,64,384]{2,1,0:T(8,128)(2,1)S(1)}, u32[]{:S(2)}, u32[]{:S(2)}) %collective-permute-start.7) | collective-permute-done | bytes 393248 | tf_op jit(solution)/shard_map/ppermute | solution.py:138
  77.8 7.1 %collective-permute-done.5.g3 = bf16[8,64,384]{2,1,0:T(8,128)(2,1)S(1)} collective-permute-done((bf16[8,64,384]{2,1,0:T(8,128)(2,1)S(1)}, bf16[8,64,384]{2,1,0:T(8,128)(2,1)S(1)}, u32[]{:S(2)}, u32[]{:S(2)}) %collective-permute-start.5) | collective-permute-done | bytes 393248 | tf_op jit(solution)/shard_map/ppermute | solution.py:138
  86.2 7.7 %shard_map.68 = (f32[384,384]{1,0:T(8,128)}, f32[384,384]{1,0:T(8,128)}, bf16[8,4,64,384]{3,2,1,0:T(8,128)(2,1)}) custom-call(s32[2]{0:T(128)} %pad_add_fusion.place, bf16[768,2048]{1,0:T(8,128)(2,1)} %all-gather.2.cloned.1.call-done.rows_ref, bf16[8,64,384]{2,1,0:T(8,128)(2,1)} %copy-done.1, bf16[8,64,384]{2,1,0:T(8,128)(2,1)} %copy-done.3, ...), custom_call_target="tpu_custom_call" | custom-call | flops 1811939328 | bytes 10000000 | tf_op jit(solution)/shard_map/pallas_call | solution.py:119
  94.0 7.5 %all-to-all-done.2 = bf16[8,4,64,384]{3,2,1,0:T(8,128)(2,1)S(1)} async-done(((bf16[8,4,64,384]{3,2,1,0:T(8,128)(2,1)}), bf16[8,4,64,384]{3,2,1,0:T(8,128)(2,1)S(1)}, u32[]{:S(2)}, u32[]{:S(2)}) %all-to-all-start.2) | async-done | bytes 1572896 | tf_op jit(solution)/shard_map/all_to_all | solution.py:156
  102.7 7.0 %shard_map.69 = (bf16[8,384,128]{2,1,0:T(8,128)(2,1)}, bf16[8,384,128]{2,1,0:T(8,128)(2,1)}) custom-call(s32[2]{0:T(128)} %pad_add_fusion.place, bf16[768,2048]{1,0:T(8,128)(2,1)} %all-gather.2.cloned.1.call-done.rows_ref, bf16[8,2,128,384]{3,2,1,0:T(8,128)(2,1)} %bitcast.17, bf16[8,64,384]{2,1,0:T(8,128)(2,1)} %copy-done.1, bf16[8,64,384]{2,1,0:T(8,128)(2,1)} %copy-done.3, ...), custom_call_target="tpu_custom_call" | custom-call | flops 1811939328 | bytes 10000000 | tf_op jit(solution)/shard_map/pallas_call | solution.py:119
  111.7 2.5 %collective-permute-done.9 = bf16[8,384,128]{2,1,0:T(8,128)(2,1)S(1)} collective-permute-done((bf16[8,384,128]{2,1,0:T(8,128)(2,1)}, bf16[8,384,128]{2,1,0:T(8,128)(2,1)S(1)}, u32[]{:S(2)}, u32[]{:S(2)}) %collective-permute-start.9) | collective-permute-done | bytes 786464 | tf_op jit(solution)/shard_map/ppermute | solution.py:148
  116.4 7.0 %all-to-all-start.3 = ((bf16[8,384,128]{2,1,0:T(8,128)(2,1)}), bf16[8,384,128]{2,1,0:T(8,128)(2,1)S(1)}, u32[]{:S(2)}, u32[]{:S(2)}) async-start(bf16[8,384,128]{2,1,0:T(8,128)(2,1)} %add_convert_fusion), calls=%async_computation.3 | async-start | bytes 1572864 | tf_op jit(solution)/shard_map/all_to_all | solution.py:220
  123.4 10.3 %reduce-scatter.2.cloned.1.call-done = bf16[256,384]{1,0:T(8,128)(2,1)} async-done(((bf16[2048,384]{1,0:T(8,128)(2,1)}), bf16[256,384]{1,0:T(8,128)(2,1)}) %reduce-scatter.2.cloned.1.call-update) | async-done | bytes 196624 | tf_op jit(solution)/shard_map/reduce_scatter | solution.py:222
  134.6 4.6 %collective-permute-start.10 = (bf16[2,64,384]{2,1,0:T(8,128)(2,1)S(1)}, bf16[2,64,384]{2,1,0:T(8,128)(2,1)S(1)}, u32[]{:S(2)}, u32[]{:S(2)}) collective-permute-start(bf16[2,64,384]{2,1,0:T(8,128)(2,1)S(1)} %pad_maximum_fusion.1), channel_id=1, source_target_pairs={{0,128},{16,144},{32,160},{48,176},{64,192},{80,208},{96,224},{112... | collective-permute-start | bytes 294920 | tf_op jit(solution)/shard_map/ppermute | solution.py:143
  139.2 3.9 %collective-permute-done.10 = bf16[2,64,384]{2,1,0:T(8,128)(2,1)S(1)} collective-permute-done((bf16[2,64,384]{2,1,0:T(8,128)(2,1)S(1)}, bf16[2,64,384]{2,1,0:T(8,128)(2,1)S(1)}, u32[]{:S(2)}, u32[]{:S(2)}) %collective-permute-start.10) | collective-permute-done | bytes 98336 | tf_op jit(solution)/shard_map/ppermute | solution.py:143
  143.9 4.6 %collective-permute-start.11 = (bf16[64,384]{1,0:T(8,128)(2,1)S(1)}, bf16[64,384]{1,0:T(8,128)(2,1)S(1)}, u32[]{:S(2)}, u32[]{:S(2)}) collective-permute-start(bf16[64,384]{1,0:T(8,128)(2,1)S(1)} %get-tuple-element.33), channel_id=1, source_target_pairs={{0,384},{16,400},{32,416},{48,432},{64,448},{80,464},{96,480},{112... | collective-permute-start | bytes 147464 | tf_op jit(solution)/shard_map/ppermute | solution.py:143
  149.3 2.7 %collective-permute-done.11 = bf16[64,384]{1,0:T(8,128)(2,1)S(1)} collective-permute-done((bf16[64,384]{1,0:T(8,128)(2,1)S(1)}, bf16[64,384]{1,0:T(8,128)(2,1)S(1)}, u32[]{:S(2)}, u32[]{:S(2)}) %collective-permute-start.11) | collective-permute-done | bytes 49184 | tf_op jit(solution)/shard_map/ppermute | solution.py:143
  (52 shorter events, 22.3 us)
Async XLA Ops:
  7.2 13.6 %copy-start.9 = (bf16[64,384]{1,0:T(8,128)(2,1)S(1)}, bf16[64,384]{1,0:T(8,128)(2,1)}, u32[]{:S(2)}) copy-start(bf16[64,384]{1,0:T(8,128)(2,1)} %param.9) | copy-start | bytes 147460
  7.2 28.3 %copy-start.8 = (bf16[64,384]{1,0:T(8,128)(2,1)S(1)}, bf16[64,384]{1,0:T(8,128)(2,1)}, u32[]{:S(2)}) copy-start(bf16[64,384]{1,0:T(8,128)(2,1)} %param.8) | copy-start | bytes 147460
  7.2 79.0 %all-gather.2.cloned.1.call-start = ((), (), s32[]{:S(2)}) async-start(), calls=%async_computation.5 | async-start | bytes 3342336 | tf_op jit(solution)/shard_map/all_gather | solution.py:176
  10.5 25.0 %all-to-all-start = ((bf16[8,64,384]{2,1,0:T(8,128)(2,1)}), bf16[8,64,384]{2,1,0:T(8,128)(2,1)S(1)}, u32[]{:S(2)}, u32[]{:S(2)}) async-start(bf16[8,64,384]{2,1,0:T(8,128)(2,1)} %broadcast_in_dim.16), calls=%async_computation | async-start | bytes 786432 | tf_op jit(solution)/shard_map/all_to_all | solution.py:156
  20.8 19.1 %collective-permute-start = (bf16[64,384]{1,0:T(8,128)(2,1)S(1)}, bf16[64,384]{1,0:T(8,128)(2,1)S(1)}, u32[]{:S(2)}, u32[]{:S(2)}) collective-permute-start(bf16[64,384]{1,0:T(8,128)(2,1)S(1)} %copy-done.9), channel_id=1, source_target_pairs={{0,16},{16,32},{32,48},{48,0},{64,80},{80,96},{96,112},{112,64},{1... | collective-permute-start | bytes 147464 | tf_op jit(solution)/shard_map/ppermute | solution.py:138
  23.2 22.6 %collective-permute-start.1 = (bf16[64,384]{1,0:T(8,128)(2,1)S(1)}, bf16[64,384]{1,0:T(8,128)(2,1)S(1)}, u32[]{:S(2)}, u32[]{:S(2)}) collective-permute-start(bf16[64,384]{1,0:T(8,128)(2,1)S(1)} %copy-done.9), channel_id=1, source_target_pairs={{0,48},{16,0},{32,16},{48,32},{64,112},{80,64},{96,80},{112,96},{1... | collective-permute-start | bytes 147464 | tf_op jit(solution)/shard_map/ppermute | solution.py:138
  26.7 19.2 %collective-permute-start.2 = (bf16[64,384]{1,0:T(8,128)(2,1)S(1)}, bf16[64,384]{1,0:T(8,128)(2,1)S(1)}, u32[]{:S(2)}, u32[]{:S(2)}) collective-permute-start(bf16[64,384]{1,0:T(8,128)(2,1)S(1)} %copy-done.9), channel_id=1, source_target_pairs={{0,32},{16,48},{32,0},{48,16},{64,96},{80,112},{96,64},{112,80},{1... | collective-permute-start | bytes 147464 | tf_op jit(solution)/shard_map/ppermute | solution.py:138
  35.5 21.3 %copy-start.1 = (bf16[8,64,384]{2,1,0:T(8,128)(2,1)}, bf16[8,64,384]{2,1,0:T(8,128)(2,1)S(1)}, u32[]{:S(2)}) copy-start(bf16[8,64,384]{2,1,0:T(8,128)(2,1)S(1)} %all-to-all-done.g0) | copy-start | bytes 1179652
  36.3 19.0 %all-to-all-start.1 = ((bf16[8,64,384]{2,1,0:T(8,128)(2,1)}), bf16[8,64,384]{2,1,0:T(8,128)(2,1)S(1)}, u32[]{:S(2)}, u32[]{:S(2)}) async-start(bf16[8,64,384]{2,1,0:T(8,128)(2,1)} %broadcast_in_dim.34), calls=%async_computation.1 | async-start | bytes 786432 | tf_op jit(solution)/shard_map/all_to_all | solution.py:156
  39.9 12.0 %collective-permute-start.3 = (bf16[8,64,384]{2,1,0:T(8,128)(2,1)S(1)}, bf16[8,64,384]{2,1,0:T(8,128)(2,1)S(1)}, u32[]{:S(2)}, u32[]{:S(2)}) collective-permute-start(bf16[8,64,384]{2,1,0:T(8,128)(2,1)S(1)} %all-to-all-done.g0), channel_id=1, source_target_pairs={{0,16},{16,32},{32,48},{48,0},{64,80},{80,96},{96,112},{112,64},{1... | collective-permute-start | bytes 1179656 | tf_op jit(solution)/shard_map/ppermute | solution.py:138
  42.4 12.9 %collective-permute-start.4 = (bf16[8,64,384]{2,1,0:T(8,128)(2,1)S(1)}, bf16[8,64,384]{2,1,0:T(8,128)(2,1)S(1)}, u32[]{:S(2)}, u32[]{:S(2)}) collective-permute-start(bf16[8,64,384]{2,1,0:T(8,128)(2,1)S(1)} %all-to-all-done.g0), channel_id=1, source_target_pairs={{0,48},{16,0},{32,16},{48,32},{64,112},{80,64},{96,80},{112,96},{1... | collective-permute-start | bytes 1179656 | tf_op jit(solution)/shard_map/ppermute | solution.py:138
  51.9 18.8 %copy-start.3 = (bf16[8,64,384]{2,1,0:T(8,128)(2,1)}, bf16[8,64,384]{2,1,0:T(8,128)(2,1)S(1)}, u32[]{:S(2)}) copy-start(bf16[8,64,384]{2,1,0:T(8,128)(2,1)S(1)} %collective-permute-done.3.g1) | copy-start | bytes 1179652
  55.3 10.6 %copy-start.2 = (bf16[8,64,384]{2,1,0:T(8,128)(2,1)}, bf16[8,64,384]{2,1,0:T(8,128)(2,1)S(1)}, u32[]{:S(2)}) copy-start(bf16[8,64,384]{2,1,0:T(8,128)(2,1)S(1)} %all-to-all-done.1.u0) | copy-start | bytes 1179652
  56.8 44.7 %all-to-all-start.2 = ((bf16[8,4,64,384]{3,2,1,0:T(8,128)(2,1)}), bf16[8,4,64,384]{3,2,1,0:T(8,128)(2,1)S(1)}, u32[]{:S(2)}, u32[]{:S(2)}) async-start(bf16[8,4,64,384]{3,2,1,0:T(8,128)(2,1)} %broadcast_in_dim.40), calls=%async_computation.2 | async-start | bytes 3145728 | tf_op jit(solution)/shard_map/all_to_all | solution.py:156
  63.6 70.1 %reduce-scatter.2.cloned.1.call-start = ((), (), s32[]{:S(2)}) async-start(), calls=%async_computation.6 | async-start | bytes 1769472 | tf_op jit(solution)/shard_map/reduce_scatter | solution.py:222
  63.7 11.6 %collective-permute-start.7 = (bf16[8,64,384]{2,1,0:T(8,128)(2,1)S(1)}, bf16[8,64,384]{2,1,0:T(8,128)(2,1)S(1)}, u32[]{:S(2)}, u32[]{:S(2)}) collective-permute-start(bf16[8,64,384]{2,1,0:T(8,128)(2,1)S(1)} %all-to-all-done.1.u0), channel_id=1, source_target_pairs={{0,48},{16,0},{32,16},{48,32},{64,112},{80,64},{96,80},{112,96},{1... | collective-permute-start | bytes 1179656 | tf_op jit(solution)/shard_map/ppermute | solution.py:138
  65.9 19.0 %collective-permute-start.6 = (bf16[8,64,384]{2,1,0:T(8,128)(2,1)S(1)}, bf16[8,64,384]{2,1,0:T(8,128)(2,1)S(1)}, u32[]{:S(2)}, u32[]{:S(2)}) collective-permute-start(bf16[8,64,384]{2,1,0:T(8,128)(2,1)S(1)} %all-to-all-done.1.u0), channel_id=1, source_target_pairs={{0,16},{16,32},{32,48},{48,0},{64,80},{80,96},{96,112},{112,64},{1... | collective-permute-start | bytes 1179656 | tf_op jit(solution)/shard_map/ppermute | solution.py:138
  70.8 14.1 %collective-permute-start.5 = (bf16[8,64,384]{2,1,0:T(8,128)(2,1)S(1)}, bf16[8,64,384]{2,1,0:T(8,128)(2,1)S(1)}, u32[]{:S(2)}, u32[]{:S(2)}) collective-permute-start(bf16[8,64,384]{2,1,0:T(8,128)(2,1)S(1)} %collective-permute-done.3.g1), channel_id=1, source_target_pairs={{0,16},{16,32},{32,48},{48,0},{64,80},{80,96},{96,112},{112,64},{1... | collective-permute-start | bytes 1179656 | tf_op jit(solution)/shard_map/ppermute | solution.py:138
  75.2 11.0 %copy-start.5 = (bf16[8,64,384]{2,1,0:T(8,128)(2,1)}, bf16[8,64,384]{2,1,0:T(8,128)(2,1)S(1)}, u32[]{:S(2)}) copy-start(bf16[8,64,384]{2,1,0:T(8,128)(2,1)S(1)} %collective-permute-done.7.u2) | copy-start | bytes 1179652
  75.2 11.0 %collective-permute-start.8 = (bf16[8,64,384]{2,1,0:T(8,128)(2,1)S(1)}, bf16[8,64,384]{2,1,0:T(8,128)(2,1)}, u32[]{:S(2)}, u32[]{:S(2)}) collective-permute-start(bf16[8,64,384]{2,1,0:T(8,128)(2,1)S(1)} %collective-permute-done.7.u2), channel_id=1, source_target_pairs={{0,48},{16,0},{32,16},{48,32},{64,112},{80,64},{96,80},{112,96},{1... | collective-permute-start | bytes 1179656 | tf_op jit(solution)/shard_map/ppermute | solution.py:138
  109.8 4.4 %collective-permute-start.9 = (bf16[8,384,128]{2,1,0:T(8,128)(2,1)}, bf16[8,384,128]{2,1,0:T(8,128)(2,1)S(1)}, u32[]{:S(2)}, u32[]{:S(2)}) collective-permute-start(bf16[8,384,128]{2,1,0:T(8,128)(2,1)} %get-tuple-element.30), channel_id=1, source_target_pairs={{0,1},{1,0},{2,3},{3,2},{4,5},{5,4},{6,7},{7,6},{8,9},{9,8},{10,11... | collective-permute-start | bytes 2359304 | tf_op jit(solution)/shard_map/ppermute | solution.py:148
  116.4 32.2 %all-to-all-start.3 = ((bf16[8,384,128]{2,1,0:T(8,128)(2,1)}), bf16[8,384,128]{2,1,0:T(8,128)(2,1)S(1)}, u32[]{:S(2)}, u32[]{:S(2)}) async-start(bf16[8,384,128]{2,1,0:T(8,128)(2,1)} %add_convert_fusion), calls=%async_computation.3 | async-start | bytes 1572864 | tf_op jit(solution)/shard_map/all_to_all | solution.py:220
  134.6 8.5 %collective-permute-start.10 = (bf16[2,64,384]{2,1,0:T(8,128)(2,1)S(1)}, bf16[2,64,384]{2,1,0:T(8,128)(2,1)S(1)}, u32[]{:S(2)}, u32[]{:S(2)}) collective-permute-start(bf16[2,64,384]{2,1,0:T(8,128)(2,1)S(1)} %pad_maximum_fusion.1), channel_id=1, source_target_pairs={{0,128},{16,144},{32,160},{48,176},{64,192},{80,208},{96,224},{112... | collective-permute-start | bytes 294920 | tf_op jit(solution)/shard_map/ppermute | solution.py:143
  143.9 8.1 %collective-permute-start.11 = (bf16[64,384]{1,0:T(8,128)(2,1)S(1)}, bf16[64,384]{1,0:T(8,128)(2,1)S(1)}, u32[]{:S(2)}, u32[]{:S(2)}) collective-permute-start(bf16[64,384]{1,0:T(8,128)(2,1)S(1)} %get-tuple-element.33), channel_id=1, source_target_pairs={{0,384},{16,400},{32,416},{48,432},{64,448},{80,464},{96,480},{112... | collective-permute-start | bytes 147464 | tf_op jit(solution)/shard_map/ppermute | solution.py:143
  (4 other events, 5.5 us)
Sparse Core Ops, SparseCore 0:
  10.6 52.2 all-gather.1
  94.1 39.6 reduce-scatter.1
